TPU v7x, 32 devices: a whole 2x2x4 slice. The times are simulated.
32 devices in a mesh: member: 2 (over y), gridy: 4 (over x, core), gridx: 4 (over z).
Axes of the slice: x: 2, y: 2, z: 4, core: 2. Of those that a mesh axis runs over, the one named last changes fastest.
Arguments:
- temp: float32 [4, 4, 256, 1024], P('member', None, 'gridy', 'gridx'), may hold values from -6 to 6
- salt: float32 [4, 4, 256, 1024], P('member', None, 'gridy', 'gridx'), may hold values from -6 to 6
- uvel: float32 [4, 4, 256, 1024], P('member', None, 'gridy', 'gridx'), may hold values from -3 to 3
- vvel: float32 [4, 4, 256, 1024], P('member', None, 'gridy', 'gridx'), may hold values from -3 to 3
- eta: float32 [4, 256, 1024], P('member', 'gridy', 'gridx'), may hold values from -6 to 6
- land_mask: int32 [256, 1024], P('gridy', 'gridx'), may hold values 0 or 1
- clone_source: int32 [4], P('member'), may hold values from 0 to 3
Outputs:
- new_temp: float32 [4, 4, 256, 1024], P('member', None, 'gridy', 'gridx')
- new_salt: float32 [4, 4, 256, 1024], P('member', None, 'gridy', 'gridx')
- new_uvel: float32 [4, 4, 256, 1024], P('member', None, 'gridy', 'gridx')
- new_vvel: float32 [4, 4, 256, 1024], P('member', None, 'gridy', 'gridx')
- new_eta: float32 [4, 256, 1024], P('member', 'gridy', 'gridx')
- overturning: float32 [4, 4, 256], P('member', None, 'gridy')
- clone_weight: float32 [4], P('member')
All inputs are finite; a program needn't handle non-finite values. No bound on the sum of `land_mask` on one device may be relied on, other than what follows from the above.
Results may differ from a plain program's by a relative error of at most 0.0001.
Values sent between devices are 32-bit elements; how exact they have to be, the bound alone decides.
No kernel may reach another device: no remote copies, remote signals or barrier semaphores. Data moves between devices by JAX's collectives and lax.ppermute only.
A program may use at most 128 MiB of HBM per device.

v0:
```python
import functools

import jax
import jax.numpy as jnp
from jax import lax
from jax.experimental import pallas as pl
from jax.experimental.pallas import tpu as pltpu
from jax.sharding import PartitionSpec as P

STEPS = 2
ITERS = 3

ALPHA_T = 0.8
BETA_S = 0.6
PRESS_K = 0.25
STEP_DT = 0.1
KAPPA = 0.1
VISCOSITY = 0.1
DRAG_K = 0.05
CORI_K = 1.0
SURF_C = 4.0
DIV_K = 0.5
GRAV_K = 0.5

ADV = STEP_DT * 0.5
DIV = DIV_K * 0.5
GRAV = GRAV_K * 0.5

WIDE = 10
TOP = 24
CHUNK = 16
LANE = 128
PER_GROUP = 11
PAIRS = [(a, b) for a in range(4) for b in range(a, 4)]
SUMS = 6 + 6 * len(PAIRS)
VMEM_LIMIT = 24 * 1024 * 1024
WHOLE_VMEM = 60 * 1024 * 1024


def rim_place(plane):
    group, place = divmod(plane, PER_GROUP)
    if place < 6:
        return group, 0, (2 * place + 1) * WIDE
    return group, 1, (2 * (place - 6) + 2) * WIDE


def groups_of(planes):
    return -(-planes // PER_GROUP)


def lanes_like(shape):
    return lax.broadcasted_iota(jnp.int32, shape, len(shape) - 1)


def fetches(fields, planes_of, mask_to, sems, levels):
    members = fields[0].shape[0]
    per_member = []
    for m in range(members):
        parts = [(fields[f].at[m], planes_of(m, pl.ds(f * levels, levels))) for f in range(4)]
        parts.append((fields[4].at[m], planes_of(m, 4 * levels)))
        per_member.append([pltpu.make_async_copy(*part, sems.at[m, i]) for i, part in enumerate(parts)])
    mask_copy = pltpu.make_async_copy(fields[5], mask_to, sems.at[0, 5])
    mask_copy.start()
    for copies in per_member:
        for copy in copies:
            copy.start()
    mask_copy.wait()
    return per_member


def pack_kernel(levels, *refs):
    fields, (to_west, to_east, rows_first, rows_second), (held, mask, sems) = refs[:6], refs[6:10], refs[10:]
    members, _, rows, cols = held.shape
    planes = 4 * levels + 2
    copies = fetches(fields, lambda m, at: held.at[m, at], mask, sems, levels)
    lane = lanes_like((rows, LANE))
    even = lax.broadcasted_iota(jnp.int32, (WIDE, cols), 0) * 0 + lax.rem(lax.axis_index("gridy"), 2) == 0
    for m in range(members):
        for copy in copies[m]:
            copy.wait()
        west_parts = [None] * groups_of(planes)
        east_parts = [None] * groups_of(planes)
        for plane in range(planes):
            value = held[m, plane] if plane < planes - 1 else mask[...].astype(jnp.float32)
            group, _, start = rim_place(plane)
            both = jnp.where(lane < WIDE, value[:, :LANE], value[:, cols - LANE :])
            both = pltpu.roll(both, start, 1)
            is_west = (lane >= start) & (lane < start + WIDE)
            is_east = (lane >= start - WIDE) & (lane < start)
            zero = jnp.zeros_like(both)
            west_parts[group] = jnp.where(is_west, both, zero if west_parts[group] is None else west_parts[group])
            east_parts[group] = jnp.where(is_east, both, zero if east_parts[group] is None else east_parts[group])
            low, high = value[:WIDE], value[rows - WIDE :]
            rows_first[m, plane * WIDE : (plane + 1) * WIDE, :] = jnp.where(even, high, low)
            rows_second[m, plane * WIDE : (plane + 1) * WIDE, :] = jnp.where(even, low, high)
        for group in range(groups_of(planes)):
            where = slice(group * LANE, (group + 1) * LANE)
            to_west[m, :, where] = west_parts[group]
            to_east[m, :, where] = east_parts[group]


def whole(count):
    return [pl.BlockSpec(memory_space=pltpu.VMEM)] * count


def in_hbm(count):
    return [pl.BlockSpec(memory_space=pltpu.HBM)] * count


def in_smem(count):
    return [pl.BlockSpec(memory_space=pltpu.SMEM)] * count


def pack_rims(temp, salt, uvel, vvel, eta, mask):
    members, levels, rows, cols = temp.shape
    planes = 4 * levels + 2
    wide = groups_of(planes) * LANE
    row_pack = -(-planes * WIDE // 8) * 8
    side = jax.ShapeDtypeStruct((members, rows, wide), jnp.float32)
    line = jax.ShapeDtypeStruct((members, row_pack, cols), jnp.float32)
    return pl.pallas_call(
        functools.partial(pack_kernel, levels),
        out_shape=(side, side, line, line),
        in_specs=in_hbm(6),
        out_specs=tuple(whole(4)),
        scratch_shapes=[
            pltpu.VMEM((members, planes - 1, rows, cols), jnp.float32),
            pltpu.VMEM((rows, cols), jnp.int32),
            pltpu.SemaphoreType.DMA((members, 6)),
        ],
        compiler_params=pltpu.CompilerParams(vmem_limit_bytes=WHOLE_VMEM),
        name="pack_rims",
    )(temp, salt, uvel, vvel, eta, mask)


def east_west(value):
    width = value.shape[-1]
    return pltpu.roll(value, width - 1, 1), pltpu.roll(value, 1, 1)


def chunks(first, last):
    return [(a, min(a + CHUNK, last)) for a in range(first, last, CHUNK)]


def assemble(ext, mask, rims, m, levels, total_rows):
    from_east, from_west, rows_first, rows_second, sides_first, sides_second = rims
    planes = 4 * levels + 2
    rows, cols = mask.shape
    tile_row = lax.axis_index("gridy")
    odd_tile = lax.rem(tile_row, 2).astype(jnp.float32)
    keep_south = jnp.where(tile_row > 0, 1.0, 0.0).astype(jnp.float32)
    keep_north = jnp.where(tile_row * rows + rows < total_rows, 1.0, 0.0).astype(jnp.float32)
    north_factors = keep_north * (1.0 - odd_tile), keep_north * odd_tile
    south_factors = keep_south * odd_tile, keep_south * (1.0 - odd_tile)

    def of_north(first, second):
        return north_factors[0] * first + north_factors[1] * second

    def of_south(first, second):
        return south_factors[0] * first + south_factors[1] * second

    wide = groups_of(planes) * LANE
    for group in range(groups_of(planes)):
        where = slice(group * LANE, (group + 1) * LANE)
        where_west = slice(wide + group * LANE, wide + (group + 1) * LANE)
        east = sides_first[m, :, where], sides_second[m, :, where]
        west = sides_first[m, :, where_west], sides_second[m, :, where_west]
        bands = [(TOP - CHUNK, of_south(*east), of_south(*west))]
        for a in range(0, rows, CHUNK):
            bands.append((TOP + a, from_east[m, a : a + CHUNK, where], from_west[m, a : a + CHUNK, where]))
        bands.append((TOP + rows, of_north(*east), of_north(*west)))
        for at, east, west in bands:
            odd = ((lanes_like(east.shape) // WIDE) & 1) == 1
            joined = (jnp.where(odd, east, west), jnp.where(odd, west, east))
            for plane in range(group * PER_GROUP, min((group + 1) * PER_GROUP, planes)):
                _, kind, offset = rim_place(plane)
                ext[plane, at : at + CHUNK, cols : cols + LANE] = pltpu.roll(joined[kind], LANE - offset, 1)
    ext[planes - 1, TOP : TOP + rows, :cols] = mask[...].astype(jnp.float32)
    for plane in range(planes):
        at = slice(plane * WIDE, (plane + 1) * WIDE)
        ext[plane, TOP - WIDE : TOP, :cols] = of_south(rows_first[m, at, :], rows_second[m, at, :])
        ext[plane, TOP + rows : TOP + rows + WIDE, :cols] = of_north(rows_first[m, at, :], rows_second[m, at, :])


def fill_rows(turn, inside, first_row, total_rows):
    shape = (CHUNK, turn.shape[1])
    for a in range(0, turn.shape[0], CHUNK):
        row = first_row + (a - TOP) + lax.broadcasted_iota(jnp.int32, shape, 0)
        latitude = row.astype(jnp.float32) + 0.5
        turn[a : a + CHUNK, :] = STEP_DT * CORI_K * (2.0 * latitude / total_rows - 1.0)
        inside[a : a + CHUNK, :] = jnp.where((row >= 0) & (row < total_rows), 1.0, 0.0)


KEPT = ["tu", "tv", "q", "v0", "v1", "v2"]
KEEP_FLOW = 1.0 - STEP_DT * DRAG_K - 4.0 * VISCOSITY
KEEP_TRACER = 1.0 - 4.0 * KAPPA
PRESS_SCALE = PRESS_K * 0.5 * STEP_DT


class Planes:
    def __init__(self, levels, rows, turn, inside):
        self.levels, self.rows, self.turn, self.inside = levels, rows, turn, inside
        self.views = {}

    def add(self, ref, names, lead=()):
        for i, name in enumerate(names):
            self.views[name] = ref.at[lead + (i,)]

    def get(self, name, a, b):
        return self.views[name][a:b, :]

    def put(self, name, a, b, value):
        self.views[name][a:b, :] = value

    def sides(self, name, a, b):
        here = self.get(name, a, b)
        east, west = east_west(here)
        return here, east, west, self.get(name, a + 1, b + 1), self.get(name, a - 1, b - 1)

    def slopes(self, name, a, b):
        _, east, west, north, south = self.sides(name, a, b)
        return east - west, north - south

    def around(self, name, a, b):
        here, east, west, north, south = self.sides(name, a, b)
        return here, (east + west) + (north + south)

    def main(self):
        return chunks(TOP, TOP + self.rows)

    def near(self):
        return [(TOP - 8, TOP)] + self.main() + [(TOP + self.rows, TOP + self.rows + 8)]

    def masked(self, a, b, value):
        if a >= TOP and b <= TOP + self.rows:
            return value
        return self.inside[a:b, :] * value

    def divergence(self, u_name, v_name, a, b):
        east, west = east_west(self.get(u_name, a, b))
        return DIV * ((east - west) + (self.get(v_name, a + 1, b + 1) - self.get(v_name, a - 1, b - 1)))

    def flow(self, u_name, v_name, press, out_u, out_v, a, b):
        ocean, turn = self.get("ocean", a, b), self.turn[a:b, :]
        u, around_u = self.around(u_name, a, b)
        v, around_v = self.around(v_name, a, b)
        push_u, push_v = turn * v, turn * u
        if press:
            slope_x, slope_y = self.slopes(press, a, b)
            push_u, push_v = push_u - slope_x, push_v + slope_y
        self.put(out_u, a, b, ocean * ((KEEP_FLOW * u + VISCOSITY * around_u) + push_u))
        self.put(out_v, a, b, ocean * ((KEEP_FLOW * v + VISCOSITY * around_v) - push_v))

    def powers(self, first, second, third):
        for a, b in self.near():
            self.put(second, a, b, self.masked(a, b, self.around(first, a, b)[1]))
        for a, b in self.near():
            value = self.around(second, a, b)[1] - 4.0 * self.get(first, a, b)
            self.put(third, a, b, self.masked(a, b, value))

    def next_right_side(self, u_name, v_name, eta_name, press, out_name):
        for a, b in self.near():
            self.flow(u_name, v_name, press, "t2u", "t2v", a, b)
        for a, b in self.near():
            div = self.divergence("t2u", "t2v", a, b)
            value = self.get(eta_name, a, b) - div if eta_name else -div
            self.put(out_name, a, b, self.masked(a, b, value))


def scaled(factor, value):
    return value if factor == 1.0 else factor * value


def surface_start(ext, work):
    levels = work.levels
    low, high = TOP - CHUNK, TOP + work.rows + CHUNK
    for a, b in chunks(low, high):
        su = sv = sp = None
        for l in range(levels):
            factor = PRESS_SCALE * (levels - l)
            dens = (factor * BETA_S) * ext[levels + l, a:b, :] - (factor * ALPHA_T) * ext[l, a:b, :]
            work.put("d%d" % l, a, b, dens)
            u, v = ext[2 * levels + l, a:b, :], ext[3 * levels + l, a:b, :]
            su, sv, sp = (u, v, dens) if l == 0 else (su + u, sv + v, sp + dens)
        work.put("su", a, b, su)
        work.put("sv", a, b, sv)
        work.put("sp", a, b, sp)
    for a, b in work.near():
        carried = None
        for l in range(levels):
            slope_x, slope_y = work.slopes("d%d" % l, a, b)
            term = ext[2 * levels + l, a:b, :] * slope_x + ext[3 * levels + l, a:b, :] * slope_y
            carried = term if l == 0 else carried + term
        here, around = work.around("sp", a, b)
        work.put("q", a, b, work.get("ocean", a, b) * ((KEEP_TRACER * here + KAPPA * around) - ADV * carried))
    for a, b in chunks(low, high):
        work.flow("su", "sv", "sp", "tu", "tv", a, b)
    for a, b in work.near():
        work.put("v0", a, b, work.masked(a, b, work.get("eta", a, b) - work.divergence("tu", "tv", a, b)))


SUM_NAMES = ["su", "sv", "sp", "v3", "pu", "pv", "t2u", "t2v"] + ["w%d_%d" % (i, k) for i in range(4) for k in range(4)]


def whether(*conditions):
    result = jnp.int32(0)
    for condition in conditions:
        result = jnp.where(condition, 1, result)
    return result


def choose(source, theirs, side, members, info):
    mine, away = side * members, (1 - side) * members
    sent = [whether(*[theirs[slot] == mine + m for slot in range(members)]) for m in range(2)]
    here = [whether(*[source[slot] == away + m for slot in range(members)]) for m in range(2)]
    first_sent, first_here = 1 - sent[0], 1 - here[0]
    for slot in range(members):
        own = jnp.where(source[slot] - mine == first_sent, 0, 1)
        far = jnp.where(source[slot] - away == first_here, 2, 3)
        info[slot] = jnp.where((source[slot] >= mine) & (source[slot] < mine + members), own, far)
    info[members] = jnp.maximum(sent[0] * sent[1], here[0] * here[1])
    info[members + 1] = jnp.int32(1)
    info[members + 2] = first_sent


def sums_kernel(levels, total_rows, source, theirs, *refs):
    fields, rims, out, kept, info = refs[:6], refs[6:12], refs[12], refs[13], refs[14]
    planes, turn, inside, red, mask, sems = refs[15:]
    members = kept.shape[0]
    rows, cols = mask.shape
    copies = fetches(fields, lambda m, at: kept.at[m, at, pl.ds(TOP, rows), pl.ds(0, cols)], mask, sems, levels)
    tile_row = lax.axis_index("gridy")
    choose(source, theirs, lax.axis_index("member"), members, info)
    fill_rows(turn, inside, tile_row * rows, total_rows)
    red[...] = jnp.zeros_like(red)
    for m in range(members):
        assemble(kept.at[m], mask, rims, m, levels, total_rows)
    for copy in sum(copies, []):
        copy.wait()

    def one(m, carry):
        ext = kept.at[m]
        work = Planes(levels, rows, turn, inside)
        work.add(planes, SUM_NAMES + ["d%d" % l for l in range(levels)])
        work.add(kept, ["ext%d" % i for i in range(4 * levels)] + ["eta", "ocean"] + KEPT, (m,))
        surface_start(ext, work)
        work.powers("v0", "v1", "v2")
        for a, b in work.main():
            work.put("v3", a, b, work.around("v2", a, b)[1])
        work.next_right_side("tu", "tv", None, "q", "w0_0")
        for k in range(1, 4):
            name = "v%d" % (k - 1)
            for a, b in work.near():
                ocean = work.get("ocean", a, b)
                slope_x, slope_y = work.slopes(name, a, b)
                work.put("pu", a, b, scaled(-levels * GRAV, ocean * slope_x))
                work.put("pv", a, b, scaled(-levels * GRAV, ocean * slope_y))
            work.next_right_side("pu", "pv", name, None, "w0_%d" % k)
        for k in range(4):
            work.powers("w0_%d" % k, "w1_%d" % k, "w2_%d" % k)
            for a, b in work.main():
                work.put("w3_%d" % k, a, b, work.around("w2_%d" % k, a, b)[1])

        def put_sums(at, first, second, pairs):
            totals = [None] * len(pairs)
            for a in range(TOP, TOP + rows, 8):
                xs = [work.get(name, a, a + 8)[:, :cols] for name in first]
                ys = [work.get(name, a, a + 8)[:, :cols] for name in second]
                for p, (i, j) in enumerate(pairs):
                    term = xs[i] * ys[j]
                    totals[p] = term if totals[p] is None else totals[p] + term
            for p, total in enumerate(totals):
                folded = total[:, :LANE]
                for c in range(LANE, cols, LANE):
                    folded = folded + total[:, c : c + LANE]
                red[m, at + p : at + p + 1, :] = jnp.sum(folded, axis=0, keepdims=True)

        for i in range(6):
            low, high = i // 2, i - i // 2
            put_sums(i, ["v%d" % low], ["v%d" % high], [(0, 0)])
            names = [["w%d_%d" % (which, k) for k in range(4)] for which in (low, high)]
            put_sums(6 + i * len(PAIRS), names[0], names[1], PAIRS)
        return carry

    lax.fori_loop(0, members, one, 0)
    for m in range(members):
        out[m : m + 1, :] = jnp.sum(jnp.transpose(red[m]), axis=0, keepdims=True)


def plane_shape(rows, cols):
    return (2 * TOP + rows, cols + LANE)


def local_sums(source, theirs, fields, rims, total_rows):
    members, levels, rows, cols = fields[0].shape
    assert SUMS <= LANE and members <= 8
    shape = plane_shape(rows, cols)
    kept = (members, 4 * levels + 2 + len(KEPT)) + shape
    return pl.pallas_call(
        functools.partial(sums_kernel, levels, total_rows),
        out_shape=(
            jax.ShapeDtypeStruct((members, LANE), jnp.float32),
            jax.ShapeDtypeStruct(kept, jnp.float32),
            jax.ShapeDtypeStruct((members + 3,), jnp.int32),
        ),
        in_specs=in_smem(2) + in_hbm(6) + whole(6),
        out_specs=tuple(whole(2) + in_smem(1)),
        scratch_shapes=[
            pltpu.VMEM((len(SUM_NAMES) + levels,) + shape, jnp.float32),
            pltpu.VMEM(shape, jnp.float32),
            pltpu.VMEM(shape, jnp.float32),
            pltpu.VMEM((members, LANE, LANE), jnp.float32),
            pltpu.VMEM((rows, cols), jnp.int32),
            pltpu.SemaphoreType.DMA((members, 6)),
        ],
        compiler_params=pltpu.CompilerParams(vmem_limit_bytes=VMEM_LIMIT),
        cost_estimate=pl.CostEstimate(flops=10**8, bytes_accessed=4 * 10**6, transcendentals=0),
        name="local_sums",
    )(source, theirs, *fields, *rims)


def krylov(moment):
    n00, n01, n11, n12, n22, x22 = moment
    n02 = n11 - 4.0 * n00
    main, near = 1.0 + 4.0 * SURF_C, SURF_C
    g00 = main * n00 - near * n01
    g01 = main * n01 - near * n11
    g02 = main * n02 - near * n12
    g11 = main * n11 - near * (n12 + 4.0 * n01)
    g12 = main * n12 - near * (n22 + 4.0 * n02)
    g22 = main * n22 - near * x22
    l1, l2 = g01 / g00, g02 / g00
    d1 = g11 - l1 * g01
    d1 = jnp.where(d1 > 3e-7 * g11, d1, jnp.inf)
    e = g12 - l1 * g02
    l12 = e / d1
    d2 = g22 - l2 * g02 - l12 * e
    d2 = jnp.where(d2 > 3e-7 * g22, d2, jnp.inf)
    z0 = n00
    z1 = n01 - l1 * z0
    z2 = n02 - l2 * z0 - l12 * z1
    y2 = z2 / d2
    y1 = z1 / d1 - l12 * y2
    y0 = z0 / g00 - l1 * y1 - l2 * y2
    return [y0, y1, y2]


def weights(read):
    first = krylov([read(i) for i in range(6)])
    lifted = [None] + first
    second = []
    for i in range(6):
        total = None
        for p, (a, b) in enumerate(PAIRS):
            term = read(6 + i * len(PAIRS) + p)
            for k in (a, b):
                if k:
                    term = term * lifted[k]
            if a != b:
                term = 2.0 * term
            total = term if total is None else total + term
        second.append(total)
    return first, krylov(second)


RUN_NAMES = ["pu", "pv", "t2u", "t2v", "eta1", "w0", "w1", "w2", "eta2", "p", "p2", "gu1", "gv1", "gu2", "gv2"]


def advance_kernel(levels, total_rows, is_first, *refs):
    if is_first:
        info, tiles, kept, out, zonal = refs[:5]
        scratch = refs[5:]
    else:
        info, tiles, kept, zonal_before, out, spread = refs[:6]
        scratch = refs[6:]
    planes, after, turn, inside, staged, sums, sem = scratch[:7]
    rows, cols = out.shape[1:]
    members = kept.shape[0]
    tile_row = lax.axis_index("gridy")
    total = tiles[0]
    for i in range(1, tiles.shape[0]):
        total = total + tiles[i]
    staged[0:members, :] = total
    copy = pltpu.make_async_copy(staged, sums, sem)
    copy.start()
    fill_rows(turn, inside, tile_row * rows, total_rows)
    if not is_first:
        zonal = scratch[7]
    zonal[...] = jnp.zeros_like(zonal) if is_first else zonal_before[...]
    copy.wait()
    member = info[members + 2] if is_first else 1 - info[members + 2]
    ext = kept.at[member]
    work = Planes(levels, rows, turn, inside)
    work.add(planes, RUN_NAMES)
    work.add(kept, ["ext%d" % i for i in range(4 * levels)] + ["eta", "ocean"] + KEPT, (member,))

    def read(i):
        return jnp.full((1, 1), sums[member, i], jnp.float32)

    def combine(factors, names, out_name):
        for a, b in work.near():
            value = None
            for factor, name in zip(factors, names):
                term = factor * work.get(name, a, b)
                value = term if value is None else value + term
            work.put(out_name, a, b, value)

    first, second = weights(read)
    combine(first, ("v0", "v1", "v2"), "eta1")
    for a, b in work.near():
        ocean = work.get("ocean", a, b)
        slope_x, slope_y = work.slopes("eta1", a, b)
        slope_x, slope_y = GRAV * ocean * slope_x, GRAV * ocean * slope_y
        work.put("gu1", a, b, slope_x)
        work.put("gv1", a, b, slope_y)
        work.put("pu", a, b, work.get("tu", a, b) - levels * slope_x)
        work.put("pv", a, b, work.get("tv", a, b) - levels * slope_y)
    work.next_right_side("pu", "pv", "eta1", "q", "w0")
    work.powers("w0", "w1", "w2")
    combine(second, ("w0", "w1", "w2"), "eta2")
    for a, b in work.main():
        ocean = work.get("ocean", a, b)
        slope_x, slope_y = work.slopes("eta2", a, b)
        work.put("gu2", a, b, GRAV * ocean * slope_x)
        work.put("gv2", a, b, GRAV * ocean * slope_y)
        out[4 * levels, a - TOP : b - TOP, :] = work.get("eta2", a, b)[:, :cols]
    low, high = TOP - 8, TOP + rows + 8
    for a, b in chunks(TOP - CHUNK, TOP + rows + CHUNK):
        work.put("p", a, b, jnp.zeros((b - a, cols + LANE), jnp.float32))
        work.put("p2", a, b, jnp.zeros((b - a, cols + LANE), jnp.float32))

    def step(ref, l, press, a, b, width):
        def of(view):
            here = view[a:b, :]
            east, west = east_west(here)
            return here[:, :width], east[:, :width], west[:, :width], view[a + 1 : b + 1, :width], view[a - 1 : b - 1, :width]

        ocean = work.views["ocean"][a:b, :width]
        coriolis = turn[a:b, :width]
        u, east, west, north, south = of(ref.at[2 * levels + l])
        around_u = (east + west) + (north + south)
        v, east, west, north, south = of(ref.at[3 * levels + l])
        around_v = (east + west) + (north + south)
        _, east, west, north, south = of(work.views[press])
        new_u = ocean * ((KEEP_FLOW * u + VISCOSITY * around_u) + (coriolis * v - (east - west)))
        new_v = ocean * ((KEEP_FLOW * v + VISCOSITY * around_v) - (coriolis * u + (north - south)))
        flow_u, flow_v = ADV * u, ADV * v
        results = []
        for at in (l, levels + l):
            here, east, west, north, south = of(ref.at[at])
            carried = flow_u * (east - west) + flow_v * (north - south)
            spread = KEEP_TRACER * here + KAPPA * ((east + west) + (north + south))
            results.append(ocean * (spread - carried))
        return results[0], results[1], new_u, new_v

    def add_press(ref, l, press, a, b):
        dens = (PRESS_SCALE * BETA_S) * ref[levels + l, a:b, :] - (PRESS_SCALE * ALPHA_T) * ref[l, a:b, :]
        work.put(press, a, b, work.get(press, a, b) + dens)

    def level(l, carry):
        for a in range(TOP - CHUNK, TOP + rows + CHUNK, 8):
            add_press(ext, l, "p", a, a + 8)
        for a in range(low, high, 8):
            temp, salt, u, v = step(ext, l, "p", a, a + 8, cols + LANE)
            after[l, a : a + 8, :] = temp
            after[levels + l, a : a + 8, :] = salt
            after[2 * levels + l, a : a + 8, :] = u - work.get("gu1", a, a + 8)
            after[3 * levels + l, a : a + 8, :] = v - work.get("gv1", a, a + 8)
        for a in range(low, high, 8):
            add_press(after, l, "p2", a, a + 8)
        for a in range(TOP, TOP + rows, 8):
            temp, salt, u, v = step(after, l, "p2", a, a + 8, cols)
            here = slice(a - TOP, a - TOP + 8)
            v = v - work.get("gv2", a, a + 8)[:, :cols]
            out[l, here, :] = temp
            out[levels + l, here, :] = salt
            out[2 * levels + l, here, :] = u - work.get("gu2", a, a + 8)[:, :cols]
            out[3 * levels + l, here, :] = v
            row_sum = jnp.sum(v, axis=1, keepdims=True)
            zonal[here, :] = jnp.where(lanes_like((8, LANE)) == member * levels + l, row_sum, zonal[here, :])
        return carry

    lax.fori_loop(0, levels, level, 0)
    if not is_first:
        square = jnp.concatenate([zonal[...]] + [jnp.zeros_like(zonal)] * (LANE // rows - 1), axis=0)
        turned = jnp.transpose(square)[: members * levels]
        line = turned[:levels]
        for m in range(1, members):
            line = line + pltpu.roll(turned, m * rows, 1)[m * levels : (m + 1) * levels]
        for i in range(spread.shape[0]):
            spread[i] = line


def advance(is_first, info, tiles, kept, zonal, rows, cols, total_rows):
    members, planes = kept.shape[:2]
    levels = (planes - 2 - len(KEPT)) // 4
    assert members * rows == LANE and members * levels == 8
    shape = plane_shape(rows, cols)
    zonal_shape = jax.ShapeDtypeStruct((rows, LANE), jnp.float32)
    out_shape = [jax.ShapeDtypeStruct((4 * levels + 1, rows, cols), jnp.float32)]
    if is_first:
        out_shape += [zonal_shape]
    else:
        out_shape += [jax.ShapeDtypeStruct((tiles.shape[0], levels, members * rows), jnp.float32)]
    return pl.pallas_call(
        functools.partial(advance_kernel, levels, total_rows, is_first),
        out_shape=tuple(out_shape),
        in_specs=in_smem(1) + whole(2 if is_first else 3),
        out_specs=tuple(whole(2)),
        scratch_shapes=[
            pltpu.VMEM((len(RUN_NAMES),) + shape, jnp.float32),
            pltpu.VMEM((4 * levels,) + shape, jnp.float32),
            pltpu.VMEM(shape, jnp.float32),
            pltpu.VMEM(shape, jnp.float32),
            pltpu.VMEM((8, LANE), jnp.float32),
            pltpu.SMEM((8, LANE), jnp.float32),
            pltpu.SemaphoreType.DMA,
        ]
        + ([] if is_first else [pltpu.VMEM((rows, LANE), jnp.float32)]),
        compiler_params=pltpu.CompilerParams(vmem_limit_bytes=VMEM_LIMIT),
        cost_estimate=pl.CostEstimate(flops=10**8, bytes_accessed=4 * 10**6, transcendentals=0),
        name="advance",
    )(info, tiles, kept, *([] if is_first else [zonal]))


def finish_kernel(count_y, count_x, total_cols, spread, overturn, score, held):
    members, levels, rows = overturn.shape
    total_rows = rows * count_y
    lane = lanes_like(spread.shape[1:])
    member_of = lane // rows
    weighted = None
    for y in range(count_y):
        total = spread[y * count_x]
        for x in range(1, count_x):
            total = total + spread[y * count_x + x]
        lines = [total[0:1]]
        for l in range(1, levels):
            lines.append(lines[-1] + total[l : l + 1])
        lines = jnp.concatenate(lines, axis=0) * (total_cols**-0.5)
        held[y] = lines
        latitude = ((lane - member_of * rows + y * rows).astype(jnp.float32) + 0.5) * (1.0 / total_rows)
        weighted = lines * latitude if weighted is None else weighted + lines * latitude
    mine = held[lax.axis_index("gridy")]
    for m in range(members):
        overturn[m] = mine[:, m * rows : (m + 1) * rows]
        score[m] = jnp.sum(jnp.where(member_of == m, weighted, 0.0)) * ((levels * total_rows) ** -0.5)


def finish(spread, members, rows, count_y, count_x, cols):
    levels = spread.shape[1]
    return pl.pallas_call(
        functools.partial(finish_kernel, count_y, count_x, cols * count_x),
        out_shape=(
            jax.ShapeDtypeStruct((members, levels, rows), jnp.float32),
            jax.ShapeDtypeStruct((members,), jnp.float32),
        ),
        in_specs=whole(1),
        out_specs=(whole(1)[0], in_smem(1)[0]),
        scratch_shapes=[pltpu.VMEM((count_y,) + spread.shape[1:], jnp.float32)],
        compiler_params=pltpu.CompilerParams(vmem_limit_bytes=VMEM_LIMIT),
        name="finish",
    )(spread)


def pick_kernel(levels, choice, source, score, their_score, *refs):
    count = len(refs) - 7
    sources, outs, weight, sem = refs[:count], refs[count : count + 5], refs[count + 5], refs[count + 6]
    slots = outs[0].shape[0]

    def parts(s, source):
        for f in range(4):
            yield source.at[pl.ds(f * levels, levels)], outs[f].at[s]
        yield source.at[4 * levels], outs[4].at[s]

    for s in range(slots):
        for k in range(count):

            @pl.when(choice[s] == k)
            def _():
                for i, (one, target) in enumerate(parts(s, sources[k])):
                    pltpu.make_async_copy(one, target, sem.at[s, i]).start()

    side = lax.axis_index("member")
    mean = (sum(score[m] for m in range(slots)) + sum(their_score[m] for m in range(slots))) * (0.5 / slots)
    for s in range(slots):
        value = jnp.float32(0.0)
        for m in range(slots):
            value = jnp.where(source[s] == side * slots + m, score[m], value)
            value = jnp.where(source[s] == (1 - side) * slots + m, their_score[m], value)
        weight[s] = value - mean
    for s in range(slots):
        for i, (one, target) in enumerate(parts(s, sources[0])):
            pltpu.make_async_copy(one, target, sem.at[s, i]).wait()


def pick(choice, source, score, their_score, sources, slots, levels):
    _, rows, cols = sources[0].shape
    volume = jax.ShapeDtypeStruct((slots, levels, rows, cols), jnp.float32)
    surface = jax.ShapeDtypeStruct((slots, rows, cols), jnp.float32)
    return pl.pallas_call(
        functools.partial(pick_kernel, levels),
        out_shape=(volume,) * 4 + (surface, jax.ShapeDtypeStruct((slots,), jnp.float32)),
        in_specs=in_smem(4) + whole(len(sources)),
        out_specs=tuple(in_hbm(5) + in_smem(1)),
        scratch_shapes=[pltpu.SemaphoreType.DMA((slots, 5))],
        compiler_params=pltpu.CompilerParams(vmem_limit_bytes=VMEM_LIMIT),
        name="pick",
    )(choice, source, score, their_score, *sources)


def shift(value, axis, by):
    count = lax.axis_size(axis)
    return lax.ppermute(value, axis, [(i, (i + by) % count) for i in range(count)])


def exchange_rims(packed):
    to_west, to_east, rows_first, rows_second = packed
    rows = to_west.shape[1]
    count = lax.axis_size("gridy")
    assert count % 2 == 0
    partners = [i ^ 1 for i in range(count)], [min(max(i - 1 + 2 * (i % 2), 0), count - 1) for i in range(count)]

    def pair(value, which):
        return lax.ppermute(value, "gridy", list(enumerate(partners[which])))

    from_east, from_west = shift(to_west, "gridx", -1), shift(to_east, "gridx", 1)
    rows_first, rows_second = pair(rows_first, 0), pair(rows_second, 1)
    low = jnp.concatenate([from_east[:, :CHUNK], from_west[:, :CHUNK]], axis=2)
    high = jnp.concatenate([from_east[:, rows - CHUNK :], from_west[:, rows - CHUNK :]], axis=2)
    even = lax.axis_index("gridy") % 2 == 0
    sides_first = pair(jnp.where(even, high, low), 0)
    sides_second = pair(jnp.where(even, low, high), 1)
    return from_east, from_west, rows_first, rows_second, sides_first, sides_second


def from_all(tiles, axes):
    return lax.all_to_all(tiles, axes, split_axis=0, concat_axis=0, tiled=True)


def swap(value):
    return lax.ppermute(value, "member", [(0, 1), (1, 0)])


def shards(temp, salt, uvel, vvel, eta, land_mask, clone_source):
    members, levels, rows, cols = temp.shape
    assert members == 2 and lax.axis_size("member") == 2
    count_y, count_x = lax.axis_size("gridy"), lax.axis_size("gridx")
    total_rows = rows * count_y
    grid = ("gridy", "gridx")

    their_source = swap(clone_source)
    fields = (temp, salt, uvel, vvel, eta, land_mask)
    rims = exchange_rims(pack_rims(*fields))
    tile, kept, info = local_sums(clone_source, their_source, fields, rims, total_rows)
    tiles = from_all(jnp.broadcast_to(tile[None], (count_y * count_x,) + tile.shape), grid)

    sent, zonal = advance(True, info, tiles, kept, None, rows, cols, total_rows)
    arrived = swap(sent)

    def rest():
        other, spread = advance(False, info, tiles, kept, zonal, rows, cols, total_rows)
        return (other, *finish(from_all(spread, grid), members, rows, count_y, count_x, cols))

    def nothing():
        return jnp.zeros_like(sent), jnp.zeros((members, levels, rows), jnp.float32), jnp.zeros((members,), jnp.float32)

    other, overturn, score = lax.cond(info[members + 1] != 0, rest, nothing)
    their_score = swap(score)

    def with_second():
        sources = (sent, other, arrived, swap(other))
        return pick(info, clone_source, score, their_score, sources, members, levels)

    def without_second():
        return pick(info, clone_source, score, their_score, (sent, other, arrived), members, levels)

    *picked, clone_weight = lax.cond(info[members] != 0, with_second, without_second)
    return (*picked, overturn, clone_weight)


def solution(mesh):
    volume = P("member", None, "gridy", "gridx")
    in_specs = (volume,) * 4 + (P("member", "gridy", "gridx"), P("gridy", "gridx"), P("member"))
    out_specs = (volume,) * 4 + (P("member", "gridy", "gridx"), P("member", None, "gridy"), P("member"))
    return jax.shard_map(shards, mesh=mesh, in_specs=in_specs, out_specs=out_specs, check_vma=False)
```

profile of v0, /device:TPU:0, one launch (start us, length us, event | category | flops | bytes accessed | tf_op | source)
XLA Modules:
  0.0 76.0 jit_solution(752940834162288730)
XLA Ops:
  0.7 2.9 %pack_rims.1 = (f32[2,64,256]{2,1,0:T(8,128)}, f32[2,64,256]{2,1,0:T(8,128)}, f32[2,184,256]{2,1,0:T(8,128)}, f32[2,184,256]{2,1,0:T(8,128)}) custom-call(f32[2,4,64,256]{3,2,1,0:T(8,128)} %refs_0_.3, f32[2,4,64,256]{3,2,1,0:T(8,128)} %refs_1_.3, f32[2,4,64,256]{3,2,1,0:T(8,128)} %refs_2_.3, f32[2,4,64,256]{3,2,1,0:T(8,128)} %refs_3_.3, ...), custom_call_target="tpu_custom_call" | custom-call | tf_op jit(solution)/shard_map/pack_rims/pallas_call | solution.py:121
  3.6 5.1 %collective-permute-start.2 = (f32[2,64,256]{2,1,0:T(8,128)}, f32[2,64,256]{2,1,0:T(8,128)S(1)}, u32[]{:S(2)}, u32[]{:S(2)}) collective-permute-start(f32[2,64,256]{2,1,0:T(8,128)} %get-tuple-element.83), channel_id=1, source_target_pairs={{0,3},{1,0},{2,1},{3,2},{4,7},{5,4},{6,5},{7,6},{8,11},{9,8},{10,9... | collective-permute-start | bytes 393224 | tf_op jit(solution)/shard_map/ppermute | solution.py:713
  8.7 0.0 collective-permute-start.3
  8.7 0.0 collective-permute-start.4
  8.7 1.6 %collective-permute-start.5 = (f32[2,184,256]{2,1,0:T(8,128)}, f32[2,184,256]{2,1,0:T(8,128)S(1)}, u32[]{:S(2)}, u32[]{:S(2)}) collective-permute-start(f32[2,184,256]{2,1,0:T(8,128)} %get-tuple-element.86), channel_id=1, source_target_pairs={{0,0},{4,8},{8,4},{12,12},{1,1},{5,9},{9,5},{13,13},{2,2},{6,10},{... | collective-permute-start | bytes 1130504 | tf_op jit(solution)/shard_map/ppermute | solution.py:724
  10.3 2.6 %collective-permute-done.2.refs_6_ = f32[2,64,256]{2,1,0:T(8,128)S(1)} collective-permute-done((f32[2,64,256]{2,1,0:T(8,128)}, f32[2,64,256]{2,1,0:T(8,128)S(1)}, u32[]{:S(2)}, u32[]{:S(2)}) %collective-permute-start.2) | collective-permute-done | bytes 131104 | tf_op jit(solution)/shard_map/ppermute | solution.py:713
  12.9 2.8 %collective-permute-done.3.refs_7_ = f32[2,64,256]{2,1,0:T(8,128)S(1)} collective-permute-done((f32[2,64,256]{2,1,0:T(8,128)}, f32[2,64,256]{2,1,0:T(8,128)S(1)}, u32[]{:S(2)}, u32[]{:S(2)}) %collective-permute-start.3) | collective-permute-done | bytes 131104 | tf_op jit(solution)/shard_map/ppermute | solution.py:713
  15.7 0.7 collective-permute-start.7
  16.3 2.9 %collective-permute-start.6 = (f32[2,16,512]{2,1,0:T(8,128)S(1)}, f32[2,16,512]{2,1,0:T(8,128)S(1)}, u32[]{:S(2)}, u32[]{:S(2)}) collective-permute-start(f32[2,16,512]{2,1,0:T(8,128)S(1)} %get-tuple-element.102), channel_id=1, source_target_pairs={{0,4},{4,0},{8,12},{12,8},{1,5},{5,1},{9,13},{13,9},{2,6},{6,2},{1... | collective-permute-start | bytes 196616 | tf_op jit(solution)/shard_map/ppermute | solution.py:724
  19.3 1.5 %collective-permute-start.1 = (s32[2]{0:T(128)S(1)}, s32[2]{0:T(128)S(1)}, u32[]{:S(2)}, u32[]{:S(2)}) collective-permute-start(s32[2]{0:T(128)S(1)} %copy-done.6), channel_id=1, source_target_pairs={{0,16},{16,0},{1,17},{17,1},{2,18},{18,2},{3,19},{19,3},{4,20},{20... | collective-permute-start | bytes 32 | tf_op jit(solution)/shard_map/ppermute | solution.py:741
  20.8 2.0 %collective-permute-done.1.theirs = s32[2]{0:T(128)S(1)} collective-permute-done((s32[2]{0:T(128)S(1)}, s32[2]{0:T(128)S(1)}, u32[]{:S(2)}, u32[]{:S(2)}) %collective-permute-start.1) | collective-permute-done | bytes 40 | tf_op jit(solution)/shard_map/ppermute | solution.py:741
  22.9 8.4 %local_sums.1 = (f32[2,128]{1,0:T(2,128)S(1)}, f32[2,24,112,384]{3,2,1,0:T(8,128)S(1)}, s32[5]{0:T(128)S(1)}) custom-call(s32[2]{0:T(128)S(1)} %copy-done.6, s32[2]{0:T(128)S(1)} %collective-permute-done.1.theirs, f32[2,4,64,256]{3,2,1,0:T(8,128)S(1)} %copy-done, f32[2,4,64,256]{3,2,1,0:T(8,128)S(1)} %copy-done.1, f32[2,4,64,256]{3,2,1,0:T(8,128)S(1)} %copy-done.2, ...), custom_call_target="tpu_custom_call" | custom-call | flops 100000000 | bytes 4000000 | tf_op jit(solution)/shard_map/local_sums/pallas_call | solution.py:399
  31.3 9.1 %all_to_all.10.refs_1_ = f32[16,2,128]{2,1,0:T(2,128)S(1)} all-to-all(f32[16,2,128]{2,1,0:T(2,128)S(1)} %broadcast_in_dim.2), channel_id=1, replica_groups=mesh['member'=2,'gridy'=4,'gridx'=4] {'gridy','gridx'}, dimensions={0} | all-to-all | bytes 32768 | tf_op jit(solution)/shard_map/all_to_all | solution.py:737
  40.3 6.5 %advance.3 = (f32[17,64,256]{2,1,0:T(8,128)S(1)}, f32[64,128]{1,0:T(8,128)S(1)}) custom-call(s32[5]{0:T(128)S(1)} %get-tuple-element.87.refs_0_, f32[16,2,128]{2,1,0:T(2,128)S(1)} %all_to_all.10.refs_1_, f32[2,24,112,384]{3,2,1,0:T(8,128)S(1)} %get-tuple-element.89.refs_2_), custom_call_target="tpu_custom_call" | custom-call | flops 100000000 | bytes 4000000 | tf_op jit(solution)/shard_map/advance/pallas_call | solution.py:605
  46.8 1.6 %collective-permute-start.9 = (f32[17,64,256]{2,1,0:T(8,128)S(1)}, f32[17,64,256]{2,1,0:T(8,128)S(1)}, u32[]{:S(2)}, u32[]{:S(2)}) collective-permute-start(f32[17,64,256]{2,1,0:T(8,128)S(1)} %get-tuple-element.92), channel_id=1, source_target_pairs={{0,16},{16,0},{1,17},{17,1},{2,18},{18,2},{3,19},{19,3},{4,20},{20... | collective-permute-start | bytes 3342344 | tf_op jit(solution)/shard_map/ppermute | solution.py:741
  48.4 0.6 fusion.4
  50.3 16.4 %conditional.2 = (f32[17,64,256]{2,1,0:T(8,128)S(1)}, f32[2,4,64]{2,1,0:T(4,128)}, f32[2]{0:T(128)S(1)}) conditional(s32[]{:T(128)} %bitcast.1, () %tuple.22, (s32[5]{0:T(128)S(1)}, f32[16,2,128]{2,1,0:T(2,128)S(1)}, f32[2,24,112,384]{3,2,1,0:T(8,128)S(1)}, f32[64,128]{1,0:T(8,128)S(1)}) %tuple.23), branch_computations={%region_0.1_spmd, %region_1.2_spmd} | conditional | flops 100000000 | bytes 4065560 | solution.py:767
  50.3 6.6 %advance.2 = (f32[17,64,256]{2,1,0:T(8,128)S(1)}, f32[16,4,128]{2,1,0:T(4,128)S(1)}) custom-call(s32[5]{0:T(128)S(1)} %get-tuple-element.36.refs_0_, f32[16,2,128]{2,1,0:T(2,128)S(1)} %get-tuple-element.37.refs_1_, f32[2,24,112,384]{3,2,1,0:T(8,128)S(1)} %get-tuple-element.38.refs_2_, f32[64,128]{1,0:T(8,128)S(1)} %get-tuple-element.39.refs_3_), custom_call_target="tpu_custom_call" | custom-call | flops 100000000 | bytes 4000000 | tf_op jit(solution)/shard_map/cond/branch_1_fun/advance/pallas_call | solution.py:605
  56.9 9.1 %all_to_all.9.spread = f32[16,4,128]{2,1,0:T(4,128)S(1)} all-to-all(f32[16,4,128]{2,1,0:T(4,128)S(1)} %get-tuple-element.41), channel_id=1, replica_groups=mesh['member'=2,'gridy'=4,'gridx'=4] {'gridy','gridx'}, dimensions={0} | all-to-all | bytes 65536 | tf_op jit(solution)/shard_map/cond/branch_1_fun/all_to_all | solution.py:737
  65.9 0.7 finish.1
  66.7 0.6 collective-permute-start.8
  67.2 6.3 %collective-permute-done.8 = f32[2]{0:T(128)S(1)} collective-permute-done((f32[2]{0:T(128)S(1)}, f32[2]{0:T(128)S(1)}, u32[]{:S(2)}, u32[]{:S(2)}) %collective-permute-start.8) | collective-permute-done | bytes 40 | tf_op jit(solution)/shard_map/ppermute | solution.py:741
  73.5 2.5 %conditional.3 = ((f32[2,4,64,256]{3,2,1,0:T(8,128)}, f32[2,4,64,256]{3,2,1,0:T(8,128)}, f32[2,4,64,256]{3,2,1,0:T(8,128)}, f32[2,4,64,256]{3,2,1,0:T(8,128)}, f32[2,64,256]{2,1,0:T(8,128)}, /*index=5*/f32[2]{0:T(128)})) conditional(s32[]{:T(128)} %bitcast, (s32[5]{0:T(128)S(1)}, s32[2]{0:T(128)S(1)}, f32[2]{0:T(128)S(1)}, f32[2]{0:T(128)S(1)}, ...), branch_computations={%region_2.3_spmd, %region_3.4_spmd} | conditional | bytes 4456496 | solution.py:777
  73.5 2.5 %pick.2 = (f32[2,4,64,256]{3,2,1,0:T(8,128)}, f32[2,4,64,256]{3,2,1,0:T(8,128)}, f32[2,4,64,256]{3,2,1,0:T(8,128)}, f32[2,4,64,256]{3,2,1,0:T(8,128)}, f32[2,64,256]{2,1,0:T(8,128)}, /*index=5*/f32[2]{0:T(128)}) custom-call(s32[5]{0:T(128)S(1)} %get-tuple-element.44.choice, s32[2]{0:T(128)S(1)} %get-tuple-element.45.source, f32[2]{0:T(128)S(1)} %get-tuple-element.46.score, ...), custom_call_target="tpu_custom_call" | custom-call | tf_op jit(solution)/shard_map/cond/branch_0_fun/pick/pallas_call | solution.py:700
  (23 shorter events, 0.1 us)
Async XLA Ops:
  0.6 22.2 %copy-start.5 = (s32[64,256]{1,0:T(8,128)S(1)}, s32[64,256]{1,0:T(8,128)}, u32[]{:S(2)}) copy-start(s32[64,256]{1,0:T(8,128)} %refs_5_.3) | copy-start | bytes 196612
  0.6 22.2 %copy-start.4 = (f32[2,64,256]{2,1,0:T(8,128)S(1)}, f32[2,64,256]{2,1,0:T(8,128)}, u32[]{:S(2)}) copy-start(f32[2,64,256]{2,1,0:T(8,128)} %refs_4_.3) | copy-start | bytes 393220
  0.7 22.2 %copy-start.3 = (f32[2,4,64,256]{3,2,1,0:T(8,128)S(1)}, f32[2,4,64,256]{3,2,1,0:T(8,128)}, u32[]{:S(2)}) copy-start(f32[2,4,64,256]{3,2,1,0:T(8,128)} %refs_3_.3) | copy-start | bytes 1572868
  0.7 22.2 %copy-start.2 = (f32[2,4,64,256]{3,2,1,0:T(8,128)S(1)}, f32[2,4,64,256]{3,2,1,0:T(8,128)}, u32[]{:S(2)}) copy-start(f32[2,4,64,256]{3,2,1,0:T(8,128)} %refs_2_.3) | copy-start | bytes 1572868
  0.7 22.2 %copy-start.1 = (f32[2,4,64,256]{3,2,1,0:T(8,128)S(1)}, f32[2,4,64,256]{3,2,1,0:T(8,128)}, u32[]{:S(2)}) copy-start(f32[2,4,64,256]{3,2,1,0:T(8,128)} %refs_1_.3) | copy-start | bytes 1572868
  0.7 22.2 %copy-start = (f32[2,4,64,256]{3,2,1,0:T(8,128)S(1)}, f32[2,4,64,256]{3,2,1,0:T(8,128)}, u32[]{:S(2)}) copy-start(f32[2,4,64,256]{3,2,1,0:T(8,128)} %refs_0_.3) | copy-start | bytes 1572868
  0.7 18.6 %copy-start.6 = (s32[2]{0:T(128)S(1)}, s32[2]{0:T(128)}, u32[]{:S(2)}) copy-start(s32[2]{0:T(128)} %source.1) | copy-start | bytes 28
  3.6 9.3 %collective-permute-start.2 = (f32[2,64,256]{2,1,0:T(8,128)}, f32[2,64,256]{2,1,0:T(8,128)S(1)}, u32[]{:S(2)}, u32[]{:S(2)}) collective-permute-start(f32[2,64,256]{2,1,0:T(8,128)} %get-tuple-element.83), channel_id=1, source_target_pairs={{0,3},{1,0},{2,1},{3,2},{4,7},{5,4},{6,5},{7,6},{8,11},{9,8},{10,9... | collective-permute-start | bytes 393224 | tf_op jit(solution)/shard_map/ppermute | solution.py:713
  8.7 7.0 %collective-permute-start.3 = (f32[2,64,256]{2,1,0:T(8,128)}, f32[2,64,256]{2,1,0:T(8,128)S(1)}, u32[]{:S(2)}, u32[]{:S(2)}) collective-permute-start(f32[2,64,256]{2,1,0:T(8,128)} %get-tuple-element.84), channel_id=1, source_target_pairs={{0,1},{1,2},{2,3},{3,0},{4,5},{5,6},{6,7},{7,4},{8,9},{9,10},{10,1... | collective-permute-start | bytes 393224 | tf_op jit(solution)/shard_map/ppermute | solution.py:713
  8.7 14.1 %collective-permute-start.4 = (f32[2,184,256]{2,1,0:T(8,128)}, f32[2,184,256]{2,1,0:T(8,128)S(1)}, u32[]{:S(2)}, u32[]{:S(2)}) collective-permute-start(f32[2,184,256]{2,1,0:T(8,128)} %get-tuple-element.85), channel_id=1, source_target_pairs={{0,4},{4,0},{8,12},{12,8},{1,5},{5,1},{9,13},{13,9},{2,6},{6,2},{1... | collective-permute-start | bytes 1130504 | tf_op jit(solution)/shard_map/ppermute | solution.py:724
  8.7 14.1 %collective-permute-start.5 = (f32[2,184,256]{2,1,0:T(8,128)}, f32[2,184,256]{2,1,0:T(8,128)S(1)}, u32[]{:S(2)}, u32[]{:S(2)}) collective-permute-start(f32[2,184,256]{2,1,0:T(8,128)} %get-tuple-element.86), channel_id=1, source_target_pairs={{0,0},{4,8},{8,4},{12,12},{1,1},{5,9},{9,5},{13,13},{2,2},{6,10},{... | collective-permute-start | bytes 1130504 | tf_op jit(solution)/shard_map/ppermute | solution.py:724
  15.7 7.1 %collective-permute-start.7 = (f32[2,16,512]{2,1,0:T(8,128)S(1)}, f32[2,16,512]{2,1,0:T(8,128)S(1)}, u32[]{:S(2)}, u32[]{:S(2)}) collective-permute-start(f32[2,16,512]{2,1,0:T(8,128)S(1)} %get-tuple-element.101), channel_id=1, source_target_pairs={{0,0},{4,8},{8,4},{12,12},{1,1},{5,9},{9,5},{13,13},{2,2},{6,10},{... | collective-permute-start | bytes 196616 | tf_op jit(solution)/shard_map/ppermute | solution.py:724
  16.3 6.5 %collective-permute-start.6 = (f32[2,16,512]{2,1,0:T(8,128)S(1)}, f32[2,16,512]{2,1,0:T(8,128)S(1)}, u32[]{:S(2)}, u32[]{:S(2)}) collective-permute-start(f32[2,16,512]{2,1,0:T(8,128)S(1)} %get-tuple-element.102), channel_id=1, source_target_pairs={{0,4},{4,0},{8,12},{12,8},{1,5},{5,1},{9,13},{13,9},{2,6},{6,2},{1... | collective-permute-start | bytes 196616 | tf_op jit(solution)/shard_map/ppermute | solution.py:724
  19.3 3.5 %collective-permute-start.1 = (s32[2]{0:T(128)S(1)}, s32[2]{0:T(128)S(1)}, u32[]{:S(2)}, u32[]{:S(2)}) collective-permute-start(s32[2]{0:T(128)S(1)} %copy-done.6), channel_id=1, source_target_pairs={{0,16},{16,0},{1,17},{17,1},{2,18},{18,2},{3,19},{19,3},{4,20},{20... | collective-permute-start | bytes 32 | tf_op jit(solution)/shard_map/ppermute | solution.py:741
  46.8 26.7 %collective-permute-start.9 = (f32[17,64,256]{2,1,0:T(8,128)S(1)}, f32[17,64,256]{2,1,0:T(8,128)S(1)}, u32[]{:S(2)}, u32[]{:S(2)}) collective-permute-start(f32[17,64,256]{2,1,0:T(8,128)S(1)} %get-tuple-element.92), channel_id=1, source_target_pairs={{0,16},{16,0},{1,17},{17,1},{2,18},{18,2},{3,19},{19,3},{4,20},{20... | collective-permute-start | bytes 3342344 | tf_op jit(solution)/shard_map/ppermute | solution.py:741
  66.7 6.8 %collective-permute-start.8 = (f32[2]{0:T(128)S(1)}, f32[2]{0:T(128)S(1)}, u32[]{:S(2)}, u32[]{:S(2)}) collective-permute-start(f32[2]{0:T(128)S(1)} %get-tuple-element.91), channel_id=1, source_target_pairs={{0,16},{16,0},{1,17},{17,1},{2,18},{18,2},{3,19},{19,3},{4,20},{20... | collective-permute-start | bytes 32 | tf_op jit(solution)/shard_map/ppermute | solution.py:741
where the time goes:
time: 76.3 us; the launch traced here: 76 us
  Pallas kernels  27.5 us (36%)
  blocking collectives  18.1 us (24%)
  starting transfers between devices  14 us (18%)
  waiting for transfers between devices  13.6 us (18%)
  between operations  2.11 us (3%)
    all_to_all x2, blocking collectives, from_all(): return lax.all_to_all(tiles, axes, split_axis=0, concat_axis=0, tiled=True)  18.1 us
    pallas_call x2, Pallas kernels, advance(): pl.pallas_call(functools.partial(advance_kernel, levels, total_rows, is_f...  13 us
    pallas_call x1, Pallas kernels, local_sums(): pl.pallas_call(functools.partial(sums_kernel, levels, total_rows), out_sh...  8.35 us
    ppermute x3, waiting for transfers between devices, swap(): return lax.ppermute(value, 'member', [(0, 1), (1, 0)])  8.29 us
    ppermute x2, waiting for transfers between devices, shift(): lax.ppermute(value, axis, [(i, (i + by) % count) for i in range(count)])  5.32 us
    ppermute x4, starting transfers between devices, pair(): return lax.ppermute(value, 'gridy', list(enumerate(partners[which])))  5.22 us
    ppermute x2, starting transfers between devices, shift(): lax.ppermute(value, axis, [(i, (i + by) % count) for i in range(count)])  5.1 us
    ppermute x3, starting transfers between devices, swap(): return lax.ppermute(value, 'member', [(0, 1), (1, 0)])  3.68 us
  transfers between devices with their start and end apart: 9, of which 4 were waited for; matrix products, arithmetic and copies ran while one was open for 1% of the time, Pallas kernels for 10%

commit v1 on v0

--- a/solution.py
+++ b/solution.py
@@ -463,18 +463,90 @@
     return first, krylov(second)
 
 
-RUN_NAMES = ["pu", "pv", "t2u", "t2v", "eta1", "w0", "w1", "w2", "eta2", "p", "p2", "gu1", "gv1", "gu2", "gv2"]
-
-
-def advance_kernel(levels, total_rows, is_first, *refs):
-    if is_first:
-        info, tiles, kept, out, zonal = refs[:5]
-        scratch = refs[5:]
-    else:
-        info, tiles, kept, zonal_before, out, spread = refs[:6]
-        scratch = refs[6:]
-    planes, after, turn, inside, staged, sums, sem = scratch[:7]
-    rows, cols = out.shape[1:]
+RUN_NAMES = ["pu", "pv", "t2u", "t2v", "eta1", "w0", "w1", "w2", "eta2", "p2", "gu1", "gv1", "gu2", "gv2"]
+
+
+def member_planes(kept, member, levels, rows, turn, inside):
+    work = Planes(levels, rows, turn, inside)
+    work.add(kept, ["ext%d" % i for i in range(4 * levels)] + ["eta", "ocean"] + KEPT, (member,))
+    return work
+
+
+def add_press(planes, l, levels, press, a, b):
+    dens = (PRESS_SCALE * BETA_S) * planes[levels + l, a:b, :] - (PRESS_SCALE * ALPHA_T) * planes[l, a:b, :]
+    press[a:b, :] = press[a:b, :] + dens
+
+
+def explicit_step(work, press, views, a, b, width):
+    def of(view):
+        here = view[a:b, :]
+        east, west = east_west(here)
+        return here[:, :width], east[:, :width], west[:, :width], view[a + 1 : b + 1, :width], view[a - 1 : b - 1, :width]
+
+    ocean = work.views["ocean"][a:b, :width]
+    coriolis = work.turn[a:b, :width]
+    u, east, west, north, south = of(views[2])
+    around_u = (east + west) + (north + south)
+    v, east, west, north, south = of(views[3])
+    around_v = (east + west) + (north + south)
+    _, east, west, north, south = of(press)
+    new_u = ocean * ((KEEP_FLOW * u + VISCOSITY * around_u) + (coriolis * v - (east - west)))
+    new_v = ocean * ((KEEP_FLOW * v + VISCOSITY * around_v) - (coriolis * u + (north - south)))
+    flow_u, flow_v = ADV * u, ADV * v
+    results = []
+    for view in views[:2]:
+        here, east, west, north, south = of(view)
+        carried = flow_u * (east - west) + flow_v * (north - south)
+        spread = KEEP_TRACER * here + KAPPA * ((east + west) + (north + south))
+        results.append(ocean * (spread - carried))
+    return results[0], results[1], new_u, new_v
+
+
+def step_kernel(levels, total_rows, kept, after, press, turn, inside):
+    members = kept.shape[0]
+    rows = kept.shape[2] - 2 * TOP
+    fill_rows(turn, inside, lax.axis_index("gridy") * rows, total_rows)
+
+    def level(i, carry):
+        m, l = i // levels, i % levels
+        work = member_planes(kept, m, levels, rows, turn, inside)
+
+        @pl.when(l == 0)
+        def _():
+            for a, b in chunks(TOP - CHUNK, TOP + rows + CHUNK):
+                press[a:b, :] = jnp.zeros((b - a, press.shape[1]), jnp.float32)
+
+        for a in range(TOP - CHUNK, TOP + rows + CHUNK, 8):
+            add_press(kept.at[m], l, levels, press, a, a + 8)
+        views = [kept.at[m, f * levels + l] for f in range(4)]
+        for a in range(TOP - 8, TOP + rows + 8, 8):
+            for f, value in enumerate(explicit_step(work, press, views, a, a + 8, press.shape[1])):
+                after[m, f * levels + l, a : a + 8, :] = value
+        return carry
+
+    lax.fori_loop(0, members * levels, level, 0)
+
+
+def first_step(kept, levels, total_rows):
+    shape = kept.shape[2:]
+    return pl.pallas_call(
+        functools.partial(step_kernel, levels, total_rows),
+        out_shape=jax.ShapeDtypeStruct((kept.shape[0], 4 * levels) + shape, jnp.float32),
+        in_specs=whole(1),
+        out_specs=whole(1)[0],
+        scratch_shapes=[pltpu.VMEM(shape, jnp.float32)] * 3,
+        compiler_params=pltpu.CompilerParams(vmem_limit_bytes=VMEM_LIMIT),
+        cost_estimate=pl.CostEstimate(flops=10**7, bytes_accessed=10**6, transcendentals=0),
+        name="first_step",
+    )(kept)
+
+
+def advance_kernel(levels, total_rows, is_first, parts, *refs):
+    info, tiles, kept, after, zonal_before = refs[:5]
+    outs, last = refs[5 : 5 + len(parts)], refs[5 + len(parts)]
+    planes, flows, turn, inside, staged, sums, sem, zonal = refs[6 + len(parts) :]
+    half = levels // 2
+    rows, cols = kept.shape[2] - 2 * TOP, kept.shape[3] - LANE
     members = kept.shape[0]
     tile_row = lax.axis_index("gridy")
     total = tiles[0]
@@ -484,15 +556,11 @@
     copy = pltpu.make_async_copy(staged, sums, sem)
     copy.start()
     fill_rows(turn, inside, tile_row * rows, total_rows)
-    if not is_first:
-        zonal = scratch[7]
-    zonal[...] = jnp.zeros_like(zonal) if is_first else zonal_before[...]
+    zonal[...] = zonal_before[...]
     copy.wait()
     member = info[members + 2] if is_first else 1 - info[members + 2]
-    ext = kept.at[member]
-    work = Planes(levels, rows, turn, inside)
+    work = member_planes(kept, member, levels, rows, turn, inside)
     work.add(planes, RUN_NAMES)
-    work.add(kept, ["ext%d" % i for i in range(4 * levels)] + ["eta", "ocean"] + KEPT, (member,))
 
     def read(i):
         return jnp.full((1, 1), sums[member, i], jnp.float32)
@@ -523,104 +591,82 @@
         slope_x, slope_y = work.slopes("eta2", a, b)
         work.put("gu2", a, b, GRAV * ocean * slope_x)
         work.put("gv2", a, b, GRAV * ocean * slope_y)
-        out[4 * levels, a - TOP : b - TOP, :] = work.get("eta2", a, b)[:, :cols]
+        if 0 in parts:
+            outs[0][4 * half, a - TOP : b - TOP, :] = work.get("eta2", a, b)[:, :cols]
     low, high = TOP - 8, TOP + rows + 8
-    for a, b in chunks(TOP - CHUNK, TOP + rows + CHUNK):
-        work.put("p", a, b, jnp.zeros((b - a, cols + LANE), jnp.float32))
-        work.put("p2", a, b, jnp.zeros((b - a, cols + LANE), jnp.float32))
-
-    def step(ref, l, press, a, b, width):
-        def of(view):
-            here = view[a:b, :]
-            east, west = east_west(here)
-            return here[:, :width], east[:, :width], west[:, :width], view[a + 1 : b + 1, :width], view[a - 1 : b - 1, :width]
-
-        ocean = work.views["ocean"][a:b, :width]
-        coriolis = turn[a:b, :width]
-        u, east, west, north, south = of(ref.at[2 * levels + l])
-        around_u = (east + west) + (north + south)
-        v, east, west, north, south = of(ref.at[3 * levels + l])
-        around_v = (east + west) + (north + south)
-        _, east, west, north, south = of(work.views[press])
-        new_u = ocean * ((KEEP_FLOW * u + VISCOSITY * around_u) + (coriolis * v - (east - west)))
-        new_v = ocean * ((KEEP_FLOW * v + VISCOSITY * around_v) - (coriolis * u + (north - south)))
-        flow_u, flow_v = ADV * u, ADV * v
-        results = []
-        for at in (l, levels + l):
-            here, east, west, north, south = of(ref.at[at])
-            carried = flow_u * (east - west) + flow_v * (north - south)
-            spread = KEEP_TRACER * here + KAPPA * ((east + west) + (north + south))
-            results.append(ocean * (spread - carried))
-        return results[0], results[1], new_u, new_v
-
-    def add_press(ref, l, press, a, b):
-        dens = (PRESS_SCALE * BETA_S) * ref[levels + l, a:b, :] - (PRESS_SCALE * ALPHA_T) * ref[l, a:b, :]
-        work.put(press, a, b, work.get(press, a, b) + dens)
-
-    def level(l, carry):
-        for a in range(TOP - CHUNK, TOP + rows + CHUNK, 8):
-            add_press(ext, l, "p", a, a + 8)
+    press = work.views["p2"]
+    for a, b in work.near():
+        press[a:b, :] = jnp.zeros((b - a, cols + LANE), jnp.float32)
+
+    def press_only(l, carry):
         for a in range(low, high, 8):
-            temp, salt, u, v = step(ext, l, "p", a, a + 8, cols + LANE)
-            after[l, a : a + 8, :] = temp
-            after[levels + l, a : a + 8, :] = salt
-            after[2 * levels + l, a : a + 8, :] = u - work.get("gu1", a, a + 8)
-            after[3 * levels + l, a : a + 8, :] = v - work.get("gv1", a, a + 8)
-        for a in range(low, high, 8):
-            add_press(after, l, "p2", a, a + 8)
-        for a in range(TOP, TOP + rows, 8):
-            temp, salt, u, v = step(after, l, "p2", a, a + 8, cols)
-            here = slice(a - TOP, a - TOP + 8)
-            v = v - work.get("gv2", a, a + 8)[:, :cols]
-            out[l, here, :] = temp
-            out[levels + l, here, :] = salt
-            out[2 * levels + l, here, :] = u - work.get("gu2", a, a + 8)[:, :cols]
-            out[3 * levels + l, here, :] = v
-            row_sum = jnp.sum(v, axis=1, keepdims=True)
-            zonal[here, :] = jnp.where(lanes_like((8, LANE)) == member * levels + l, row_sum, zonal[here, :])
+            add_press(after.at[member], l, levels, press, a, a + 8)
         return carry
 
-    lax.fori_loop(0, levels, level, 0)
-    if not is_first:
+    def level_of(out, start):
+        def level(l, carry):
+            press_only(l, carry)
+            for a in range(low, high, 8):
+                flows[0, a : a + 8, :] = after[member, 2 * levels + l, a : a + 8, :] - work.get("gu1", a, a + 8)
+                flows[1, a : a + 8, :] = after[member, 3 * levels + l, a : a + 8, :] - work.get("gv1", a, a + 8)
+            views = [after.at[member, l], after.at[member, levels + l], flows.at[0], flows.at[1]]
+            for a in range(TOP, TOP + rows, 8):
+                temp, salt, u, v = explicit_step(work, press, views, a, a + 8, cols)
+                here = slice(a - TOP, a - TOP + 8)
+                v = v - work.get("gv2", a, a + 8)[:, :cols]
+                out[l - start, here, :] = temp
+                out[half + l - start, here, :] = salt
+                out[2 * half + l - start, here, :] = u - work.get("gu2", a, a + 8)[:, :cols]
+                out[3 * half + l - start, here, :] = v
+                row_sum = jnp.sum(v, axis=1, keepdims=True)
+                zonal[here, :] = jnp.where(lanes_like((8, LANE)) == member * levels + l, row_sum, zonal[here, :])
+            return carry
+
+        return level
+
+    if parts[0]:
+        lax.fori_loop(0, half, press_only, 0)
+    for part, out in zip(parts, outs):
+        lax.fori_loop(part * half, part * half + half, level_of(out, part * half), 0)
+    if is_first:
+        last[...] = zonal[...]
+    else:
         square = jnp.concatenate([zonal[...]] + [jnp.zeros_like(zonal)] * (LANE // rows - 1), axis=0)
         turned = jnp.transpose(square)[: members * levels]
         line = turned[:levels]
         for m in range(1, members):
             line = line + pltpu.roll(turned, m * rows, 1)[m * levels : (m + 1) * levels]
-        for i in range(spread.shape[0]):
-            spread[i] = line
-
-
-def advance(is_first, info, tiles, kept, zonal, rows, cols, total_rows):
-    members, planes = kept.shape[:2]
-    levels = (planes - 2 - len(KEPT)) // 4
-    assert members * rows == LANE and members * levels == 8
-    shape = plane_shape(rows, cols)
-    zonal_shape = jax.ShapeDtypeStruct((rows, LANE), jnp.float32)
-    out_shape = [jax.ShapeDtypeStruct((4 * levels + 1, rows, cols), jnp.float32)]
-    if is_first:
-        out_shape += [zonal_shape]
-    else:
-        out_shape += [jax.ShapeDtypeStruct((tiles.shape[0], levels, members * rows), jnp.float32)]
+        for i in range(last.shape[0]):
+            last[i] = line
+
+
+def advance(is_first, parts, info, tiles, kept, after, zonal, total_rows):
+    members, _, *shape = kept.shape
+    levels = after.shape[1] // 4
+    rows, cols = shape[0] - 2 * TOP, shape[1] - LANE
+    shape = tuple(shape)
+    assert members * rows == LANE and members * levels == 8 and levels % 2 == 0
+    out_shape = [jax.ShapeDtypeStruct((2 * levels + (part == 0), rows, cols), jnp.float32) for part in parts]
+    last = (rows, LANE) if is_first else (tiles.shape[0], levels, members * rows)
     return pl.pallas_call(
-        functools.partial(advance_kernel, levels, total_rows, is_first),
-        out_shape=tuple(out_shape),
-        in_specs=in_smem(1) + whole(2 if is_first else 3),
-        out_specs=tuple(whole(2)),
+        functools.partial(advance_kernel, levels, total_rows, is_first, parts),
+        out_shape=tuple(out_shape) + (jax.ShapeDtypeStruct(last, jnp.float32),),
+        in_specs=in_smem(1) + whole(4),
+        out_specs=tuple(whole(len(parts) + 1)),
         scratch_shapes=[
             pltpu.VMEM((len(RUN_NAMES),) + shape, jnp.float32),
-            pltpu.VMEM((4 * levels,) + shape, jnp.float32),
+            pltpu.VMEM((2,) + shape, jnp.float32),
             pltpu.VMEM(shape, jnp.float32),
             pltpu.VMEM(shape, jnp.float32),
             pltpu.VMEM((8, LANE), jnp.float32),
             pltpu.SMEM((8, LANE), jnp.float32),
             pltpu.SemaphoreType.DMA,
-        ]
-        + ([] if is_first else [pltpu.VMEM((rows, LANE), jnp.float32)]),
+            pltpu.VMEM((rows, LANE), jnp.float32),
+        ],
         compiler_params=pltpu.CompilerParams(vmem_limit_bytes=VMEM_LIMIT),
         cost_estimate=pl.CostEstimate(flops=10**8, bytes_accessed=4 * 10**6, transcendentals=0),
         name="advance",
-    )(info, tiles, kept, *([] if is_first else [zonal]))
+    )(info, tiles, kept, after, zonal)
 
 
 def finish_kernel(count_y, count_x, total_cols, spread, overturn, score, held):
@@ -663,14 +709,17 @@
 
 
 def pick_kernel(levels, choice, source, score, their_score, *refs):
-    count = len(refs) - 7
-    sources, outs, weight, sem = refs[:count], refs[count : count + 5], refs[count + 5], refs[count + 6]
+    count = (len(refs) - 7) // 2
+    sources = [refs[2 * k : 2 * k + 2] for k in range(count)]
+    outs, weight, sem = refs[2 * count : 2 * count + 5], refs[2 * count + 5], refs[2 * count + 6]
     slots = outs[0].shape[0]
+    half = levels // 2
 
     def parts(s, source):
-        for f in range(4):
-            yield source.at[pl.ds(f * levels, levels)], outs[f].at[s]
-        yield source.at[4 * levels], outs[4].at[s]
+        for part in range(2):
+            for f in range(4):
+                yield source[part].at[pl.ds(f * half, half)], outs[f].at[s, pl.ds(part * half, half)]
+        yield source[0].at[4 * half], outs[4].at[s]
 
     for s in range(slots):
         for k in range(count):
@@ -694,18 +743,18 @@
 
 
 def pick(choice, source, score, their_score, sources, slots, levels):
-    _, rows, cols = sources[0].shape
+    _, rows, cols = sources[0][0].shape
     volume = jax.ShapeDtypeStruct((slots, levels, rows, cols), jnp.float32)
     surface = jax.ShapeDtypeStruct((slots, rows, cols), jnp.float32)
     return pl.pallas_call(
         functools.partial(pick_kernel, levels),
         out_shape=(volume,) * 4 + (surface, jax.ShapeDtypeStruct((slots,), jnp.float32)),
-        in_specs=in_smem(4) + whole(len(sources)),
+        in_specs=in_smem(4) + whole(2 * len(sources)),
         out_specs=tuple(in_hbm(5) + in_smem(1)),
-        scratch_shapes=[pltpu.SemaphoreType.DMA((slots, 5))],
+        scratch_shapes=[pltpu.SemaphoreType.DMA((slots, 9))],
         compiler_params=pltpu.CompilerParams(vmem_limit_bytes=VMEM_LIMIT),
         name="pick",
-    )(choice, source, score, their_score, *sources)
+    )(choice, source, score, their_score, *sum(sources, ()))
 
 
 def shift(value, axis, by):
@@ -748,31 +797,48 @@
     total_rows = rows * count_y
     grid = ("gridy", "gridx")
 
-    their_source = swap(clone_source)
     fields = (temp, salt, uvel, vvel, eta, land_mask)
-    rims = exchange_rims(pack_rims(*fields))
+    packed, their_source = lax.optimization_barrier((pack_rims(*fields), swap(clone_source)))
+    rims = exchange_rims(packed)
     tile, kept, info = local_sums(clone_source, their_source, fields, rims, total_rows)
     tiles = from_all(jnp.broadcast_to(tile[None], (count_y * count_x,) + tile.shape), grid)
-
-    sent, zonal = advance(True, info, tiles, kept, None, rows, cols, total_rows)
-    arrived = swap(sent)
-
-    def rest():
-        other, spread = advance(False, info, tiles, kept, zonal, rows, cols, total_rows)
-        return (other, *finish(from_all(spread, grid), members, rows, count_y, count_x, cols))
-
-    def nothing():
-        return jnp.zeros_like(sent), jnp.zeros((members, levels, rows), jnp.float32), jnp.zeros((members,), jnp.float32)
-
-    other, overturn, score = lax.cond(info[members + 1] != 0, rest, nothing)
+    after = first_step(kept, levels, total_rows)
+
+    def advanced(is_first, parts, zonal):
+        return advance(is_first, parts, info, tiles, kept, after, zonal, total_rows)
+
+    def lower_half():
+        low, zonal = advanced(True, (1,), zonal_high)
+        arrived_low = swap(low)
+
+        def rest():
+            *other, spread = advanced(False, (0, 1), zonal)
+            return (*other, *finish(from_all(spread, grid), members, rows, count_y, count_x, cols))
+
+        def nothing():
+            surface = jnp.zeros((members, levels, rows), jnp.float32)
+            return jnp.zeros_like(high), jnp.zeros_like(low), surface, jnp.zeros((members,), jnp.float32)
+
+        return (low, arrived_low, *lax.cond(always, rest, nothing))
+
+    def no_half():
+        low = jnp.zeros((2 * levels, rows, cols), jnp.float32)
+        surface = jnp.zeros((members, levels, rows), jnp.float32)
+        return low, low, jnp.zeros_like(high), low, surface, jnp.zeros((members,), jnp.float32)
+
+    always = info[members + 1] != 0
+    high, zonal_high = advanced(True, (0,), jnp.zeros((rows, LANE), jnp.float32))
+    arrived_high = swap(high)
+    low, arrived_low, other_high, other_low, overturn, score = lax.cond(always, lower_half, no_half)
     their_score = swap(score)
 
     def with_second():
-        sources = (sent, other, arrived, swap(other))
+        sources = ((high, low), (other_high, other_low), (arrived_high, arrived_low), (swap(other_high), swap(other_low)))
         return pick(info, clone_source, score, their_score, sources, members, levels)
 
     def without_second():
-        return pick(info, clone_source, score, their_score, (sent, other, arrived), members, levels)
+        sources = ((high, low), (other_high, other_low), (arrived_high, arrived_low))
+        return pick(info, clone_source, score, their_score, sources, members, levels)
 
     *picked, clone_weight = lax.cond(info[members] != 0, with_second, without_second)
     return (*picked, overturn, clone_weight)

time: 76.3 us -> 103 us (1.35)
  Pallas kernels: 27.5 us -> 51.6 us
  local copies, waits for them, and re-layouts: 0.63 us -> 7.12 us
  blocking collectives: 18.1 us -> 12.3 us
  starting transfers between devices: 14 us -> 19.5 us
  waiting for transfers between devices: 13.6 us -> 9.36 us
    pallas_call x2 -> x3, Pallas kernels: 13 us -> 25.8 us  [advance(): pl.pallas_call(functools.partial(advance_kernel, levels, total_rows, is_f...]
    pallas_call x0 -> x1, Pallas kernels: none -> 9.66 us  [first_step(): pl.pallas_call(functools.partial(step_kernel, levels, total_rows), out_sh...]
    unnamed x14, local copies, waits for them, and re-layouts: 0.03 us -> 5.92 us
    all_to_all x2 -> x1, blocking collectives: 18.1 us -> 12.3 us  [from_all(): return lax.all_to_all(tiles, axes, split_axis=0, concat_axis=0, tiled=True)]
    ppermute x3 -> x4, waiting for transfers between devices: 8.29 us -> 3.12 us  [swap(): return lax.ppermute(value, 'member', [(0, 1), (1, 0)])]
    all_to_all x0 -> x1, starting transfers between devices: none -> 4.88 us  [from_all(): return lax.all_to_all(tiles, axes, split_axis=0, concat_axis=0, tiled=True)]
    ppermute x3 -> x4, starting transfers between devices: 3.68 us -> 5.74 us  [swap(): return lax.ppermute(value, 'member', [(0, 1), (1, 0)])]
    ppermute x2, starting transfers between devices: 5.1 us -> 3.66 us  [shift(): lax.ppermute(value, axis, [(i, (i + by) % count) for i in range(count)])]
  transfers between devices with their start and end apart: 9 -> 11, of which waited for: 4 -> 4; matrix products, arithmetic and copies ran while one was open for 1% -> 1% of each run, Pallas kernels for 10% -> 31%
where the time goes in v1:
time: 103 us; the launch traced here: 102 us
  Pallas kernels  51.6 us (50%)
  starting transfers between devices  19.5 us (19%)
  blocking collectives  12.3 us (12%)
  waiting for transfers between devices  9.36 us (9%)
  local copies, waits for them, and re-layouts  7.12 us (7%)
  between operations  2.02 us (2%)
    pallas_call x3, Pallas kernels, advance(): pl.pallas_call(functools.partial(advance_kernel, levels, total_rows, is_f...  25.8 us
    all_to_all x1, blocking collectives, from_all(): return lax.all_to_all(tiles, axes, split_axis=0, concat_axis=0, tiled=True)  12.3 us
    pallas_call x1, Pallas kernels, first_step(): pl.pallas_call(functools.partial(step_kernel, levels, total_rows), out_sh...  9.66 us
    pallas_call x1, Pallas kernels, local_sums(): pl.pallas_call(functools.partial(sums_kernel, levels, total_rows), out_sh...  9.11 us
    unnamed x14, local copies, waits for them, and re-layouts  5.92 us
    ppermute x4, starting transfers between devices, swap(): return lax.ppermute(value, 'member', [(0, 1), (1, 0)])  5.74 us
    ppermute x2, waiting for transfers between devices, shift(): lax.ppermute(value, axis, [(i, (i + by) % count) for i in range(count)])  5.32 us
    ppermute x4, starting transfers between devices, pair(): return lax.ppermute(value, 'gridy', list(enumerate(partners[which])))  5.22 us
  transfers between devices with their start and end apart: 11, of which 4 were waited for; matrix products, arithmetic and copies ran while one was open for 1% of the time, Pallas kernels for 31%

profile of v1, /device:TPU:0, one launch (start us, length us, event | category | flops | bytes accessed | tf_op | source)
XLA Modules:
  0.0 101.9 jit_solution(16457594114081157996)
XLA Ops:
  0.6 3.0 %collective-permute-start.3 = (s32[2]{0:T(128)}, s32[2]{0:T(128)S(1)}, u32[]{:S(2)}, u32[]{:S(2)}) collective-permute-start(s32[2]{0:T(128)} %source.1), channel_id=1, source_target_pairs={{0,16},{16,0},{1,17},{17,1},{2,18},{18,2},{3,19},{19,3},{4,20},{20... | collective-permute-start | bytes 32 | tf_op jit(solution)/shard_map/ppermute | solution.py:790
  3.7 2.7 %pack_rims.1 = (f32[2,64,256]{2,1,0:T(8,128)}, f32[2,64,256]{2,1,0:T(8,128)}, f32[2,184,256]{2,1,0:T(8,128)}, f32[2,184,256]{2,1,0:T(8,128)}) custom-call(f32[2,4,64,256]{3,2,1,0:T(8,128)} %refs_0_.3, f32[2,4,64,256]{3,2,1,0:T(8,128)} %refs_1_.3, f32[2,4,64,256]{3,2,1,0:T(8,128)} %refs_2_.3, f32[2,4,64,256]{3,2,1,0:T(8,128)} %refs_3_.3, ...), custom_call_target="tpu_custom_call" | custom-call | tf_op jit(solution)/shard_map/pack_rims/pallas_call | solution.py:121
  6.4 3.7 %collective-permute-start.4 = (f32[2,64,256]{2,1,0:T(8,128)}, f32[2,64,256]{2,1,0:T(8,128)S(1)}, u32[]{:S(2)}, u32[]{:S(2)}) collective-permute-start(f32[2,64,256]{2,1,0:T(8,128)} %get-tuple-element.142), channel_id=1, source_target_pairs={{0,3},{1,0},{2,1},{3,2},{4,7},{5,4},{6,5},{7,6},{8,11},{9,8},{10,9... | collective-permute-start | bytes 393224 | tf_op jit(solution)/shard_map/ppermute | solution.py:762
  10.1 1.6 %collective-permute-start.7 = (f32[2,184,256]{2,1,0:T(8,128)}, f32[2,184,256]{2,1,0:T(8,128)S(1)}, u32[]{:S(2)}, u32[]{:S(2)}) collective-permute-start(f32[2,184,256]{2,1,0:T(8,128)} %get-tuple-element.145), channel_id=1, source_target_pairs={{0,0},{4,8},{8,4},{12,12},{1,1},{5,9},{9,5},{13,13},{2,2},{6,10},{... | collective-permute-start | bytes 1130504 | tf_op jit(solution)/shard_map/ppermute | solution.py:773
  11.7 2.6 %collective-permute-done.4.refs_6_ = f32[2,64,256]{2,1,0:T(8,128)S(1)} collective-permute-done((f32[2,64,256]{2,1,0:T(8,128)}, f32[2,64,256]{2,1,0:T(8,128)S(1)}, u32[]{:S(2)}, u32[]{:S(2)}) %collective-permute-start.4) | collective-permute-done | bytes 131104 | tf_op jit(solution)/shard_map/ppermute | solution.py:762
  14.3 2.7 %collective-permute-done.5.refs_7_ = f32[2,64,256]{2,1,0:T(8,128)S(1)} collective-permute-done((f32[2,64,256]{2,1,0:T(8,128)}, f32[2,64,256]{2,1,0:T(8,128)S(1)}, u32[]{:S(2)}, u32[]{:S(2)}) %collective-permute-start.5) | collective-permute-done | bytes 131104 | tf_op jit(solution)/shard_map/ppermute | solution.py:762
  17.7 2.9 %collective-permute-start.8 = (f32[2,16,512]{2,1,0:T(8,128)S(1)}, f32[2,16,512]{2,1,0:T(8,128)S(1)}, u32[]{:S(2)}, u32[]{:S(2)}) collective-permute-start(f32[2,16,512]{2,1,0:T(8,128)S(1)} %get-tuple-element.164), channel_id=1, source_target_pairs={{0,4},{4,0},{8,12},{12,8},{1,5},{5,1},{9,13},{13,9},{2,6},{6,2},{1... | collective-permute-start | bytes 196616 | tf_op jit(solution)/shard_map/ppermute | solution.py:773
  21.5 1.0 %copy-done = f32[2,4,64,256]{3,2,1,0:T(8,128)S(1)} copy-done((f32[2,4,64,256]{3,2,1,0:T(8,128)S(1)}, f32[2,4,64,256]{3,2,1,0:T(8,128)}, u32[]{:S(2)}) %copy-start) | copy-done | bytes 524312
  22.6 1.0 %copy-done.1 = f32[2,4,64,256]{3,2,1,0:T(8,128)S(1)} copy-done((f32[2,4,64,256]{3,2,1,0:T(8,128)S(1)}, f32[2,4,64,256]{3,2,1,0:T(8,128)}, u32[]{:S(2)}) %copy-start.1) | copy-done | bytes 524312
  23.6 1.0 %copy-done.2 = f32[2,4,64,256]{3,2,1,0:T(8,128)S(1)} copy-done((f32[2,4,64,256]{3,2,1,0:T(8,128)S(1)}, f32[2,4,64,256]{3,2,1,0:T(8,128)}, u32[]{:S(2)}) %copy-start.2) | copy-done | bytes 524312
  24.7 1.0 %copy-done.3 = f32[2,4,64,256]{3,2,1,0:T(8,128)S(1)} copy-done((f32[2,4,64,256]{3,2,1,0:T(8,128)S(1)}, f32[2,4,64,256]{3,2,1,0:T(8,128)}, u32[]{:S(2)}) %copy-start.3) | copy-done | bytes 524312
  27.5 9.1 %local_sums.1 = (f32[2,128]{1,0:T(2,128)S(1)}, f32[2,24,112,384]{3,2,1,0:T(8,128)}, s32[5]{0:T(128)S(1)}) custom-call(s32[2]{0:T(128)} %source.1, s32[2]{0:T(128)S(1)} %collective-permute-done.3.theirs, f32[2,4,64,256]{3,2,1,0:T(8,128)S(1)} %copy-done, f32[2,4,64,256]{3,2,1,0:T(8,128)S(1)} %copy-done.1, f32[2,4,64,256]{3,2,1,0:T(8,128)S(1)} %copy-done.2, ...), custom_call_target="tpu_custom_call" | custom-call | flops 100000000 | bytes 4000000 | tf_op jit(solution)/shard_map/local_sums/pallas_call | solution.py:399
  37.2 4.9 %all-to-all-start.1 = ((f32[16,2,128]{2,1,0:T(2,128)}), f32[16,2,128]{2,1,0:T(2,128)S(1)}, u32[]{:S(2)}, u32[]{:S(2)}) async-start(f32[16,2,128]{2,1,0:T(2,128)} %broadcast_in_dim.4), calls=%async_computation.1 | async-start | bytes 32768 | tf_op jit(solution)/shard_map/all_to_all | solution.py:786
  42.1 9.7 %first_step.1.refs_3_ = f32[2,16,112,384]{3,2,1,0:T(8,128)} custom-call(f32[2,24,112,384]{3,2,1,0:T(8,128)} %get-tuple-element.148.kept.refs_2_), custom_call_target="tpu_custom_call" | custom-call | flops 10000000 | bytes 1000000 | tf_op jit(solution)/shard_map/first_step/pallas_call | solution.py:532
  51.7 7.6 %advance.5 = (f32[9,64,256]{2,1,0:T(8,128)S(1)}, f32[64,128]{1,0:T(8,128)S(1)}) custom-call(s32[5]{0:T(128)S(1)} %get-tuple-element.146.refs_0_, f32[16,2,128]{2,1,0:T(2,128)S(1)} %all-to-all-done.1.refs_1_, f32[2,24,112,384]{3,2,1,0:T(8,128)} %get-tuple-element.148.kept.refs_2_, f32[2,16,112,384]{3,2,1,0:T(8,128)} %first_step.1.refs_3_, ...), custom_call_target="tpu_custom_call" | custom-call | flops 100000000 | bytes 4000000 | tf_op jit(solution)/shard_map/advance/pallas_call | solution.py:651
  61.8 32.9 %conditional.3 = (f32[8,64,256]{2,1,0:T(8,128)}, f32[8,64,256]{2,1,0:T(8,128)}, f32[9,64,256]{2,1,0:T(8,128)}, f32[8,64,256]{2,1,0:T(8,128)}, f32[2,4,64]{2,1,0:T(4,128)}, /*index=5*/f32[2]{0:T(128)}) conditional(s32[]{:T(128)} %convert_element_type.14, () %tuple.32, (s32[5]{0:T(128)S(1)}, f32[16,2,128]{2,1,0:T(2,128)S(1)}, ...), branch_computations={%region_0.1_spmd, %region_1.4_spmd} | conditional | flops 200000000 | bytes 10162853 | solution.py:832
  61.8 8.5 %advance.4 = (f32[8,64,256]{2,1,0:T(8,128)}, f32[64,128]{1,0:T(8,128)S(1)}) custom-call(s32[5]{0:T(128)S(1)} %get-tuple-element.72.refs_0_, f32[16,2,128]{2,1,0:T(2,128)S(1)} %get-tuple-element.73.refs_1_, f32[2,24,112,384]{3,2,1,0:T(8,128)} %get-tuple-element.74.refs_2_, f32[2,16,112,384]{3,2,1,0:T(8,128)} %get-tuple-element.75.refs_3_, ...), custom_call_target="tpu_custom_call" | custom-call | flops 100000000 | bytes 4000000 | tf_op jit(solution)/shard_map/cond/branch_1_fun/advance/pallas_call | solution.py:651
  70.3 1.6 %collective-permute-start = (f32[8,64,256]{2,1,0:T(8,128)}, f32[8,64,256]{2,1,0:T(8,128)}, u32[]{:S(2)}, u32[]{:S(2)}) collective-permute-start(f32[8,64,256]{2,1,0:T(8,128)} %get-tuple-element.185), channel_id=1, source_target_pairs={{0,16},{16,0},{1,17},{17,1},{2,18},{18,2},{3,19},{19,3},{4,20},{20... | collective-permute-start | bytes 1572872 | tf_op jit(solution)/shard_map/cond/branch_1_fun/ppermute | solution.py:790
  71.9 22.8 %conditional = (f32[9,64,256]{2,1,0:T(8,128)}, f32[8,64,256]{2,1,0:T(8,128)}, f32[2,4,64]{2,1,0:T(4,128)}, f32[2]{0:T(128)}) conditional(s32[]{:T(128)} %convert_element_type.8, () %tuple.21, (s32[5]{0:T(128)S(1)}, f32[16,2,128]{2,1,0:T(2,128)S(1)}, f32[2,24,112,384]{3,2,1,0:T(8,128)}, f32[2,16,112,384]{3,2,1,0:T(8,128)}, ...), branch_computations={%region_2.2_spmd, %region_3.3_spmd} | conditional | flops 100000000 | bytes 4065568 | solution.py:822
  71.9 9.7 %advance.3 = (f32[9,64,256]{2,1,0:T(8,128)}, f32[8,64,256]{2,1,0:T(8,128)}, f32[16,4,128]{2,1,0:T(4,128)S(1)}) custom-call(s32[5]{0:T(128)S(1)} %get-tuple-element.62.refs_0_, f32[16,2,128]{2,1,0:T(2,128)S(1)} %get-tuple-element.63.refs_1_, f32[2,24,112,384]{3,2,1,0:T(8,128)} %get-tuple-element.64.refs_2_, f32[2,16,112,384]{3,2,1,0:T(8,128)} %get-tuple-element.65.refs_3_, ...), custom_call_target="tpu_custom_call" | custom-call | flops 100000000 | bytes 4000000 | tf_op jit(solution)/shard_map/cond/branch_1_fun/cond/branch_1_fun/advance/pallas_call | solution.py:651
  81.7 12.3 %all_to_all.9.spread = f32[16,4,128]{2,1,0:T(4,128)S(1)} all-to-all(f32[16,4,128]{2,1,0:T(4,128)S(1)} %get-tuple-element.69), channel_id=1, replica_groups=mesh['member'=2,'gridy'=4,'gridx'=4] {'gridy','gridx'}, dimensions={0} | all-to-all | bytes 65536 | tf_op jit(solution)/shard_map/cond/branch_1_fun/cond/branch_1_fun/all_to_all | solution.py:786
  95.2 3.1 %collective-permute-done.10 = f32[2]{0:T(128)S(1)} collective-permute-done((f32[2]{0:T(128)}, f32[2]{0:T(128)S(1)}, u32[]{:S(2)}, u32[]{:S(2)}) %collective-permute-start.10) | collective-permute-done | bytes 40 | tf_op jit(solution)/shard_map/ppermute | solution.py:790
  98.4 3.6 %conditional.4 = ((f32[2,4,64,256]{3,2,1,0:T(8,128)}, f32[2,4,64,256]{3,2,1,0:T(8,128)}, f32[2,4,64,256]{3,2,1,0:T(8,128)}, f32[2,4,64,256]{3,2,1,0:T(8,128)}, f32[2,64,256]{2,1,0:T(8,128)}, /*index=5*/f32[2]{0:T(128)})) conditional(s32[]{:T(128)} %bitcast, (s32[5]{0:T(128)S(1)}, s32[2]{0:T(128)S(1)}, f32[2]{0:T(128)}, f32[2]{0:T(128)S(1)}, ...), branch_computations={%region_4.5_spmd, %region_5.6_spmd} | conditional | bytes 4456536 | solution.py:843
  98.4 3.6 %pick.2 = (f32[2,4,64,256]{3,2,1,0:T(8,128)}, f32[2,4,64,256]{3,2,1,0:T(8,128)}, f32[2,4,64,256]{3,2,1,0:T(8,128)}, f32[2,4,64,256]{3,2,1,0:T(8,128)}, f32[2,64,256]{2,1,0:T(8,128)}, /*index=5*/f32[2]{0:T(128)}) custom-call(s32[5]{0:T(128)S(1)} %get-tuple-element.84.choice, s32[2]{0:T(128)S(1)} %get-tuple-element.85.source, f32[2]{0:T(128)} %get-tuple-element.86.score, ...), custom_call_target="tpu_custom_call" | custom-call | tf_op jit(solution)/shard_map/cond/branch_0_fun/pick/pallas_call | solution.py:749
  (30 shorter events, 6.4 us)
Async XLA Ops:
  0.6 5.8 %collective-permute-start.3 = (s32[2]{0:T(128)}, s32[2]{0:T(128)S(1)}, u32[]{:S(2)}, u32[]{:S(2)}) collective-permute-start(s32[2]{0:T(128)} %source.1), channel_id=1, source_target_pairs={{0,16},{16,0},{1,17},{17,1},{2,18},{18,2},{3,19},{19,3},{4,20},{20... | collective-permute-start | bytes 32 | tf_op jit(solution)/shard_map/ppermute | solution.py:790
  6.4 7.9 %collective-permute-start.4 = (f32[2,64,256]{2,1,0:T(8,128)}, f32[2,64,256]{2,1,0:T(8,128)S(1)}, u32[]{:S(2)}, u32[]{:S(2)}) collective-permute-start(f32[2,64,256]{2,1,0:T(8,128)} %get-tuple-element.142), channel_id=1, source_target_pairs={{0,3},{1,0},{2,1},{3,2},{4,7},{5,4},{6,5},{7,6},{8,11},{9,8},{10,9... | collective-permute-start | bytes 393224 | tf_op jit(solution)/shard_map/ppermute | solution.py:762
  10.1 7.0 %collective-permute-start.5 = (f32[2,64,256]{2,1,0:T(8,128)}, f32[2,64,256]{2,1,0:T(8,128)S(1)}, u32[]{:S(2)}, u32[]{:S(2)}) collective-permute-start(f32[2,64,256]{2,1,0:T(8,128)} %get-tuple-element.143), channel_id=1, source_target_pairs={{0,1},{1,2},{2,3},{3,0},{4,5},{5,6},{6,7},{7,4},{8,9},{9,10},{10,1... | collective-permute-start | bytes 393224 | tf_op jit(solution)/shard_map/ppermute | solution.py:762
  10.1 11.5 %collective-permute-start.6 = (f32[2,184,256]{2,1,0:T(8,128)}, f32[2,184,256]{2,1,0:T(8,128)S(1)}, u32[]{:S(2)}, u32[]{:S(2)}) collective-permute-start(f32[2,184,256]{2,1,0:T(8,128)} %get-tuple-element.144), channel_id=1, source_target_pairs={{0,4},{4,0},{8,12},{12,8},{1,5},{5,1},{9,13},{13,9},{2,6},{6,2},{1... | collective-permute-start | bytes 1130504 | tf_op jit(solution)/shard_map/ppermute | solution.py:773
  10.1 11.5 %collective-permute-start.7 = (f32[2,184,256]{2,1,0:T(8,128)}, f32[2,184,256]{2,1,0:T(8,128)S(1)}, u32[]{:S(2)}, u32[]{:S(2)}) collective-permute-start(f32[2,184,256]{2,1,0:T(8,128)} %get-tuple-element.145), channel_id=1, source_target_pairs={{0,0},{4,8},{8,4},{12,12},{1,1},{5,9},{9,5},{13,13},{2,2},{6,10},{... | collective-permute-start | bytes 1130504 | tf_op jit(solution)/shard_map/ppermute | solution.py:773
  17.0 3.6 %collective-permute-start.9 = (f32[2,16,512]{2,1,0:T(8,128)S(1)}, f32[2,16,512]{2,1,0:T(8,128)S(1)}, u32[]{:S(2)}, u32[]{:S(2)}) collective-permute-start(f32[2,16,512]{2,1,0:T(8,128)S(1)} %get-tuple-element.163), channel_id=1, source_target_pairs={{0,0},{4,8},{8,4},{12,12},{1,1},{5,9},{9,5},{13,13},{2,2},{6,10},{... | collective-permute-start | bytes 196616 | tf_op jit(solution)/shard_map/ppermute | solution.py:773
  17.7 3.8 %collective-permute-start.8 = (f32[2,16,512]{2,1,0:T(8,128)S(1)}, f32[2,16,512]{2,1,0:T(8,128)S(1)}, u32[]{:S(2)}, u32[]{:S(2)}) collective-permute-start(f32[2,16,512]{2,1,0:T(8,128)S(1)} %get-tuple-element.164), channel_id=1, source_target_pairs={{0,4},{4,0},{8,12},{12,8},{1,5},{5,1},{9,13},{13,9},{2,6},{6,2},{1... | collective-permute-start | bytes 196616 | tf_op jit(solution)/shard_map/ppermute | solution.py:773
  21.5 1.0 %copy-start = (f32[2,4,64,256]{3,2,1,0:T(8,128)S(1)}, f32[2,4,64,256]{3,2,1,0:T(8,128)}, u32[]{:S(2)}) copy-start(f32[2,4,64,256]{3,2,1,0:T(8,128)} %refs_0_.3) | copy-start | bytes 1572868
  22.6 1.0 %copy-start.1 = (f32[2,4,64,256]{3,2,1,0:T(8,128)S(1)}, f32[2,4,64,256]{3,2,1,0:T(8,128)}, u32[]{:S(2)}) copy-start(f32[2,4,64,256]{3,2,1,0:T(8,128)} %refs_1_.3) | copy-start | bytes 1572868
  23.6 1.0 %copy-start.2 = (f32[2,4,64,256]{3,2,1,0:T(8,128)S(1)}, f32[2,4,64,256]{3,2,1,0:T(8,128)}, u32[]{:S(2)}) copy-start(f32[2,4,64,256]{3,2,1,0:T(8,128)} %refs_2_.3) | copy-start | bytes 1572868
  24.7 1.0 %copy-start.3 = (f32[2,4,64,256]{3,2,1,0:T(8,128)S(1)}, f32[2,4,64,256]{3,2,1,0:T(8,128)}, u32[]{:S(2)}) copy-start(f32[2,4,64,256]{3,2,1,0:T(8,128)} %refs_3_.3) | copy-start | bytes 1572868
  25.7 0.9 copy-start.4
  26.6 0.8 copy-start.5
  37.2 14.6 %all-to-all-start.1 = ((f32[16,2,128]{2,1,0:T(2,128)}), f32[16,2,128]{2,1,0:T(2,128)S(1)}, u32[]{:S(2)}, u32[]{:S(2)}) async-start(f32[16,2,128]{2,1,0:T(2,128)} %broadcast_in_dim.4), calls=%async_computation.1 | async-start | bytes 32768 | tf_op jit(solution)/shard_map/all_to_all | solution.py:786
  59.4 39.0 %collective-permute-start.11 = (f32[9,64,256]{2,1,0:T(8,128)S(1)}, f32[9,64,256]{2,1,0:T(8,128)S(1)}, u32[]{:S(2)}, u32[]{:S(2)}) collective-permute-start(f32[9,64,256]{2,1,0:T(8,128)S(1)} %get-tuple-element.151), channel_id=1, source_target_pairs={{0,16},{16,0},{1,17},{17,1},{2,18},{18,2},{3,19},{19,3},{4,20},{20... | collective-permute-start | bytes 1769480 | tf_op jit(solution)/shard_map/ppermute | solution.py:790
  61.8 36.5 %copy-start.6 = (s32[2]{0:T(128)S(1)}, s32[2]{0:T(128)}, u32[]{:S(2)}) copy-start(s32[2]{0:T(128)} %source.1) | copy-start | bytes 28
  70.3 24.4 %collective-permute-start = (f32[8,64,256]{2,1,0:T(8,128)}, f32[8,64,256]{2,1,0:T(8,128)}, u32[]{:S(2)}, u32[]{:S(2)}) collective-permute-start(f32[8,64,256]{2,1,0:T(8,128)} %get-tuple-element.185), channel_id=1, source_target_pairs={{0,16},{16,0},{1,17},{17,1},{2,18},{18,2},{3,19},{19,3},{4,20},{20... | collective-permute-start | bytes 1572872 | tf_op jit(solution)/shard_map/cond/branch_1_fun/ppermute | solution.py:790
  94.7 3.7 %collective-permute-start.10 = (f32[2]{0:T(128)}, f32[2]{0:T(128)S(1)}, u32[]{:S(2)}, u32[]{:S(2)}) collective-permute-start(f32[2]{0:T(128)} %get-tuple-element.150), channel_id=1, source_target_pairs={{0,16},{16,0},{1,17},{17,1},{2,18},{18,2},{3,19},{19,3},{4,20},{20... | collective-permute-start | bytes 32 | tf_op jit(solution)/shard_map/ppermute | solution.py:790

commit v2 on v0

--- a/solution.py
+++ b/solution.py
@@ -25,27 +25,41 @@
 ADV = STEP_DT * 0.5
 DIV = DIV_K * 0.5
 GRAV = GRAV_K * 0.5
-
-WIDE = 10
+KEEP_FLOW = 1.0 - STEP_DT * DRAG_K - 4.0 * VISCOSITY
+KEEP_TRACER = 1.0 - 4.0 * KAPPA
+PRESS_SCALE = PRESS_K * 0.5 * STEP_DT
+
 TOP = 24
 CHUNK = 16
 LANE = 128
-PER_GROUP = 11
 PAIRS = [(a, b) for a in range(4) for b in range(a, 4)]
 SUMS = 6 + 6 * len(PAIRS)
 VMEM_LIMIT = 24 * 1024 * 1024
 WHOLE_VMEM = 60 * 1024 * 1024
 
 
-def rim_place(plane):
-    group, place = divmod(plane, PER_GROUP)
-    if place < 6:
-        return group, 0, (2 * place + 1) * WIDE
-    return group, 1, (2 * (place - 6) + 2) * WIDE
-
-
-def groups_of(planes):
-    return -(-planes // PER_GROUP)
+def rim_layout(levels):
+    widths = [("d%d" % l, 6) for l in range(levels)]
+    widths += [("ext%d" % (2 * levels + i), 5) for i in range(2 * levels)]
+    widths += [("ext%d" % i, 2) for i in range(2 * levels)]
+    widths += [("su", 10), ("sv", 10), ("sp", 10), ("eta", 8), ("ocean", 10)]
+    layout, start = [], 0
+    for name, width in widths:
+        layout.append((name, width, start))
+        start += width
+    assert start <= LANE
+    return layout
+
+
+def level_sums(ext, levels):
+    dens = []
+    for l in range(levels):
+        factor = PRESS_SCALE * (levels - l)
+        dens.append((factor * BETA_S) * ext(levels + l) - (factor * ALPHA_T) * ext(l))
+    su, sv, sp = ext(2 * levels), ext(3 * levels), dens[0]
+    for l in range(1, levels):
+        su, sv, sp = su + ext(2 * levels + l), sv + ext(3 * levels + l), sp + dens[l]
+    return dens, su, sv, sp
 
 
 def lanes_like(shape):
@@ -53,50 +67,44 @@
 
 
 def fetches(fields, planes_of, mask_to, sems, levels):
-    members = fields[0].shape[0]
-    per_member = []
-    for m in range(members):
+    def copies(m):
         parts = [(fields[f].at[m], planes_of(m, pl.ds(f * levels, levels))) for f in range(4)]
         parts.append((fields[4].at[m], planes_of(m, 4 * levels)))
-        per_member.append([pltpu.make_async_copy(*part, sems.at[m, i]) for i, part in enumerate(parts)])
+        return [pltpu.make_async_copy(*part, sems.at[m, i]) for i, part in enumerate(parts)]
+
     mask_copy = pltpu.make_async_copy(fields[5], mask_to, sems.at[0, 5])
     mask_copy.start()
-    for copies in per_member:
-        for copy in copies:
+    for m in range(fields[0].shape[0]):
+        for copy in copies(m):
             copy.start()
     mask_copy.wait()
-    return per_member
+    return copies
 
 
 def pack_kernel(levels, *refs):
     fields, (to_west, to_east, rows_first, rows_second), (held, mask, sems) = refs[:6], refs[6:10], refs[10:]
     members, _, rows, cols = held.shape
-    planes = 4 * levels + 2
     copies = fetches(fields, lambda m, at: held.at[m, at], mask, sems, levels)
     lane = lanes_like((rows, LANE))
-    even = lax.broadcasted_iota(jnp.int32, (WIDE, cols), 0) * 0 + lax.rem(lax.axis_index("gridy"), 2) == 0
+    even = lax.broadcasted_iota(jnp.int32, (CHUNK, cols), 0) * 0 + lax.rem(lax.axis_index("gridy"), 2) == 0
     for m in range(members):
-        for copy in copies[m]:
+        for copy in copies(m):
             copy.wait()
-        west_parts = [None] * groups_of(planes)
-        east_parts = [None] * groups_of(planes)
-        for plane in range(planes):
-            value = held[m, plane] if plane < planes - 1 else mask[...].astype(jnp.float32)
-            group, _, start = rim_place(plane)
-            both = jnp.where(lane < WIDE, value[:, :LANE], value[:, cols - LANE :])
-            both = pltpu.roll(both, start, 1)
-            is_west = (lane >= start) & (lane < start + WIDE)
-            is_east = (lane >= start - WIDE) & (lane < start)
-            zero = jnp.zeros_like(both)
-            west_parts[group] = jnp.where(is_west, both, zero if west_parts[group] is None else west_parts[group])
-            east_parts[group] = jnp.where(is_east, both, zero if east_parts[group] is None else east_parts[group])
-            low, high = value[:WIDE], value[rows - WIDE :]
-            rows_first[m, plane * WIDE : (plane + 1) * WIDE, :] = jnp.where(even, high, low)
-            rows_second[m, plane * WIDE : (plane + 1) * WIDE, :] = jnp.where(even, low, high)
-        for group in range(groups_of(planes)):
-            where = slice(group * LANE, (group + 1) * LANE)
-            to_west[m, :, where] = west_parts[group]
-            to_east[m, :, where] = east_parts[group]
+        dens, *sums = level_sums(lambda i: held[m, i], levels)
+        planes = dict(zip(["su", "sv", "sp"], sums), eta=held[m, 4 * levels], ocean=mask[...].astype(jnp.float32))
+        planes.update({"d%d" % l: dens[l] for l in range(levels)})
+        west = east = jnp.zeros((rows, LANE), jnp.float32)
+        for name, width, start in rim_layout(levels):
+            value = held[m, int(name[3:])] if name.startswith("ext") else planes[name]
+            here = (lane >= start) & (lane < start + width)
+            both = jnp.where(lane < LANE // 2, value[:, :LANE], value[:, cols - LANE :])
+            west = jnp.where(here, pltpu.roll(both, start, 1) if start else both, west)
+            east = jnp.where(here, pltpu.roll(both, (start + width) % LANE, 1) if start + width < LANE else both, east)
+            low, high = value[:width], value[rows - width :]
+            rows_first[m, start : start + width, :] = jnp.where(even[:width], high, low)
+            rows_second[m, start : start + width, :] = jnp.where(even[:width], low, high)
+        to_west[m] = west
+        to_east[m] = east
 
 
 def whole(count):
@@ -113,18 +121,15 @@
 
 def pack_rims(temp, salt, uvel, vvel, eta, mask):
     members, levels, rows, cols = temp.shape
-    planes = 4 * levels + 2
-    wide = groups_of(planes) * LANE
-    row_pack = -(-planes * WIDE // 8) * 8
-    side = jax.ShapeDtypeStruct((members, rows, wide), jnp.float32)
-    line = jax.ShapeDtypeStruct((members, row_pack, cols), jnp.float32)
+    side = jax.ShapeDtypeStruct((members, rows, LANE), jnp.float32)
+    line = jax.ShapeDtypeStruct((members, LANE, cols), jnp.float32)
     return pl.pallas_call(
         functools.partial(pack_kernel, levels),
         out_shape=(side, side, line, line),
         in_specs=in_hbm(6),
         out_specs=tuple(whole(4)),
         scratch_shapes=[
-            pltpu.VMEM((members, planes - 1, rows, cols), jnp.float32),
+            pltpu.VMEM((members, 4 * levels + 1, rows, cols), jnp.float32),
             pltpu.VMEM((rows, cols), jnp.int32),
             pltpu.SemaphoreType.DMA((members, 6)),
         ],
@@ -142,9 +147,8 @@
     return [(a, min(a + CHUNK, last)) for a in range(first, last, CHUNK)]
 
 
-def assemble(ext, mask, rims, m, levels, total_rows):
+def assemble(views, mask, rims, m, levels, total_rows):
     from_east, from_west, rows_first, rows_second, sides_first, sides_second = rims
-    planes = 4 * levels + 2
     rows, cols = mask.shape
     tile_row = lax.axis_index("gridy")
     odd_tile = lax.rem(tile_row, 2).astype(jnp.float32)
@@ -159,27 +163,24 @@
     def of_south(first, second):
         return south_factors[0] * first + south_factors[1] * second
 
-    wide = groups_of(planes) * LANE
-    for group in range(groups_of(planes)):
-        where = slice(group * LANE, (group + 1) * LANE)
-        where_west = slice(wide + group * LANE, wide + (group + 1) * LANE)
-        east = sides_first[m, :, where], sides_second[m, :, where]
-        west = sides_first[m, :, where_west], sides_second[m, :, where_west]
-        bands = [(TOP - CHUNK, of_south(*east), of_south(*west))]
-        for a in range(0, rows, CHUNK):
-            bands.append((TOP + a, from_east[m, a : a + CHUNK, where], from_west[m, a : a + CHUNK, where]))
-        bands.append((TOP + rows, of_north(*east), of_north(*west)))
-        for at, east, west in bands:
-            odd = ((lanes_like(east.shape) // WIDE) & 1) == 1
-            joined = (jnp.where(odd, east, west), jnp.where(odd, west, east))
-            for plane in range(group * PER_GROUP, min((group + 1) * PER_GROUP, planes)):
-                _, kind, offset = rim_place(plane)
-                ext[plane, at : at + CHUNK, cols : cols + LANE] = pltpu.roll(joined[kind], LANE - offset, 1)
-    ext[planes - 1, TOP : TOP + rows, :cols] = mask[...].astype(jnp.float32)
-    for plane in range(planes):
-        at = slice(plane * WIDE, (plane + 1) * WIDE)
-        ext[plane, TOP - WIDE : TOP, :cols] = of_south(rows_first[m, at, :], rows_second[m, at, :])
-        ext[plane, TOP + rows : TOP + rows + WIDE, :cols] = of_north(rows_first[m, at, :], rows_second[m, at, :])
+    east = sides_first[m, :, :LANE], sides_second[m, :, :LANE]
+    west = sides_first[m, :, LANE:], sides_second[m, :, LANE:]
+    bands = [(TOP - CHUNK, of_south(*east), of_south(*west))]
+    for a in range(0, rows, CHUNK):
+        bands.append((TOP + a, from_east[m, a : a + CHUNK, :], from_west[m, a : a + CHUNK, :]))
+    bands.append((TOP + rows, of_north(*east), of_north(*west)))
+    is_east = lanes_like((CHUNK, LANE)) < LANE // 2
+    layout = rim_layout(levels)
+    for at, east, west in bands:
+        for name, width, start in layout:
+            left = pltpu.roll(east, LANE - start, 1) if start else east
+            right = pltpu.roll(west, LANE - width - start, 1) if start + width < LANE else west
+            views[name][at : at + CHUNK, cols : cols + LANE] = jnp.where(is_east, left, right)
+    for name, width, start in layout:
+        at = slice(start, start + width)
+        views[name][TOP - width : TOP, :cols] = of_south(rows_first[m, at, :], rows_second[m, at, :])
+        views[name][TOP + rows : TOP + rows + width, :cols] = of_north(rows_first[m, at, :], rows_second[m, at, :])
+    views["ocean"][TOP : TOP + rows, :cols] = mask[...].astype(jnp.float32)
 
 
 def fill_rows(turn, inside, first_row, total_rows):
@@ -192,9 +193,6 @@
 
 
 KEPT = ["tu", "tv", "q", "v0", "v1", "v2"]
-KEEP_FLOW = 1.0 - STEP_DT * DRAG_K - 4.0 * VISCOSITY
-KEEP_TRACER = 1.0 - 4.0 * KAPPA
-PRESS_SCALE = PRESS_K * 0.5 * STEP_DT
 
 
 class Planes:
@@ -274,17 +272,13 @@
 def surface_start(ext, work):
     levels = work.levels
     low, high = TOP - CHUNK, TOP + work.rows + CHUNK
-    for a, b in chunks(low, high):
-        su = sv = sp = None
+    cols = work.turn.shape[1] - LANE
+    for a, b in work.main():
+        dens, *sums = level_sums(lambda i: ext[i, a:b, :cols], levels)
         for l in range(levels):
-            factor = PRESS_SCALE * (levels - l)
-            dens = (factor * BETA_S) * ext[levels + l, a:b, :] - (factor * ALPHA_T) * ext[l, a:b, :]
-            work.put("d%d" % l, a, b, dens)
-            u, v = ext[2 * levels + l, a:b, :], ext[3 * levels + l, a:b, :]
-            su, sv, sp = (u, v, dens) if l == 0 else (su + u, sv + v, sp + dens)
-        work.put("su", a, b, su)
-        work.put("sv", a, b, sv)
-        work.put("sp", a, b, sp)
+            work.views["d%d" % l][a:b, :cols] = dens[l]
+        for name, value in zip(("su", "sv", "sp"), sums):
+            work.views[name][a:b, :cols] = value
     for a, b in work.near():
         carried = None
         for l in range(levels):
@@ -328,21 +322,20 @@
     planes, turn, inside, red, mask, sems = refs[15:]
     members = kept.shape[0]
     rows, cols = mask.shape
-    copies = fetches(fields, lambda m, at: kept.at[m, at, pl.ds(TOP, rows), pl.ds(0, cols)], mask, sems, levels)
+    member_copies = fetches(fields, lambda m, at: kept.at[m, at, pl.ds(TOP, rows), pl.ds(0, cols)], mask, sems, levels)
     tile_row = lax.axis_index("gridy")
     choose(source, theirs, lax.axis_index("member"), members, info)
     fill_rows(turn, inside, tile_row * rows, total_rows)
     red[...] = jnp.zeros_like(red)
-    for m in range(members):
-        assemble(kept.at[m], mask, rims, m, levels, total_rows)
-    for copy in sum(copies, []):
-        copy.wait()
 
     def one(m, carry):
         ext = kept.at[m]
         work = Planes(levels, rows, turn, inside)
         work.add(planes, SUM_NAMES + ["d%d" % l for l in range(levels)])
         work.add(kept, ["ext%d" % i for i in range(4 * levels)] + ["eta", "ocean"] + KEPT, (m,))
+        assemble(work.views, mask, rims, m, levels, total_rows)
+        for copy in member_copies(m):
+            copy.wait()
         surface_start(ext, work)
         work.powers("v0", "v1", "v2")
         for a, b in work.main():
@@ -748,9 +741,9 @@
     total_rows = rows * count_y
     grid = ("gridy", "gridx")
 
-    their_source = swap(clone_source)
     fields = (temp, salt, uvel, vvel, eta, land_mask)
-    rims = exchange_rims(pack_rims(*fields))
+    packed, their_source = lax.optimization_barrier((pack_rims(*fields), swap(clone_source)))
+    rims = exchange_rims(packed)
     tile, kept, info = local_sums(clone_source, their_source, fields, rims, total_rows)
     tiles = from_all(jnp.broadcast_to(tile[None], (count_y * count_x,) + tile.shape), grid)
 

time: 76.3 us -> 76.6 us (level)
  waiting for transfers between devices: 13.6 us -> 11.8 us
  Pallas kernels: 27.5 us -> 28.7 us
  blocking collectives: 18.1 us -> 19 us
    ppermute x3, waiting for transfers between devices: 8.29 us -> 6.27 us  [swap(): return lax.ppermute(value, 'member', [(0, 1), (1, 0)])]
    ppermute x3, starting transfers between devices: 3.68 us -> 5.19 us  [swap(): return lax.ppermute(value, 'member', [(0, 1), (1, 0)])]
    ppermute x2, starting transfers between devices: 5.1 us -> 3.66 us  [shift(): lax.ppermute(value, axis, [(i, (i + by) % count) for i in range(count)])]
    pallas_call x1, Pallas kernels: 8.35 us -> 9.41 us  [local_sums(): pl.pallas_call(functools.partial(sums_kernel, levels, total_rows), out_sh...]
    ppermute x4, waiting for transfers between devices: 0.01 us -> 0.86 us  [pair(): return lax.ppermute(value, 'gridy', list(enumerate(partners[which])))]
    all_to_all x2, blocking collectives: 18.1 us -> 19 us  [from_all(): return lax.all_to_all(tiles, axes, split_axis=0, concat_axis=0, tiled=True)]
  transfers between devices with their start and end apart: 9 -> 9, of which waited for: 4 -> 4; matrix products, arithmetic and copies ran while one was open for 1% -> 1% of each run, Pallas kernels for 10% -> 14%
where the time goes in v2:
time: 76.6 us; the launch traced here: 76.3 us
  Pallas kernels  28.7 us (37%)
  blocking collectives  19 us (25%)
  starting transfers between devices  14 us (18%)
  waiting for transfers between devices  11.8 us (15%)
  between operations  2.11 us (3%)
    all_to_all x2, blocking collectives, from_all(): return lax.all_to_all(tiles, axes, split_axis=0, concat_axis=0, tiled=True)  19 us
    pallas_call x2, Pallas kernels, advance(): pl.pallas_call(functools.partial(advance_kernel, levels, total_rows, is_f...  13 us
    pallas_call x1, Pallas kernels, local_sums(): pl.pallas_call(functools.partial(sums_kernel, levels, total_rows), out_sh...  9.41 us
    ppermute x3, waiting for transfers between devices, swap(): return lax.ppermute(value, 'member', [(0, 1), (1, 0)])  6.27 us
    ppermute x3, starting transfers between devices, swap(): return lax.ppermute(value, 'member', [(0, 1), (1, 0)])  5.19 us
    ppermute x4, starting transfers between devices, pair(): return lax.ppermute(value, 'gridy', list(enumerate(partners[which])))  5.18 us
    ppermute x2, waiting for transfers between devices, shift(): lax.ppermute(value, axis, [(i, (i + by) % count) for i in range(count)])  4.66 us
    ppermute x2, starting transfers between devices, shift(): lax.ppermute(value, axis, [(i, (i + by) % count) for i in range(count)])  3.66 us
  transfers between devices with their start and end apart: 9, of which 4 were waited for; matrix products, arithmetic and copies ran while one was open for 1% of the time, Pallas kernels for 14%

profile of v2, /device:TPU:0, one launch (start us, length us, event | category | flops | bytes accessed | tf_op | source)
XLA Modules:
  0.0 76.3 jit_solution(10177770591610155433)
XLA Ops:
  0.7 3.0 %collective-permute-start.1 = (s32[2]{0:T(128)}, s32[2]{0:T(128)S(1)}, u32[]{:S(2)}, u32[]{:S(2)}) collective-permute-start(s32[2]{0:T(128)} %source.1), channel_id=1, source_target_pairs={{0,16},{16,0},{1,17},{17,1},{2,18},{18,2},{3,19},{19,3},{4,20},{20... | collective-permute-start | bytes 32 | tf_op jit(solution)/shard_map/ppermute | solution.py:734
  3.7 3.0 %pack_rims.1 = (f32[2,64,128]{2,1,0:T(8,128)}, f32[2,64,128]{2,1,0:T(8,128)}, f32[2,128,256]{2,1,0:T(8,128)}, f32[2,128,256]{2,1,0:T(8,128)}) custom-call(f32[2,4,64,256]{3,2,1,0:T(8,128)} %refs_0_.3, f32[2,4,64,256]{3,2,1,0:T(8,128)} %refs_1_.3, f32[2,4,64,256]{3,2,1,0:T(8,128)} %refs_2_.3, f32[2,4,64,256]{3,2,1,0:T(8,128)} %refs_3_.3, ...), custom_call_target="tpu_custom_call" | custom-call | tf_op jit(solution)/shard_map/pack_rims/pallas_call | solution.py:126
  6.8 3.7 %collective-permute-start.2 = (f32[2,64,128]{2,1,0:T(8,128)}, f32[2,64,128]{2,1,0:T(8,128)S(1)}, u32[]{:S(2)}, u32[]{:S(2)}) collective-permute-start(f32[2,64,128]{2,1,0:T(8,128)} %get-tuple-element.93), channel_id=1, source_target_pairs={{0,3},{1,0},{2,1},{3,2},{4,7},{5,4},{6,5},{7,6},{8,11},{9,8},{10,9... | collective-permute-start | bytes 196616 | tf_op jit(solution)/shard_map/ppermute | solution.py:706
  10.4 0.0 collective-permute-start.3
  10.5 1.6 %collective-permute-start.5 = (f32[2,128,256]{2,1,0:T(8,128)}, f32[2,128,256]{2,1,0:T(8,128)S(1)}, u32[]{:S(2)}, u32[]{:S(2)}) collective-permute-start(f32[2,128,256]{2,1,0:T(8,128)} %get-tuple-element.96), channel_id=1, source_target_pairs={{0,0},{4,8},{8,4},{12,12},{1,1},{5,9},{9,5},{13,13},{2,2},{6,10},{... | collective-permute-start | bytes 786440 | tf_op jit(solution)/shard_map/ppermute | solution.py:717
  12.1 0.6 collective-permute-done.2.refs_6_
  12.7 4.0 %collective-permute-done.3.refs_7_ = f32[2,64,128]{2,1,0:T(8,128)S(1)} collective-permute-done((f32[2,64,128]{2,1,0:T(8,128)}, f32[2,64,128]{2,1,0:T(8,128)S(1)}, u32[]{:S(2)}, u32[]{:S(2)}) %collective-permute-start.3) | collective-permute-done | bytes 65568 | tf_op jit(solution)/shard_map/ppermute | solution.py:706
  16.7 0.7 collective-permute-start.7
  17.4 2.9 %collective-permute-start.6 = (f32[2,16,256]{2,1,0:T(8,128)S(1)}, f32[2,16,256]{2,1,0:T(8,128)S(1)}, u32[]{:S(2)}, u32[]{:S(2)}) collective-permute-start(f32[2,16,256]{2,1,0:T(8,128)S(1)} %get-tuple-element.112), channel_id=1, source_target_pairs={{0,4},{4,0},{8,12},{12,8},{1,5},{5,1},{9,13},{13,9},{2,6},{6,2},{1... | collective-permute-start | bytes 98312 | tf_op jit(solution)/shard_map/ppermute | solution.py:717
  20.3 0.9 %collective-permute-done.6.refs_10_ = f32[2,16,256]{2,1,0:T(8,128)S(1)} collective-permute-done((f32[2,16,256]{2,1,0:T(8,128)S(1)}, f32[2,16,256]{2,1,0:T(8,128)S(1)}, u32[]{:S(2)}, u32[]{:S(2)}) %collective-permute-start.6) | collective-permute-done | bytes 32800 | tf_op jit(solution)/shard_map/ppermute | solution.py:717
  21.2 0.0 collective-permute-done.4.refs_8_
  21.3 9.4 %local_sums.1 = (f32[2,128]{1,0:T(2,128)S(1)}, f32[2,24,112,384]{3,2,1,0:T(8,128)S(1)}, s32[5]{0:T(128)S(1)}) custom-call(s32[2]{0:T(128)S(1)} %copy-done.6, s32[2]{0:T(128)S(1)} %collective-permute-done.1.theirs, f32[2,4,64,256]{3,2,1,0:T(8,128)S(1)} %copy-done, f32[2,4,64,256]{3,2,1,0:T(8,128)S(1)} %copy-done.1, f32[2,4,64,256]{3,2,1,0:T(8,128)S(1)} %copy-done.2, ...), custom_call_target="tpu_custom_call" | custom-call | flops 100000000 | bytes 4000000 | tf_op jit(solution)/shard_map/local_sums/pallas_call | solution.py:392
  30.7 9.9 %all_to_all.10.refs_1_ = f32[16,2,128]{2,1,0:T(2,128)S(1)} all-to-all(f32[16,2,128]{2,1,0:T(2,128)S(1)} %broadcast_in_dim.2), channel_id=1, replica_groups=mesh['member'=2,'gridy'=4,'gridx'=4] {'gridy','gridx'}, dimensions={0} | all-to-all | bytes 32768 | tf_op jit(solution)/shard_map/all_to_all | solution.py:730
  40.6 6.5 %advance.3 = (f32[17,64,256]{2,1,0:T(8,128)S(1)}, f32[64,128]{1,0:T(8,128)S(1)}) custom-call(s32[5]{0:T(128)S(1)} %get-tuple-element.97.refs_0_, f32[16,2,128]{2,1,0:T(2,128)S(1)} %all_to_all.10.refs_1_, f32[2,24,112,384]{3,2,1,0:T(8,128)S(1)} %get-tuple-element.99.refs_2_), custom_call_target="tpu_custom_call" | custom-call | flops 100000000 | bytes 4000000 | tf_op jit(solution)/shard_map/advance/pallas_call | solution.py:598
  47.1 0.7 collective-permute-start.9
  47.7 0.6 fusion.4
  49.6 16.4 %conditional.2 = (f32[17,64,256]{2,1,0:T(8,128)S(1)}, f32[2,4,64]{2,1,0:T(4,128)}, f32[2]{0:T(128)S(1)}) conditional(s32[]{:T(128)} %bitcast.1, () %tuple.24, (s32[5]{0:T(128)S(1)}, f32[16,2,128]{2,1,0:T(2,128)S(1)}, f32[2,24,112,384]{3,2,1,0:T(8,128)S(1)}, f32[64,128]{1,0:T(8,128)S(1)}) %tuple.25), branch_computations={%region_0.1_spmd, %region_1.2_spmd} | conditional | flops 100000000 | bytes 4065560 | solution.py:760
  49.6 6.6 %advance.2 = (f32[17,64,256]{2,1,0:T(8,128)S(1)}, f32[16,4,128]{2,1,0:T(4,128)S(1)}) custom-call(s32[5]{0:T(128)S(1)} %get-tuple-element.36.refs_0_, f32[16,2,128]{2,1,0:T(2,128)S(1)} %get-tuple-element.37.refs_1_, f32[2,24,112,384]{3,2,1,0:T(8,128)S(1)} %get-tuple-element.38.refs_2_, f32[64,128]{1,0:T(8,128)S(1)} %get-tuple-element.39.refs_3_), custom_call_target="tpu_custom_call" | custom-call | flops 100000000 | bytes 4000000 | tf_op jit(solution)/shard_map/cond/branch_1_fun/advance/pallas_call | solution.py:598
  56.2 9.1 %all_to_all.9.spread = f32[16,4,128]{2,1,0:T(4,128)S(1)} all-to-all(f32[16,4,128]{2,1,0:T(4,128)S(1)} %get-tuple-element.41), channel_id=1, replica_groups=mesh['member'=2,'gridy'=4,'gridx'=4] {'gridy','gridx'}, dimensions={0} | all-to-all | bytes 65536 | tf_op jit(solution)/shard_map/cond/branch_1_fun/all_to_all | solution.py:730
  65.3 0.7 finish.1
  66.0 1.5 %collective-permute-start.8 = (f32[2]{0:T(128)S(1)}, f32[2]{0:T(128)S(1)}, u32[]{:S(2)}, u32[]{:S(2)}) collective-permute-start(f32[2]{0:T(128)S(1)} %get-tuple-element.101), channel_id=1, source_target_pairs={{0,16},{16,0},{1,17},{17,1},{2,18},{18,2},{3,19},{19,3},{4,20},{20... | collective-permute-start | bytes 32 | tf_op jit(solution)/shard_map/ppermute | solution.py:734
  67.5 6.3 %collective-permute-done.8 = f32[2]{0:T(128)S(1)} collective-permute-done((f32[2]{0:T(128)S(1)}, f32[2]{0:T(128)S(1)}, u32[]{:S(2)}, u32[]{:S(2)}) %collective-permute-start.8) | collective-permute-done | bytes 40 | tf_op jit(solution)/shard_map/ppermute | solution.py:734
  73.8 2.5 %conditional.3 = ((f32[2,4,64,256]{3,2,1,0:T(8,128)}, f32[2,4,64,256]{3,2,1,0:T(8,128)}, f32[2,4,64,256]{3,2,1,0:T(8,128)}, f32[2,4,64,256]{3,2,1,0:T(8,128)}, f32[2,64,256]{2,1,0:T(8,128)}, /*index=5*/f32[2]{0:T(128)})) conditional(s32[]{:T(128)} %bitcast, (s32[5]{0:T(128)S(1)}, s32[2]{0:T(128)S(1)}, f32[2]{0:T(128)S(1)}, f32[2]{0:T(128)S(1)}, ...), branch_computations={%region_2.3_spmd, %region_3.4_spmd} | conditional | bytes 4456496 | solution.py:770
  73.8 2.5 %pick.2 = (f32[2,4,64,256]{3,2,1,0:T(8,128)}, f32[2,4,64,256]{3,2,1,0:T(8,128)}, f32[2,4,64,256]{3,2,1,0:T(8,128)}, f32[2,4,64,256]{3,2,1,0:T(8,128)}, f32[2,64,256]{2,1,0:T(8,128)}, /*index=5*/f32[2]{0:T(128)}) custom-call(s32[5]{0:T(128)S(1)} %get-tuple-element.44.choice, s32[2]{0:T(128)S(1)} %get-tuple-element.45.source, f32[2]{0:T(128)S(1)} %get-tuple-element.46.score, ...), custom_call_target="tpu_custom_call" | custom-call | tf_op jit(solution)/shard_map/cond/branch_0_fun/pick/pallas_call | solution.py:693
  (23 shorter events, 0.1 us)
Async XLA Ops:
  0.6 20.6 %copy-start.6 = (s32[2]{0:T(128)S(1)}, s32[2]{0:T(128)}, u32[]{:S(2)}) copy-start(s32[2]{0:T(128)} %source.1) | copy-start | bytes 28
  0.6 20.6 %copy-start.5 = (s32[64,256]{1,0:T(8,128)S(1)}, s32[64,256]{1,0:T(8,128)}, u32[]{:S(2)}) copy-start(s32[64,256]{1,0:T(8,128)} %refs_5_.3) | copy-start | bytes 196612
  0.7 20.6 %copy-start.4 = (f32[2,64,256]{2,1,0:T(8,128)S(1)}, f32[2,64,256]{2,1,0:T(8,128)}, u32[]{:S(2)}) copy-start(f32[2,64,256]{2,1,0:T(8,128)} %refs_4_.3) | copy-start | bytes 393220
  0.7 20.6 %copy-start.3 = (f32[2,4,64,256]{3,2,1,0:T(8,128)S(1)}, f32[2,4,64,256]{3,2,1,0:T(8,128)}, u32[]{:S(2)}) copy-start(f32[2,4,64,256]{3,2,1,0:T(8,128)} %refs_3_.3) | copy-start | bytes 1572868
  0.7 20.6 %copy-start.2 = (f32[2,4,64,256]{3,2,1,0:T(8,128)S(1)}, f32[2,4,64,256]{3,2,1,0:T(8,128)}, u32[]{:S(2)}) copy-start(f32[2,4,64,256]{3,2,1,0:T(8,128)} %refs_2_.3) | copy-start | bytes 1572868
  0.7 20.6 %copy-start.1 = (f32[2,4,64,256]{3,2,1,0:T(8,128)S(1)}, f32[2,4,64,256]{3,2,1,0:T(8,128)}, u32[]{:S(2)}) copy-start(f32[2,4,64,256]{3,2,1,0:T(8,128)} %refs_1_.3) | copy-start | bytes 1572868
  0.7 20.6 %copy-start = (f32[2,4,64,256]{3,2,1,0:T(8,128)S(1)}, f32[2,4,64,256]{3,2,1,0:T(8,128)}, u32[]{:S(2)}) copy-start(f32[2,4,64,256]{3,2,1,0:T(8,128)} %refs_0_.3) | copy-start | bytes 1572868
  0.7 6.1 %collective-permute-start.1 = (s32[2]{0:T(128)}, s32[2]{0:T(128)S(1)}, u32[]{:S(2)}, u32[]{:S(2)}) collective-permute-start(s32[2]{0:T(128)} %source.1), channel_id=1, source_target_pairs={{0,16},{16,0},{1,17},{17,1},{2,18},{18,2},{3,19},{19,3},{4,20},{20... | collective-permute-start | bytes 32 | tf_op jit(solution)/shard_map/ppermute | solution.py:734
  6.8 5.9 %collective-permute-start.2 = (f32[2,64,128]{2,1,0:T(8,128)}, f32[2,64,128]{2,1,0:T(8,128)S(1)}, u32[]{:S(2)}, u32[]{:S(2)}) collective-permute-start(f32[2,64,128]{2,1,0:T(8,128)} %get-tuple-element.93), channel_id=1, source_target_pairs={{0,3},{1,0},{2,1},{3,2},{4,7},{5,4},{6,5},{7,6},{8,11},{9,8},{10,9... | collective-permute-start | bytes 196616 | tf_op jit(solution)/shard_map/ppermute | solution.py:706
  10.4 6.3 %collective-permute-start.3 = (f32[2,64,128]{2,1,0:T(8,128)}, f32[2,64,128]{2,1,0:T(8,128)S(1)}, u32[]{:S(2)}, u32[]{:S(2)}) collective-permute-start(f32[2,64,128]{2,1,0:T(8,128)} %get-tuple-element.94), channel_id=1, source_target_pairs={{0,1},{1,2},{2,3},{3,0},{4,5},{5,6},{6,7},{7,4},{8,9},{9,10},{10,1... | collective-permute-start | bytes 196616 | tf_op jit(solution)/shard_map/ppermute | solution.py:706
  10.4 10.7 %collective-permute-start.4 = (f32[2,128,256]{2,1,0:T(8,128)}, f32[2,128,256]{2,1,0:T(8,128)S(1)}, u32[]{:S(2)}, u32[]{:S(2)}) collective-permute-start(f32[2,128,256]{2,1,0:T(8,128)} %get-tuple-element.95), channel_id=1, source_target_pairs={{0,4},{4,0},{8,12},{12,8},{1,5},{5,1},{9,13},{13,9},{2,6},{6,2},{1... | collective-permute-start | bytes 786440 | tf_op jit(solution)/shard_map/ppermute | solution.py:717
  10.5 10.7 %collective-permute-start.5 = (f32[2,128,256]{2,1,0:T(8,128)}, f32[2,128,256]{2,1,0:T(8,128)S(1)}, u32[]{:S(2)}, u32[]{:S(2)}) collective-permute-start(f32[2,128,256]{2,1,0:T(8,128)} %get-tuple-element.96), channel_id=1, source_target_pairs={{0,0},{4,8},{8,4},{12,12},{1,1},{5,9},{9,5},{13,13},{2,2},{6,10},{... | collective-permute-start | bytes 786440 | tf_op jit(solution)/shard_map/ppermute | solution.py:717
  16.7 3.6 %collective-permute-start.7 = (f32[2,16,256]{2,1,0:T(8,128)S(1)}, f32[2,16,256]{2,1,0:T(8,128)S(1)}, u32[]{:S(2)}, u32[]{:S(2)}) collective-permute-start(f32[2,16,256]{2,1,0:T(8,128)S(1)} %get-tuple-element.111), channel_id=1, source_target_pairs={{0,0},{4,8},{8,4},{12,12},{1,1},{5,9},{9,5},{13,13},{2,2},{6,10},{... | collective-permute-start | bytes 98312 | tf_op jit(solution)/shard_map/ppermute | solution.py:717
  17.4 3.8 %collective-permute-start.6 = (f32[2,16,256]{2,1,0:T(8,128)S(1)}, f32[2,16,256]{2,1,0:T(8,128)S(1)}, u32[]{:S(2)}, u32[]{:S(2)}) collective-permute-start(f32[2,16,256]{2,1,0:T(8,128)S(1)} %get-tuple-element.112), channel_id=1, source_target_pairs={{0,4},{4,0},{8,12},{12,8},{1,5},{5,1},{9,13},{13,9},{2,6},{6,2},{1... | collective-permute-start | bytes 98312 | tf_op jit(solution)/shard_map/ppermute | solution.py:717
  47.1 26.7 %collective-permute-start.9 = (f32[17,64,256]{2,1,0:T(8,128)S(1)}, f32[17,64,256]{2,1,0:T(8,128)S(1)}, u32[]{:S(2)}, u32[]{:S(2)}) collective-permute-start(f32[17,64,256]{2,1,0:T(8,128)S(1)} %get-tuple-element.102), channel_id=1, source_target_pairs={{0,16},{16,0},{1,17},{17,1},{2,18},{18,2},{3,19},{19,3},{4,20},{20... | collective-permute-start | bytes 3342344 | tf_op jit(solution)/shard_map/ppermute | solution.py:734
  66.0 7.8 %collective-permute-start.8 = (f32[2]{0:T(128)S(1)}, f32[2]{0:T(128)S(1)}, u32[]{:S(2)}, u32[]{:S(2)}) collective-permute-start(f32[2]{0:T(128)S(1)} %get-tuple-element.101), channel_id=1, source_target_pairs={{0,16},{16,0},{1,17},{17,1},{2,18},{18,2},{3,19},{19,3},{4,20},{20... | collective-permute-start | bytes 32 | tf_op jit(solution)/shard_map/ppermute | solution.py:734

commit v3 on v0

--- a/solution.py
+++ b/solution.py
@@ -29,6 +29,8 @@
 WIDE = 10
 TOP = 24
 CHUNK = 16
+CHUNK_2D = 8
+CHUNK_3D = 16
 LANE = 128
 PER_GROUP = 11
 PAIRS = [(a, b) for a in range(4) for b in range(a, 4)]
@@ -138,8 +140,8 @@
     return pltpu.roll(value, width - 1, 1), pltpu.roll(value, 1, 1)
 
 
-def chunks(first, last):
-    return [(a, min(a + CHUNK, last)) for a in range(first, last, CHUNK)]
+def chunks(first, last, size=CHUNK_2D):
+    return [(a, min(a + size, last)) for a in range(first, last, size)]
 
 
 def assemble(ext, mask, rims, m, levels, total_rows):
@@ -558,26 +560,26 @@
         work.put(press, a, b, work.get(press, a, b) + dens)
 
     def level(l, carry):
-        for a in range(TOP - CHUNK, TOP + rows + CHUNK, 8):
-            add_press(ext, l, "p", a, a + 8)
-        for a in range(low, high, 8):
-            temp, salt, u, v = step(ext, l, "p", a, a + 8, cols + LANE)
-            after[l, a : a + 8, :] = temp
-            after[levels + l, a : a + 8, :] = salt
-            after[2 * levels + l, a : a + 8, :] = u - work.get("gu1", a, a + 8)
-            after[3 * levels + l, a : a + 8, :] = v - work.get("gv1", a, a + 8)
-        for a in range(low, high, 8):
-            add_press(after, l, "p2", a, a + 8)
-        for a in range(TOP, TOP + rows, 8):
-            temp, salt, u, v = step(after, l, "p2", a, a + 8, cols)
-            here = slice(a - TOP, a - TOP + 8)
-            v = v - work.get("gv2", a, a + 8)[:, :cols]
+        for a, b in chunks(TOP - CHUNK, TOP + rows + CHUNK, CHUNK_3D):
+            add_press(ext, l, "p", a, b)
+        for a, b in chunks(low, high, CHUNK_3D):
+            temp, salt, u, v = step(ext, l, "p", a, b, cols + LANE)
+            after[l, a:b, :] = temp
+            after[levels + l, a:b, :] = salt
+            after[2 * levels + l, a:b, :] = u - work.get("gu1", a, b)
+            after[3 * levels + l, a:b, :] = v - work.get("gv1", a, b)
+        for a, b in chunks(low, high, CHUNK_3D):
+            add_press(after, l, "p2", a, b)
+        for a, b in chunks(TOP, TOP + rows, CHUNK_3D):
+            temp, salt, u, v = step(after, l, "p2", a, b, cols)
+            here = slice(a - TOP, b - TOP)
+            v = v - work.get("gv2", a, b)[:, :cols]
             out[l, here, :] = temp
             out[levels + l, here, :] = salt
-            out[2 * levels + l, here, :] = u - work.get("gu2", a, a + 8)[:, :cols]
+            out[2 * levels + l, here, :] = u - work.get("gu2", a, b)[:, :cols]
             out[3 * levels + l, here, :] = v
             row_sum = jnp.sum(v, axis=1, keepdims=True)
-            zonal[here, :] = jnp.where(lanes_like((8, LANE)) == member * levels + l, row_sum, zonal[here, :])
+            zonal[here, :] = jnp.where(lanes_like((b - a, LANE)) == member * levels + l, row_sum, zonal[here, :])
         return carry
 
     lax.fori_loop(0, levels, level, 0)
@@ -748,9 +750,9 @@
     total_rows = rows * count_y
     grid = ("gridy", "gridx")
 
-    their_source = swap(clone_source)
     fields = (temp, salt, uvel, vvel, eta, land_mask)
-    rims = exchange_rims(pack_rims(*fields))
+    packed, their_source = lax.optimization_barrier((pack_rims(*fields), swap(clone_source)))
+    rims = exchange_rims(packed)
     tile, kept, info = local_sums(clone_source, their_source, fields, rims, total_rows)
     tiles = from_all(jnp.broadcast_to(tile[None], (count_y * count_x,) + tile.shape), grid)
 

time: 76.3 us -> 102 us (1.34)
  waiting for transfers between devices: 13.6 us -> 38.3 us
  Pallas kernels: 27.5 us -> 25.4 us
  blocking collectives: 18.1 us -> 20.2 us
    ppermute x3 -> x4, waiting for transfers between devices: 8.29 us -> 32.1 us  [swap(): return lax.ppermute(value, 'member', [(0, 1), (1, 0)])]
    ppermute x3 -> x4, starting transfers between devices: 3.68 us -> 5.85 us  [swap(): return lax.ppermute(value, 'member', [(0, 1), (1, 0)])]
    all_to_all x2, blocking collectives: 18.1 us -> 20.2 us  [from_all(): return lax.all_to_all(tiles, axes, split_axis=0, concat_axis=0, tiled=True)]
    pallas_call x2, Pallas kernels: 13 us -> 11.4 us  [advance(): pl.pallas_call(functools.partial(advance_kernel, levels, total_rows, is_f...]
    ppermute x2, starting transfers between devices: 5.1 us -> 3.66 us  [shift(): lax.ppermute(value, axis, [(i, (i + by) % count) for i in range(count)])]
  transfers between devices with their start and end apart: 9 -> 10, of which waited for: 4 -> 5; matrix products, arithmetic and copies ran while one was open for 1% -> 1% of each run, Pallas kernels for 10% -> 9%
where the time goes in v3:
time: 102 us; the launch traced here: 101 us
  waiting for transfers between devices  38.3 us (38%)
  Pallas kernels  25.4 us (25%)
  blocking collectives  20.2 us (20%)
  starting transfers between devices  14.7 us (14%)
  between operations  2.11 us (2%)
    ppermute x4, waiting for transfers between devices, swap(): return lax.ppermute(value, 'member', [(0, 1), (1, 0)])  32.1 us
    all_to_all x2, blocking collectives, from_all(): return lax.all_to_all(tiles, axes, split_axis=0, concat_axis=0, tiled=True)  20.2 us
    pallas_call x2, Pallas kernels, advance(): pl.pallas_call(functools.partial(advance_kernel, levels, total_rows, is_f...  11.4 us
    pallas_call x1, Pallas kernels, local_sums(): pl.pallas_call(functools.partial(sums_kernel, levels, total_rows), out_sh...  8.09 us
    ppermute x4, starting transfers between devices, swap(): return lax.ppermute(value, 'member', [(0, 1), (1, 0)])  5.85 us
    ppermute x2, waiting for transfers between devices, shift(): lax.ppermute(value, axis, [(i, (i + by) % count) for i in range(count)])  5.32 us
    ppermute x4, starting transfers between devices, pair(): return lax.ppermute(value, 'gridy', list(enumerate(partners[which])))  5.22 us
    ppermute x2, starting transfers between devices, shift(): lax.ppermute(value, axis, [(i, (i + by) % count) for i in range(count)])  3.66 us
  transfers between devices with their start and end apart: 10, of which 5 were waited for; matrix products, arithmetic and copies ran while one was open for 1% of the time, Pallas kernels for 9%

profile of v3, /device:TPU:0, one launch (start us, length us, event | category | flops | bytes accessed | tf_op | source)
XLA Modules:
  0.0 101.5 jit_solution(1720115451503407346)
XLA Ops:
  0.7 3.0 %collective-permute-start.1 = (s32[2]{0:T(128)}, s32[2]{0:T(128)S(1)}, u32[]{:S(2)}, u32[]{:S(2)}) collective-permute-start(s32[2]{0:T(128)} %source.1), channel_id=1, source_target_pairs={{0,16},{16,0},{1,17},{17,1},{2,18},{18,2},{3,19},{19,3},{4,20},{20... | collective-permute-start | bytes 32 | tf_op jit(solution)/shard_map/ppermute | solution.py:743
  3.7 2.7 %pack_rims.1 = (f32[2,64,256]{2,1,0:T(8,128)}, f32[2,64,256]{2,1,0:T(8,128)}, f32[2,184,256]{2,1,0:T(8,128)}, f32[2,184,256]{2,1,0:T(8,128)}) custom-call(f32[2,4,64,256]{3,2,1,0:T(8,128)} %refs_0_.3, f32[2,4,64,256]{3,2,1,0:T(8,128)} %refs_1_.3, f32[2,4,64,256]{3,2,1,0:T(8,128)} %refs_2_.3, f32[2,4,64,256]{3,2,1,0:T(8,128)} %refs_3_.3, ...), custom_call_target="tpu_custom_call" | custom-call | tf_op jit(solution)/shard_map/pack_rims/pallas_call | solution.py:123
  6.5 3.7 %collective-permute-start.2 = (f32[2,64,256]{2,1,0:T(8,128)}, f32[2,64,256]{2,1,0:T(8,128)S(1)}, u32[]{:S(2)}, u32[]{:S(2)}) collective-permute-start(f32[2,64,256]{2,1,0:T(8,128)} %get-tuple-element.93), channel_id=1, source_target_pairs={{0,3},{1,0},{2,1},{3,2},{4,7},{5,4},{6,5},{7,6},{8,11},{9,8},{10,9... | collective-permute-start | bytes 393224 | tf_op jit(solution)/shard_map/ppermute | solution.py:715
  10.1 1.6 %collective-permute-start.5 = (f32[2,184,256]{2,1,0:T(8,128)}, f32[2,184,256]{2,1,0:T(8,128)S(1)}, u32[]{:S(2)}, u32[]{:S(2)}) collective-permute-start(f32[2,184,256]{2,1,0:T(8,128)} %get-tuple-element.96), channel_id=1, source_target_pairs={{0,0},{4,8},{8,4},{12,12},{1,1},{5,9},{9,5},{13,13},{2,2},{6,10},{... | collective-permute-start | bytes 1130504 | tf_op jit(solution)/shard_map/ppermute | solution.py:726
  11.8 2.6 %collective-permute-done.2.refs_6_ = f32[2,64,256]{2,1,0:T(8,128)S(1)} collective-permute-done((f32[2,64,256]{2,1,0:T(8,128)}, f32[2,64,256]{2,1,0:T(8,128)S(1)}, u32[]{:S(2)}, u32[]{:S(2)}) %collective-permute-start.2) | collective-permute-done | bytes 131104 | tf_op jit(solution)/shard_map/ppermute | solution.py:715
  14.4 2.7 %collective-permute-done.3.refs_7_ = f32[2,64,256]{2,1,0:T(8,128)S(1)} collective-permute-done((f32[2,64,256]{2,1,0:T(8,128)}, f32[2,64,256]{2,1,0:T(8,128)S(1)}, u32[]{:S(2)}, u32[]{:S(2)}) %collective-permute-start.3) | collective-permute-done | bytes 131104 | tf_op jit(solution)/shard_map/ppermute | solution.py:715
  17.1 0.7 collective-permute-start.7
  17.8 2.9 %collective-permute-start.6 = (f32[2,16,512]{2,1,0:T(8,128)S(1)}, f32[2,16,512]{2,1,0:T(8,128)S(1)}, u32[]{:S(2)}, u32[]{:S(2)}) collective-permute-start(f32[2,16,512]{2,1,0:T(8,128)S(1)} %get-tuple-element.112), channel_id=1, source_target_pairs={{0,4},{4,0},{8,12},{12,8},{1,5},{5,1},{9,13},{13,9},{2,6},{6,2},{1... | collective-permute-start | bytes 196616 | tf_op jit(solution)/shard_map/ppermute | solution.py:726
  20.7 0.9 collective-permute-done.6.refs_10_
  21.7 8.1 %local_sums.1 = (f32[2,128]{1,0:T(2,128)S(1)}, f32[2,24,112,384]{3,2,1,0:T(8,128)S(1)}, s32[5]{0:T(128)S(1)}) custom-call(s32[2]{0:T(128)S(1)} %copy-done.6, s32[2]{0:T(128)S(1)} %collective-permute-done.1.theirs, f32[2,4,64,256]{3,2,1,0:T(8,128)S(1)} %copy-done, f32[2,4,64,256]{3,2,1,0:T(8,128)S(1)} %copy-done.1, f32[2,4,64,256]{3,2,1,0:T(8,128)S(1)} %copy-done.2, ...), custom_call_target="tpu_custom_call" | custom-call | flops 100000000 | bytes 4000000 | tf_op jit(solution)/shard_map/local_sums/pallas_call | solution.py:401
  29.8 11.1 %all_to_all.10.refs_1_ = f32[16,2,128]{2,1,0:T(2,128)S(1)} all-to-all(f32[16,2,128]{2,1,0:T(2,128)S(1)} %broadcast_in_dim.2), channel_id=1, replica_groups=mesh['member'=2,'gridy'=4,'gridx'=4] {'gridy','gridx'}, dimensions={0} | all-to-all | bytes 32768 | tf_op jit(solution)/shard_map/all_to_all | solution.py:739
  40.9 5.6 %advance.3 = (f32[17,64,256]{2,1,0:T(8,128)S(1)}, f32[64,128]{1,0:T(8,128)S(1)}) custom-call(s32[5]{0:T(128)S(1)} %get-tuple-element.97.refs_0_, f32[16,2,128]{2,1,0:T(2,128)S(1)} %all_to_all.10.refs_1_, f32[2,24,112,384]{3,2,1,0:T(8,128)S(1)} %get-tuple-element.99.refs_2_), custom_call_target="tpu_custom_call" | custom-call | flops 100000000 | bytes 4000000 | tf_op jit(solution)/shard_map/advance/pallas_call | solution.py:607
  46.5 0.7 collective-permute-start.9
  47.3 0.6 fusion.4
  49.2 15.6 %conditional.2 = (f32[17,64,256]{2,1,0:T(8,128)S(1)}, f32[2,4,64]{2,1,0:T(4,128)}, f32[2]{0:T(128)S(1)}) conditional(s32[]{:T(128)} %bitcast.1, () %tuple.24, (s32[5]{0:T(128)S(1)}, f32[16,2,128]{2,1,0:T(2,128)S(1)}, f32[2,24,112,384]{3,2,1,0:T(8,128)S(1)}, f32[64,128]{1,0:T(8,128)S(1)}) %tuple.25), branch_computations={%region_0.1_spmd, %region_1.2_spmd} | conditional | flops 100000000 | bytes 4065560 | solution.py:769
  49.2 5.8 %advance.2 = (f32[17,64,256]{2,1,0:T(8,128)S(1)}, f32[16,4,128]{2,1,0:T(4,128)S(1)}) custom-call(s32[5]{0:T(128)S(1)} %get-tuple-element.36.refs_0_, f32[16,2,128]{2,1,0:T(2,128)S(1)} %get-tuple-element.37.refs_1_, f32[2,24,112,384]{3,2,1,0:T(8,128)S(1)} %get-tuple-element.38.refs_2_, f32[64,128]{1,0:T(8,128)S(1)} %get-tuple-element.39.refs_3_), custom_call_target="tpu_custom_call" | custom-call | flops 100000000 | bytes 4000000 | tf_op jit(solution)/shard_map/cond/branch_1_fun/advance/pallas_call | solution.py:607
  55.0 9.1 %all_to_all.9.spread = f32[16,4,128]{2,1,0:T(4,128)S(1)} all-to-all(f32[16,4,128]{2,1,0:T(4,128)S(1)} %get-tuple-element.41), channel_id=1, replica_groups=mesh['member'=2,'gridy'=4,'gridx'=4] {'gridy','gridx'}, dimensions={0} | all-to-all | bytes 65536 | tf_op jit(solution)/shard_map/cond/branch_1_fun/all_to_all | solution.py:739
  64.0 0.7 finish.1
  64.7 1.4 %collective-permute-start.8 = (f32[2]{0:T(128)S(1)}, f32[2]{0:T(128)S(1)}, u32[]{:S(2)}, u32[]{:S(2)}) collective-permute-start(f32[2]{0:T(128)S(1)} %get-tuple-element.101), channel_id=1, source_target_pairs={{0,16},{16,0},{1,17},{17,1},{2,18},{18,2},{3,19},{19,3},{4,20},{20... | collective-permute-start | bytes 32 | tf_op jit(solution)/shard_map/ppermute | solution.py:743
  66.2 7.1 %collective-permute-done.8 = f32[2]{0:T(128)S(1)} collective-permute-done((f32[2]{0:T(128)S(1)}, f32[2]{0:T(128)S(1)}, u32[]{:S(2)}, u32[]{:S(2)}) %collective-permute-start.8) | collective-permute-done | bytes 40 | tf_op jit(solution)/shard_map/ppermute | solution.py:743
  73.3 28.2 %conditional.3 = ((f32[2,4,64,256]{3,2,1,0:T(8,128)}, f32[2,4,64,256]{3,2,1,0:T(8,128)}, f32[2,4,64,256]{3,2,1,0:T(8,128)}, f32[2,4,64,256]{3,2,1,0:T(8,128)}, f32[2,64,256]{2,1,0:T(8,128)}, /*index=5*/f32[2]{0:T(128)})) conditional(s32[]{:T(128)} %bitcast, (s32[5]{0:T(128)S(1)}, s32[2]{0:T(128)S(1)}, f32[2]{0:T(128)S(1)}, f32[2]{0:T(128)S(1)}, ...), branch_computations={%region_2.3_spmd, %region_3.4_spmd} | conditional | bytes 4456496 | solution.py:779
  73.3 0.7 collective-permute-start
  73.9 25.0 %collective-permute-done.refs_3_ = f32[17,64,256]{2,1,0:T(8,128)S(1)} collective-permute-done((f32[17,64,256]{2,1,0:T(8,128)S(1)}, f32[17,64,256]{2,1,0:T(8,128)S(1)}, u32[]{:S(2)}, u32[]{:S(2)}) %collective-permute-start) | collective-permute-done | bytes 1114144 | tf_op jit(solution)/shard_map/cond/branch_1_fun/ppermute | solution.py:743
  99.0 2.5 %pick.3 = (f32[2,4,64,256]{3,2,1,0:T(8,128)}, f32[2,4,64,256]{3,2,1,0:T(8,128)}, f32[2,4,64,256]{3,2,1,0:T(8,128)}, f32[2,4,64,256]{3,2,1,0:T(8,128)}, f32[2,64,256]{2,1,0:T(8,128)}, /*index=5*/f32[2]{0:T(128)}) custom-call(s32[5]{0:T(128)S(1)} %get-tuple-element.51.choice, s32[2]{0:T(128)S(1)} %get-tuple-element.52.source, f32[2]{0:T(128)S(1)} %get-tuple-element.53.score, ...), custom_call_target="tpu_custom_call" | custom-call | tf_op jit(solution)/shard_map/cond/branch_1_fun/pick/pallas_call | solution.py:702
  (25 shorter events, 0.1 us)
Async XLA Ops:
  0.6 21.0 %copy-start.6 = (s32[2]{0:T(128)S(1)}, s32[2]{0:T(128)}, u32[]{:S(2)}) copy-start(s32[2]{0:T(128)} %source.1) | copy-start | bytes 28
  0.6 21.0 %copy-start.5 = (s32[64,256]{1,0:T(8,128)S(1)}, s32[64,256]{1,0:T(8,128)}, u32[]{:S(2)}) copy-start(s32[64,256]{1,0:T(8,128)} %refs_5_.3) | copy-start | bytes 196612
  0.7 21.0 %copy-start.4 = (f32[2,64,256]{2,1,0:T(8,128)S(1)}, f32[2,64,256]{2,1,0:T(8,128)}, u32[]{:S(2)}) copy-start(f32[2,64,256]{2,1,0:T(8,128)} %refs_4_.3) | copy-start | bytes 393220
  0.7 21.0 %copy-start.3 = (f32[2,4,64,256]{3,2,1,0:T(8,128)S(1)}, f32[2,4,64,256]{3,2,1,0:T(8,128)}, u32[]{:S(2)}) copy-start(f32[2,4,64,256]{3,2,1,0:T(8,128)} %refs_3_.3) | copy-start | bytes 1572868
  0.7 21.0 %copy-start.2 = (f32[2,4,64,256]{3,2,1,0:T(8,128)S(1)}, f32[2,4,64,256]{3,2,1,0:T(8,128)}, u32[]{:S(2)}) copy-start(f32[2,4,64,256]{3,2,1,0:T(8,128)} %refs_2_.3) | copy-start | bytes 1572868
  0.7 21.0 %copy-start.1 = (f32[2,4,64,256]{3,2,1,0:T(8,128)S(1)}, f32[2,4,64,256]{3,2,1,0:T(8,128)}, u32[]{:S(2)}) copy-start(f32[2,4,64,256]{3,2,1,0:T(8,128)} %refs_1_.3) | copy-start | bytes 1572868
  0.7 21.0 %copy-start = (f32[2,4,64,256]{3,2,1,0:T(8,128)S(1)}, f32[2,4,64,256]{3,2,1,0:T(8,128)}, u32[]{:S(2)}) copy-start(f32[2,4,64,256]{3,2,1,0:T(8,128)} %refs_0_.3) | copy-start | bytes 1572868
  0.7 5.8 %collective-permute-start.1 = (s32[2]{0:T(128)}, s32[2]{0:T(128)S(1)}, u32[]{:S(2)}, u32[]{:S(2)}) collective-permute-start(s32[2]{0:T(128)} %source.1), channel_id=1, source_target_pairs={{0,16},{16,0},{1,17},{17,1},{2,18},{18,2},{3,19},{19,3},{4,20},{20... | collective-permute-start | bytes 32 | tf_op jit(solution)/shard_map/ppermute | solution.py:743
  6.5 7.9 %collective-permute-start.2 = (f32[2,64,256]{2,1,0:T(8,128)}, f32[2,64,256]{2,1,0:T(8,128)S(1)}, u32[]{:S(2)}, u32[]{:S(2)}) collective-permute-start(f32[2,64,256]{2,1,0:T(8,128)} %get-tuple-element.93), channel_id=1, source_target_pairs={{0,3},{1,0},{2,1},{3,2},{4,7},{5,4},{6,5},{7,6},{8,11},{9,8},{10,9... | collective-permute-start | bytes 393224 | tf_op jit(solution)/shard_map/ppermute | solution.py:715
  10.1 7.0 %collective-permute-start.3 = (f32[2,64,256]{2,1,0:T(8,128)}, f32[2,64,256]{2,1,0:T(8,128)S(1)}, u32[]{:S(2)}, u32[]{:S(2)}) collective-permute-start(f32[2,64,256]{2,1,0:T(8,128)} %get-tuple-element.94), channel_id=1, source_target_pairs={{0,1},{1,2},{2,3},{3,0},{4,5},{5,6},{6,7},{7,4},{8,9},{9,10},{10,1... | collective-permute-start | bytes 393224 | tf_op jit(solution)/shard_map/ppermute | solution.py:715
  10.1 11.5 %collective-permute-start.4 = (f32[2,184,256]{2,1,0:T(8,128)}, f32[2,184,256]{2,1,0:T(8,128)S(1)}, u32[]{:S(2)}, u32[]{:S(2)}) collective-permute-start(f32[2,184,256]{2,1,0:T(8,128)} %get-tuple-element.95), channel_id=1, source_target_pairs={{0,4},{4,0},{8,12},{12,8},{1,5},{5,1},{9,13},{13,9},{2,6},{6,2},{1... | collective-permute-start | bytes 1130504 | tf_op jit(solution)/shard_map/ppermute | solution.py:726
  10.1 11.5 %collective-permute-start.5 = (f32[2,184,256]{2,1,0:T(8,128)}, f32[2,184,256]{2,1,0:T(8,128)S(1)}, u32[]{:S(2)}, u32[]{:S(2)}) collective-permute-start(f32[2,184,256]{2,1,0:T(8,128)} %get-tuple-element.96), channel_id=1, source_target_pairs={{0,0},{4,8},{8,4},{12,12},{1,1},{5,9},{9,5},{13,13},{2,2},{6,10},{... | collective-permute-start | bytes 1130504 | tf_op jit(solution)/shard_map/ppermute | solution.py:726
  17.1 3.6 %collective-permute-start.7 = (f32[2,16,512]{2,1,0:T(8,128)S(1)}, f32[2,16,512]{2,1,0:T(8,128)S(1)}, u32[]{:S(2)}, u32[]{:S(2)}) collective-permute-start(f32[2,16,512]{2,1,0:T(8,128)S(1)} %get-tuple-element.111), channel_id=1, source_target_pairs={{0,0},{4,8},{8,4},{12,12},{1,1},{5,9},{9,5},{13,13},{2,2},{6,10},{... | collective-permute-start | bytes 196616 | tf_op jit(solution)/shard_map/ppermute | solution.py:726
  17.8 3.8 %collective-permute-start.6 = (f32[2,16,512]{2,1,0:T(8,128)S(1)}, f32[2,16,512]{2,1,0:T(8,128)S(1)}, u32[]{:S(2)}, u32[]{:S(2)}) collective-permute-start(f32[2,16,512]{2,1,0:T(8,128)S(1)} %get-tuple-element.112), channel_id=1, source_target_pairs={{0,4},{4,0},{8,12},{12,8},{1,5},{5,1},{9,13},{13,9},{2,6},{6,2},{1... | collective-permute-start | bytes 196616 | tf_op jit(solution)/shard_map/ppermute | solution.py:726
  46.5 26.7 %collective-permute-start.9 = (f32[17,64,256]{2,1,0:T(8,128)S(1)}, f32[17,64,256]{2,1,0:T(8,128)S(1)}, u32[]{:S(2)}, u32[]{:S(2)}) collective-permute-start(f32[17,64,256]{2,1,0:T(8,128)S(1)} %get-tuple-element.102), channel_id=1, source_target_pairs={{0,16},{16,0},{1,17},{17,1},{2,18},{18,2},{3,19},{19,3},{4,20},{20... | collective-permute-start | bytes 3342344 | tf_op jit(solution)/shard_map/ppermute | solution.py:743
  64.7 8.5 %collective-permute-start.8 = (f32[2]{0:T(128)S(1)}, f32[2]{0:T(128)S(1)}, u32[]{:S(2)}, u32[]{:S(2)}) collective-permute-start(f32[2]{0:T(128)S(1)} %get-tuple-element.101), channel_id=1, source_target_pairs={{0,16},{16,0},{1,17},{17,1},{2,18},{18,2},{3,19},{19,3},{4,20},{20... | collective-permute-start | bytes 32 | tf_op jit(solution)/shard_map/ppermute | solution.py:743
  73.3 25.7 %collective-permute-start = (f32[17,64,256]{2,1,0:T(8,128)S(1)}, f32[17,64,256]{2,1,0:T(8,128)S(1)}, u32[]{:S(2)}, u32[]{:S(2)}) collective-permute-start(f32[17,64,256]{2,1,0:T(8,128)S(1)} %get-tuple-element.56.refs_1_), channel_id=1, source_target_pairs={{0,16},{16,0},{1,17},{17,1},{2,18},{18,2},{3,19},{19,3},{4,20},{20... | collective-permute-start | bytes 3342344 | tf_op jit(solution)/shard_map/cond/branch_1_fun/ppermute | solution.py:743

commit v4 on v3

--- a/solution.py
+++ b/solution.py
@@ -30,7 +30,7 @@
 TOP = 24
 CHUNK = 16
 CHUNK_2D = 8
-CHUNK_3D = 16
+CHUNK_3D = 32
 LANE = 128
 PER_GROUP = 11
 PAIRS = [(a, b) for a in range(4) for b in range(a, 4)]
@@ -144,10 +144,10 @@
     return [(a, min(a + size, last)) for a in range(first, last, size)]
 
 
-def assemble(ext, mask, rims, m, levels, total_rows):
+def assemble(ext, fields, rims, m, levels, total_rows):
     from_east, from_west, rows_first, rows_second, sides_first, sides_second = rims
     planes = 4 * levels + 2
-    rows, cols = mask.shape
+    rows, cols = fields[5].shape
     tile_row = lax.axis_index("gridy")
     odd_tile = lax.rem(tile_row, 2).astype(jnp.float32)
     keep_south = jnp.where(tile_row > 0, 1.0, 0.0).astype(jnp.float32)
@@ -177,8 +177,12 @@
             for plane in range(group * PER_GROUP, min((group + 1) * PER_GROUP, planes)):
                 _, kind, offset = rim_place(plane)
                 ext[plane, at : at + CHUNK, cols : cols + LANE] = pltpu.roll(joined[kind], LANE - offset, 1)
-    ext[planes - 1, TOP : TOP + rows, :cols] = mask[...].astype(jnp.float32)
     for plane in range(planes):
+        if plane < 4 * levels:
+            value = fields[plane // levels][m, plane % levels]
+        else:
+            value = fields[4][m] if plane == 4 * levels else fields[5][...].astype(jnp.float32)
+        ext[plane, TOP : TOP + rows, :cols] = value
         at = slice(plane * WIDE, (plane + 1) * WIDE)
         ext[plane, TOP - WIDE : TOP, :cols] = of_south(rows_first[m, at, :], rows_second[m, at, :])
         ext[plane, TOP + rows : TOP + rows + WIDE, :cols] = of_north(rows_first[m, at, :], rows_second[m, at, :])
@@ -327,21 +331,17 @@
 
 def sums_kernel(levels, total_rows, source, theirs, *refs):
     fields, rims, out, kept, info = refs[:6], refs[6:12], refs[12], refs[13], refs[14]
-    planes, turn, inside, red, mask, sems = refs[15:]
+    planes, turn, inside, red = refs[15:]
     members = kept.shape[0]
-    rows, cols = mask.shape
-    copies = fetches(fields, lambda m, at: kept.at[m, at, pl.ds(TOP, rows), pl.ds(0, cols)], mask, sems, levels)
+    rows, cols = fields[5].shape
     tile_row = lax.axis_index("gridy")
     choose(source, theirs, lax.axis_index("member"), members, info)
     fill_rows(turn, inside, tile_row * rows, total_rows)
     red[...] = jnp.zeros_like(red)
-    for m in range(members):
-        assemble(kept.at[m], mask, rims, m, levels, total_rows)
-    for copy in sum(copies, []):
-        copy.wait()
 
     def one(m, carry):
         ext = kept.at[m]
+        assemble(ext, fields, rims, m, levels, total_rows)
         work = Planes(levels, rows, turn, inside)
         work.add(planes, SUM_NAMES + ["d%d" % l for l in range(levels)])
         work.add(kept, ["ext%d" % i for i in range(4 * levels)] + ["eta", "ocean"] + KEPT, (m,))
@@ -405,15 +405,13 @@
             jax.ShapeDtypeStruct(kept, jnp.float32),
             jax.ShapeDtypeStruct((members + 3,), jnp.int32),
         ),
-        in_specs=in_smem(2) + in_hbm(6) + whole(6),
+        in_specs=in_smem(2) + whole(12),
         out_specs=tuple(whole(2) + in_smem(1)),
         scratch_shapes=[
             pltpu.VMEM((len(SUM_NAMES) + levels,) + shape, jnp.float32),
             pltpu.VMEM(shape, jnp.float32),
             pltpu.VMEM(shape, jnp.float32),
             pltpu.VMEM((members, LANE, LANE), jnp.float32),
-            pltpu.VMEM((rows, cols), jnp.int32),
-            pltpu.SemaphoreType.DMA((members, 6)),
         ],
         compiler_params=pltpu.CompilerParams(vmem_limit_bytes=VMEM_LIMIT),
         cost_estimate=pl.CostEstimate(flops=10**8, bytes_accessed=4 * 10**6, transcendentals=0),
@@ -715,7 +713,7 @@
     return lax.ppermute(value, axis, [(i, (i + by) % count) for i in range(count)])
 
 
-def exchange_rims(packed):
+def exchange_rims(packed, clone_source):
     to_west, to_east, rows_first, rows_second = packed
     rows = to_west.shape[1]
     count = lax.axis_size("gridy")
@@ -729,10 +727,11 @@
     rows_first, rows_second = pair(rows_first, 0), pair(rows_second, 1)
     low = jnp.concatenate([from_east[:, :CHUNK], from_west[:, :CHUNK]], axis=2)
     high = jnp.concatenate([from_east[:, rows - CHUNK :], from_west[:, rows - CHUNK :]], axis=2)
+    low, high, their_source = lax.optimization_barrier((low, high, swap(clone_source)))
     even = lax.axis_index("gridy") % 2 == 0
     sides_first = pair(jnp.where(even, high, low), 0)
     sides_second = pair(jnp.where(even, low, high), 1)
-    return from_east, from_west, rows_first, rows_second, sides_first, sides_second
+    return (from_east, from_west, rows_first, rows_second, sides_first, sides_second), their_source
 
 
 def from_all(tiles, axes):
@@ -751,8 +750,7 @@
     grid = ("gridy", "gridx")
 
     fields = (temp, salt, uvel, vvel, eta, land_mask)
-    packed, their_source = lax.optimization_barrier((pack_rims(*fields), swap(clone_source)))
-    rims = exchange_rims(packed)
+    rims, their_source = exchange_rims(pack_rims(*fields), clone_source)
     tile, kept, info = local_sums(clone_source, their_source, fields, rims, total_rows)
     tiles = from_all(jnp.broadcast_to(tile[None], (count_y * count_x,) + tile.shape), grid)
 

time: 102 us -> 74.9 us (0.73)
  waiting for transfers between devices: 38.3 us -> 13.8 us
  Pallas kernels: 25.4 us -> 24.1 us
    ppermute x4 -> x3, waiting for transfers between devices: 32.1 us -> 7.59 us  [swap(): return lax.ppermute(value, 'member', [(0, 1), (1, 0)])]
    ppermute x4 -> x3, starting transfers between devices: 5.85 us -> 3.68 us  [swap(): return lax.ppermute(value, 'member', [(0, 1), (1, 0)])]
    ppermute x2, starting transfers between devices: 3.66 us -> 5.1 us  [shift(): lax.ppermute(value, axis, [(i, (i + by) % count) for i in range(count)])]
  transfers between devices with their start and end apart: 10 -> 9, of which waited for: 5 -> 4; matrix products, arithmetic and copies ran while one was open for 1% -> 1% of each run, Pallas kernels for 9% -> 8%
where the time goes in v4:
time: 74.9 us; the launch traced here: 74.6 us
  Pallas kernels  24.1 us (32%)
  blocking collectives  19.9 us (27%)
  starting transfers between devices  14 us (19%)
  waiting for transfers between devices  13.8 us (18%)
  between operations  2.11 us (3%)
    all_to_all x2, blocking collectives, from_all(): return lax.all_to_all(tiles, axes, split_axis=0, concat_axis=0, tiled=True)  19.9 us
    pallas_call x2, Pallas kernels, advance(): pl.pallas_call(functools.partial(advance_kernel, levels, total_rows, is_f...  10.4 us
    ppermute x3, waiting for transfers between devices, swap(): return lax.ppermute(value, 'member', [(0, 1), (1, 0)])  7.59 us
    pallas_call x1, Pallas kernels, local_sums(): pl.pallas_call(functools.partial(sums_kernel, levels, total_rows), out_sh...  7.57 us
    ppermute x2, waiting for transfers between devices, shift(): lax.ppermute(value, axis, [(i, (i + by) % count) for i in range(count)])  5.32 us
    ppermute x4, starting transfers between devices, pair(): return lax.ppermute(value, 'gridy', list(enumerate(partners[which])))  5.22 us
    ppermute x2, starting transfers between devices, shift(): lax.ppermute(value, axis, [(i, (i + by) % count) for i in range(count)])  5.1 us
    ppermute x3, starting transfers between devices, swap(): return lax.ppermute(value, 'member', [(0, 1), (1, 0)])  3.68 us
  transfers between devices with their start and end apart: 9, of which 4 were waited for; matrix products, arithmetic and copies ran while one was open for 1% of the time, Pallas kernels for 8%

profile of v4, /device:TPU:0, one launch (start us, length us, event | category | flops | bytes accessed | tf_op | source)
XLA Modules:
  0.0 74.6 jit_solution(3702872502900022678)
XLA Ops:
  0.7 2.9 %pack_rims.1 = (f32[2,64,256]{2,1,0:T(8,128)}, f32[2,64,256]{2,1,0:T(8,128)}, f32[2,184,256]{2,1,0:T(8,128)}, f32[2,184,256]{2,1,0:T(8,128)}) custom-call(f32[2,4,64,256]{3,2,1,0:T(8,128)} %refs_0_.3, f32[2,4,64,256]{3,2,1,0:T(8,128)} %refs_1_.3, f32[2,4,64,256]{3,2,1,0:T(8,128)} %refs_2_.3, f32[2,4,64,256]{3,2,1,0:T(8,128)} %refs_3_.3, ...), custom_call_target="tpu_custom_call" | custom-call | tf_op jit(solution)/shard_map/pack_rims/pallas_call | solution.py:123
  3.6 5.1 %collective-permute-start.1 = (f32[2,64,256]{2,1,0:T(8,128)}, f32[2,64,256]{2,1,0:T(8,128)S(1)}, u32[]{:S(2)}, u32[]{:S(2)}) collective-permute-start(f32[2,64,256]{2,1,0:T(8,128)} %get-tuple-element.86), channel_id=1, source_target_pairs={{0,3},{1,0},{2,1},{3,2},{4,7},{5,4},{6,5},{7,6},{8,11},{9,8},{10,9... | collective-permute-start | bytes 393224 | tf_op jit(solution)/shard_map/ppermute | solution.py:713
  8.7 1.5 %collective-permute-start.3 = (s32[2]{0:T(128)S(1)}, s32[2]{0:T(128)S(1)}, u32[]{:S(2)}, u32[]{:S(2)}) collective-permute-start(s32[2]{0:T(128)S(1)} %copy-done.6), channel_id=1, source_target_pairs={{0,16},{16,0},{1,17},{17,1},{2,18},{18,2},{3,19},{19,3},{4,20},{20... | collective-permute-start | bytes 32 | tf_op jit(solution)/shard_map/ppermute | solution.py:742
  10.2 1.6 %collective-permute-start.5 = (f32[2,184,256]{2,1,0:T(8,128)}, f32[2,184,256]{2,1,0:T(8,128)S(1)}, u32[]{:S(2)}, u32[]{:S(2)}) collective-permute-start(f32[2,184,256]{2,1,0:T(8,128)} %get-tuple-element.90), channel_id=1, source_target_pairs={{0,0},{4,8},{8,4},{12,12},{1,1},{5,9},{9,5},{13,13},{2,2},{6,10},{... | collective-permute-start | bytes 1130504 | tf_op jit(solution)/shard_map/ppermute | solution.py:724
  11.8 1.1 %collective-permute-done.1.refs_6_ = f32[2,64,256]{2,1,0:T(8,128)S(1)} collective-permute-done((f32[2,64,256]{2,1,0:T(8,128)}, f32[2,64,256]{2,1,0:T(8,128)S(1)}, u32[]{:S(2)}, u32[]{:S(2)}) %collective-permute-start.1) | collective-permute-done | bytes 131104 | tf_op jit(solution)/shard_map/ppermute | solution.py:713
  12.9 4.3 %collective-permute-done.2.refs_7_ = f32[2,64,256]{2,1,0:T(8,128)S(1)} collective-permute-done((f32[2,64,256]{2,1,0:T(8,128)}, f32[2,64,256]{2,1,0:T(8,128)S(1)}, u32[]{:S(2)}, u32[]{:S(2)}) %collective-permute-start.2) | collective-permute-done | bytes 131104 | tf_op jit(solution)/shard_map/ppermute | solution.py:713
  17.2 0.0 collective-permute-done.3.theirs
  17.2 0.7 collective-permute-start.7
  17.9 2.9 %collective-permute-start.6 = (f32[2,16,512]{2,1,0:T(8,128)S(1)}, f32[2,16,512]{2,1,0:T(8,128)S(1)}, u32[]{:S(2)}, u32[]{:S(2)}) collective-permute-start(f32[2,16,512]{2,1,0:T(8,128)S(1)} %get-tuple-element.108), channel_id=1, source_target_pairs={{0,4},{4,0},{8,12},{12,8},{1,5},{5,1},{9,13},{13,9},{2,6},{6,2},{1... | collective-permute-start | bytes 196616 | tf_op jit(solution)/shard_map/ppermute | solution.py:724
  20.8 0.9 %collective-permute-done.6.refs_10_ = f32[2,16,512]{2,1,0:T(8,128)S(1)} collective-permute-done((f32[2,16,512]{2,1,0:T(8,128)S(1)}, f32[2,16,512]{2,1,0:T(8,128)S(1)}, u32[]{:S(2)}, u32[]{:S(2)}) %collective-permute-start.6) | collective-permute-done | bytes 65568 | tf_op jit(solution)/shard_map/ppermute | solution.py:724
  21.7 0.0 collective-permute-done.4.refs_8_
  21.8 7.6 %local_sums.1 = (f32[2,128]{1,0:T(2,128)S(1)}, f32[2,24,112,384]{3,2,1,0:T(8,128)S(1)}, s32[5]{0:T(128)S(1)}) custom-call(s32[2]{0:T(128)S(1)} %copy-done.6, s32[2]{0:T(128)S(1)} %collective-permute-done.3.theirs, f32[2,4,64,256]{3,2,1,0:T(8,128)S(1)} %copy-done, f32[2,4,64,256]{3,2,1,0:T(8,128)S(1)} %copy-done.1, f32[2,4,64,256]{3,2,1,0:T(8,128)S(1)} %copy-done.2, ...), custom_call_target="tpu_custom_call" | custom-call | flops 100000000 | bytes 4000000 | tf_op jit(solution)/shard_map/local_sums/pallas_call | solution.py:401
  29.4 10.8 %all_to_all.10.refs_1_ = f32[16,2,128]{2,1,0:T(2,128)S(1)} all-to-all(f32[16,2,128]{2,1,0:T(2,128)S(1)} %broadcast_in_dim.2), channel_id=1, replica_groups=mesh['member'=2,'gridy'=4,'gridx'=4] {'gridy','gridx'}, dimensions={0} | all-to-all | bytes 32768 | tf_op jit(solution)/shard_map/all_to_all | solution.py:738
  40.2 5.2 %advance.3 = (f32[17,64,256]{2,1,0:T(8,128)S(1)}, f32[64,128]{1,0:T(8,128)S(1)}) custom-call(s32[5]{0:T(128)S(1)} %get-tuple-element.93.refs_0_, f32[16,2,128]{2,1,0:T(2,128)S(1)} %all_to_all.10.refs_1_, f32[2,24,112,384]{3,2,1,0:T(8,128)S(1)} %get-tuple-element.95.refs_2_), custom_call_target="tpu_custom_call" | custom-call | flops 100000000 | bytes 4000000 | tf_op jit(solution)/shard_map/advance/pallas_call | solution.py:605
  45.3 0.6 collective-permute-start.9
  45.9 0.6 fusion.2
  47.8 15.1 %conditional.2 = (f32[17,64,256]{2,1,0:T(8,128)S(1)}, f32[2,4,64]{2,1,0:T(4,128)}, f32[2]{0:T(128)S(1)}) conditional(s32[]{:T(128)} %bitcast.1, () %tuple.24, (s32[5]{0:T(128)S(1)}, f32[16,2,128]{2,1,0:T(2,128)S(1)}, f32[2,24,112,384]{3,2,1,0:T(8,128)S(1)}, f32[64,128]{1,0:T(8,128)S(1)}) %tuple.25), branch_computations={%region_0.1_spmd, %region_1.2_spmd} | conditional | flops 100000000 | bytes 4065560 | solution.py:767
  47.8 5.3 %advance.2 = (f32[17,64,256]{2,1,0:T(8,128)S(1)}, f32[16,4,128]{2,1,0:T(4,128)S(1)}) custom-call(s32[5]{0:T(128)S(1)} %get-tuple-element.36.refs_0_, f32[16,2,128]{2,1,0:T(2,128)S(1)} %get-tuple-element.37.refs_1_, f32[2,24,112,384]{3,2,1,0:T(8,128)S(1)} %get-tuple-element.38.refs_2_, f32[64,128]{1,0:T(8,128)S(1)} %get-tuple-element.39.refs_3_), custom_call_target="tpu_custom_call" | custom-call | flops 100000000 | bytes 4000000 | tf_op jit(solution)/shard_map/cond/branch_1_fun/advance/pallas_call | solution.py:605
  53.1 9.1 %all_to_all.9.spread = f32[16,4,128]{2,1,0:T(4,128)S(1)} all-to-all(f32[16,4,128]{2,1,0:T(4,128)S(1)} %get-tuple-element.41), channel_id=1, replica_groups=mesh['member'=2,'gridy'=4,'gridx'=4] {'gridy','gridx'}, dimensions={0} | all-to-all | bytes 65536 | tf_op jit(solution)/shard_map/cond/branch_1_fun/all_to_all | solution.py:738
  62.1 0.7 finish.1
  62.9 1.6 %collective-permute-start.8 = (f32[2]{0:T(128)S(1)}, f32[2]{0:T(128)S(1)}, u32[]{:S(2)}, u32[]{:S(2)}) collective-permute-start(f32[2]{0:T(128)S(1)} %get-tuple-element.97), channel_id=1, source_target_pairs={{0,16},{16,0},{1,17},{17,1},{2,18},{18,2},{3,19},{19,3},{4,20},{20... | collective-permute-start | bytes 32 | tf_op jit(solution)/shard_map/ppermute | solution.py:742
  64.5 7.6 %collective-permute-done.8 = f32[2]{0:T(128)S(1)} collective-permute-done((f32[2]{0:T(128)S(1)}, f32[2]{0:T(128)S(1)}, u32[]{:S(2)}, u32[]{:S(2)}) %collective-permute-start.8) | collective-permute-done | bytes 40 | tf_op jit(solution)/shard_map/ppermute | solution.py:742
  72.1 2.5 %conditional.3 = ((f32[2,4,64,256]{3,2,1,0:T(8,128)}, f32[2,4,64,256]{3,2,1,0:T(8,128)}, f32[2,4,64,256]{3,2,1,0:T(8,128)}, f32[2,4,64,256]{3,2,1,0:T(8,128)}, f32[2,64,256]{2,1,0:T(8,128)}, /*index=5*/f32[2]{0:T(128)})) conditional(s32[]{:T(128)} %bitcast, (s32[5]{0:T(128)S(1)}, s32[2]{0:T(128)S(1)}, f32[2]{0:T(128)S(1)}, f32[2]{0:T(128)S(1)}, ...), branch_computations={%region_2.3_spmd, %region_3.4_spmd} | conditional | bytes 4456496 | solution.py:777
  72.1 2.5 %pick.2 = (f32[2,4,64,256]{3,2,1,0:T(8,128)}, f32[2,4,64,256]{3,2,1,0:T(8,128)}, f32[2,4,64,256]{3,2,1,0:T(8,128)}, f32[2,4,64,256]{3,2,1,0:T(8,128)}, f32[2,64,256]{2,1,0:T(8,128)}, /*index=5*/f32[2]{0:T(128)}) custom-call(s32[5]{0:T(128)S(1)} %get-tuple-element.44.choice, s32[2]{0:T(128)S(1)} %get-tuple-element.45.source, f32[2]{0:T(128)S(1)} %get-tuple-element.46.score, ...), custom_call_target="tpu_custom_call" | custom-call | tf_op jit(solution)/shard_map/cond/branch_0_fun/pick/pallas_call | solution.py:700
  (24 shorter events, 0.1 us)
Async XLA Ops:
  0.6 21.1 %copy-start.5 = (s32[64,256]{1,0:T(8,128)S(1)}, s32[64,256]{1,0:T(8,128)}, u32[]{:S(2)}) copy-start(s32[64,256]{1,0:T(8,128)} %refs_5_.3) | copy-start | bytes 196612
  0.6 21.1 %copy-start.4 = (f32[2,64,256]{2,1,0:T(8,128)S(1)}, f32[2,64,256]{2,1,0:T(8,128)}, u32[]{:S(2)}) copy-start(f32[2,64,256]{2,1,0:T(8,128)} %refs_4_.3) | copy-start | bytes 393220
  0.7 21.1 %copy-start.3 = (f32[2,4,64,256]{3,2,1,0:T(8,128)S(1)}, f32[2,4,64,256]{3,2,1,0:T(8,128)}, u32[]{:S(2)}) copy-start(f32[2,4,64,256]{3,2,1,0:T(8,128)} %refs_3_.3) | copy-start | bytes 1572868
  0.7 21.1 %copy-start.2 = (f32[2,4,64,256]{3,2,1,0:T(8,128)S(1)}, f32[2,4,64,256]{3,2,1,0:T(8,128)}, u32[]{:S(2)}) copy-start(f32[2,4,64,256]{3,2,1,0:T(8,128)} %refs_2_.3) | copy-start | bytes 1572868
  0.7 21.1 %copy-start.1 = (f32[2,4,64,256]{3,2,1,0:T(8,128)S(1)}, f32[2,4,64,256]{3,2,1,0:T(8,128)}, u32[]{:S(2)}) copy-start(f32[2,4,64,256]{3,2,1,0:T(8,128)} %refs_1_.3) | copy-start | bytes 1572868
  0.7 21.1 %copy-start = (f32[2,4,64,256]{3,2,1,0:T(8,128)S(1)}, f32[2,4,64,256]{3,2,1,0:T(8,128)}, u32[]{:S(2)}) copy-start(f32[2,4,64,256]{3,2,1,0:T(8,128)} %refs_0_.3) | copy-start | bytes 1572868
  0.7 8.0 %copy-start.6 = (s32[2]{0:T(128)S(1)}, s32[2]{0:T(128)}, u32[]{:S(2)}) copy-start(s32[2]{0:T(128)} %source.1) | copy-start | bytes 28
  3.6 9.3 %collective-permute-start.1 = (f32[2,64,256]{2,1,0:T(8,128)}, f32[2,64,256]{2,1,0:T(8,128)S(1)}, u32[]{:S(2)}, u32[]{:S(2)}) collective-permute-start(f32[2,64,256]{2,1,0:T(8,128)} %get-tuple-element.86), channel_id=1, source_target_pairs={{0,3},{1,0},{2,1},{3,2},{4,7},{5,4},{6,5},{7,6},{8,11},{9,8},{10,9... | collective-permute-start | bytes 393224 | tf_op jit(solution)/shard_map/ppermute | solution.py:713
  8.7 8.5 %collective-permute-start.3 = (s32[2]{0:T(128)S(1)}, s32[2]{0:T(128)S(1)}, u32[]{:S(2)}, u32[]{:S(2)}) collective-permute-start(s32[2]{0:T(128)S(1)} %copy-done.6), channel_id=1, source_target_pairs={{0,16},{16,0},{1,17},{17,1},{2,18},{18,2},{3,19},{19,3},{4,20},{20... | collective-permute-start | bytes 32 | tf_op jit(solution)/shard_map/ppermute | solution.py:742
  10.2 7.0 %collective-permute-start.2 = (f32[2,64,256]{2,1,0:T(8,128)}, f32[2,64,256]{2,1,0:T(8,128)S(1)}, u32[]{:S(2)}, u32[]{:S(2)}) collective-permute-start(f32[2,64,256]{2,1,0:T(8,128)} %get-tuple-element.87), channel_id=1, source_target_pairs={{0,1},{1,2},{2,3},{3,0},{4,5},{5,6},{6,7},{7,4},{8,9},{9,10},{10,1... | collective-permute-start | bytes 393224 | tf_op jit(solution)/shard_map/ppermute | solution.py:713
  10.2 11.5 %collective-permute-start.4 = (f32[2,184,256]{2,1,0:T(8,128)}, f32[2,184,256]{2,1,0:T(8,128)S(1)}, u32[]{:S(2)}, u32[]{:S(2)}) collective-permute-start(f32[2,184,256]{2,1,0:T(8,128)} %get-tuple-element.89), channel_id=1, source_target_pairs={{0,4},{4,0},{8,12},{12,8},{1,5},{5,1},{9,13},{13,9},{2,6},{6,2},{1... | collective-permute-start | bytes 1130504 | tf_op jit(solution)/shard_map/ppermute | solution.py:724
  10.2 11.5 %collective-permute-start.5 = (f32[2,184,256]{2,1,0:T(8,128)}, f32[2,184,256]{2,1,0:T(8,128)S(1)}, u32[]{:S(2)}, u32[]{:S(2)}) collective-permute-start(f32[2,184,256]{2,1,0:T(8,128)} %get-tuple-element.90), channel_id=1, source_target_pairs={{0,0},{4,8},{8,4},{12,12},{1,1},{5,9},{9,5},{13,13},{2,2},{6,10},{... | collective-permute-start | bytes 1130504 | tf_op jit(solution)/shard_map/ppermute | solution.py:724
  17.2 3.6 %collective-permute-start.7 = (f32[2,16,512]{2,1,0:T(8,128)S(1)}, f32[2,16,512]{2,1,0:T(8,128)S(1)}, u32[]{:S(2)}, u32[]{:S(2)}) collective-permute-start(f32[2,16,512]{2,1,0:T(8,128)S(1)} %get-tuple-element.107), channel_id=1, source_target_pairs={{0,0},{4,8},{8,4},{12,12},{1,1},{5,9},{9,5},{13,13},{2,2},{6,10},{... | collective-permute-start | bytes 196616 | tf_op jit(solution)/shard_map/ppermute | solution.py:724
  17.9 3.8 %collective-permute-start.6 = (f32[2,16,512]{2,1,0:T(8,128)S(1)}, f32[2,16,512]{2,1,0:T(8,128)S(1)}, u32[]{:S(2)}, u32[]{:S(2)}) collective-permute-start(f32[2,16,512]{2,1,0:T(8,128)S(1)} %get-tuple-element.108), channel_id=1, source_target_pairs={{0,4},{4,0},{8,12},{12,8},{1,5},{5,1},{9,13},{13,9},{2,6},{6,2},{1... | collective-permute-start | bytes 196616 | tf_op jit(solution)/shard_map/ppermute | solution.py:724
  45.3 26.7 %collective-permute-start.9 = (f32[17,64,256]{2,1,0:T(8,128)S(1)}, f32[17,64,256]{2,1,0:T(8,128)S(1)}, u32[]{:S(2)}, u32[]{:S(2)}) collective-permute-start(f32[17,64,256]{2,1,0:T(8,128)S(1)} %get-tuple-element.98), channel_id=1, source_target_pairs={{0,16},{16,0},{1,17},{17,1},{2,18},{18,2},{3,19},{19,3},{4,20},{20... | collective-permute-start | bytes 3342344 | tf_op jit(solution)/shard_map/ppermute | solution.py:742
  62.9 9.2 %collective-permute-start.8 = (f32[2]{0:T(128)S(1)}, f32[2]{0:T(128)S(1)}, u32[]{:S(2)}, u32[]{:S(2)}) collective-permute-start(f32[2]{0:T(128)S(1)} %get-tuple-element.97), channel_id=1, source_target_pairs={{0,16},{16,0},{1,17},{17,1},{2,18},{18,2},{3,19},{19,3},{4,20},{20... | collective-permute-start | bytes 32 | tf_op jit(solution)/shard_map/ppermute | solution.py:742

commit v5 on v4

--- a/solution.py
+++ b/solution.py
@@ -30,7 +30,7 @@
 TOP = 24
 CHUNK = 16
 CHUNK_2D = 8
-CHUNK_3D = 32
+CHUNK_3D = 64
 LANE = 128
 PER_GROUP = 11
 PAIRS = [(a, b) for a in range(4) for b in range(a, 4)]
@@ -70,18 +70,17 @@
     return per_member
 
 
-def pack_kernel(levels, *refs):
-    fields, (to_west, to_east, rows_first, rows_second), (held, mask, sems) = refs[:6], refs[6:10], refs[10:]
+def pack_columns_kernel(levels, *refs):
+    fields, (to_west, to_east), (held, mask, sems) = refs[:6], refs[6:8], refs[8:]
     members, _, rows, cols = held.shape
     planes = 4 * levels + 2
     copies = fetches(fields, lambda m, at: held.at[m, at], mask, sems, levels)
     lane = lanes_like((rows, LANE))
-    even = lax.broadcasted_iota(jnp.int32, (WIDE, cols), 0) * 0 + lax.rem(lax.axis_index("gridy"), 2) == 0
     for m in range(members):
         for copy in copies[m]:
             copy.wait()
-        west_parts = [None] * groups_of(planes)
-        east_parts = [None] * groups_of(planes)
+        west_parts = [jnp.zeros((rows, LANE), jnp.float32)] * groups_of(planes)
+        east_parts = list(west_parts)
         for plane in range(planes):
             value = held[m, plane] if plane < planes - 1 else mask[...].astype(jnp.float32)
             group, _, start = rim_place(plane)
@@ -89,18 +88,30 @@
             both = pltpu.roll(both, start, 1)
             is_west = (lane >= start) & (lane < start + WIDE)
             is_east = (lane >= start - WIDE) & (lane < start)
-            zero = jnp.zeros_like(both)
-            west_parts[group] = jnp.where(is_west, both, zero if west_parts[group] is None else west_parts[group])
-            east_parts[group] = jnp.where(is_east, both, zero if east_parts[group] is None else east_parts[group])
-            low, high = value[:WIDE], value[rows - WIDE :]
-            rows_first[m, plane * WIDE : (plane + 1) * WIDE, :] = jnp.where(even, high, low)
-            rows_second[m, plane * WIDE : (plane + 1) * WIDE, :] = jnp.where(even, low, high)
+            west_parts[group] = jnp.where(is_west, both, west_parts[group])
+            east_parts[group] = jnp.where(is_east, both, east_parts[group])
         for group in range(groups_of(planes)):
             where = slice(group * LANE, (group + 1) * LANE)
             to_west[m, :, where] = west_parts[group]
             to_east[m, :, where] = east_parts[group]
 
 
+def pack_rows_kernel(levels, *refs):
+    fields, (rows_first, rows_second), (held, mask, sems) = refs[:6], refs[6:8], refs[8:]
+    members, _, rows, cols = held.shape
+    planes = 4 * levels + 2
+    copies = fetches(fields, lambda m, at: held.at[m, at], mask, sems, levels)
+    even = lax.broadcasted_iota(jnp.int32, (WIDE, cols), 0) * 0 + lax.rem(lax.axis_index("gridy"), 2) == 0
+    for m in range(members):
+        for copy in copies[m]:
+            copy.wait()
+        for plane in range(planes):
+            value = held[m, plane] if plane < planes - 1 else mask[...].astype(jnp.float32)
+            low, high = value[:WIDE], value[rows - WIDE :]
+            rows_first[m, plane * WIDE : (plane + 1) * WIDE, :] = jnp.where(even, high, low)
+            rows_second[m, plane * WIDE : (plane + 1) * WIDE, :] = jnp.where(even, low, high)
+
+
 def whole(count):
     return [pl.BlockSpec(memory_space=pltpu.VMEM)] * count
 
@@ -113,26 +124,34 @@
     return [pl.BlockSpec(memory_space=pltpu.SMEM)] * count
 
 
-def pack_rims(temp, salt, uvel, vvel, eta, mask):
-    members, levels, rows, cols = temp.shape
-    planes = 4 * levels + 2
-    wide = groups_of(planes) * LANE
-    row_pack = -(-planes * WIDE // 8) * 8
-    side = jax.ShapeDtypeStruct((members, rows, wide), jnp.float32)
-    line = jax.ShapeDtypeStruct((members, row_pack, cols), jnp.float32)
+def pack(kernel, shape, fields, name):
+    members, levels, rows, cols = fields[0].shape
     return pl.pallas_call(
-        functools.partial(pack_kernel, levels),
-        out_shape=(side, side, line, line),
+        functools.partial(kernel, levels),
+        out_shape=(jax.ShapeDtypeStruct(shape, jnp.float32),) * 2,
         in_specs=in_hbm(6),
-        out_specs=tuple(whole(4)),
+        out_specs=tuple(whole(2)),
         scratch_shapes=[
-            pltpu.VMEM((members, planes - 1, rows, cols), jnp.float32),
+            pltpu.VMEM((members, 4 * levels + 1, rows, cols), jnp.float32),
             pltpu.VMEM((rows, cols), jnp.int32),
             pltpu.SemaphoreType.DMA((members, 6)),
         ],
         compiler_params=pltpu.CompilerParams(vmem_limit_bytes=WHOLE_VMEM),
-        name="pack_rims",
-    )(temp, salt, uvel, vvel, eta, mask)
+        cost_estimate=pl.CostEstimate(flops=10**6, bytes_accessed=10**6, transcendentals=0),
+        name=name,
+    )(*fields)
+
+
+def pack_columns(fields):
+    members, levels, rows, _ = fields[0].shape
+    wide = groups_of(4 * levels + 2) * LANE
+    return pack(pack_columns_kernel, (members, rows, wide), fields, "pack_columns")
+
+
+def pack_rows(fields):
+    members, levels, _, cols = fields[0].shape
+    height = -(-(4 * levels + 2) * WIDE // 8) * 8
+    return pack(pack_rows_kernel, (members, height, cols), fields, "pack_rows")
 
 
 def east_west(value):
@@ -713,8 +732,8 @@
     return lax.ppermute(value, axis, [(i, (i + by) % count) for i in range(count)])
 
 
-def exchange_rims(packed, clone_source):
-    to_west, to_east, rows_first, rows_second = packed
+def exchange_rims(fields, clone_source):
+    to_west, to_east = pack_columns(fields)
     rows = to_west.shape[1]
     count = lax.axis_size("gridy")
     assert count % 2 == 0
@@ -724,6 +743,7 @@
         return lax.ppermute(value, "gridy", list(enumerate(partners[which])))
 
     from_east, from_west = shift(to_west, "gridx", -1), shift(to_east, "gridx", 1)
+    rows_first, rows_second = pack_rows(fields)
     rows_first, rows_second = pair(rows_first, 0), pair(rows_second, 1)
     low = jnp.concatenate([from_east[:, :CHUNK], from_west[:, :CHUNK]], axis=2)
     high = jnp.concatenate([from_east[:, rows - CHUNK :], from_west[:, rows - CHUNK :]], axis=2)
@@ -750,7 +770,7 @@
     grid = ("gridy", "gridx")
 
     fields = (temp, salt, uvel, vvel, eta, land_mask)
-    rims, their_source = exchange_rims(pack_rims(*fields), clone_source)
+    rims, their_source = exchange_rims(fields, clone_source)
     tile, kept, info = local_sums(clone_source, their_source, fields, rims, total_rows)
     tiles = from_all(jnp.broadcast_to(tile[None], (count_y * count_x,) + tile.shape), grid)
 

time: 74.9 us -> 77.6 us (1.036)
  waiting for transfers between devices: 13.8 us -> 10.6 us
  Pallas kernels: 24.1 us -> 27.3 us
  blocking collectives: 19.9 us -> 22.4 us
    ppermute x2, waiting for transfers between devices: 5.32 us -> 2.48 us  [shift(): lax.ppermute(value, axis, [(i, (i + by) % count) for i in range(count)])]
    all_to_all x2, blocking collectives: 19.9 us -> 22.4 us  [from_all(): return lax.all_to_all(tiles, axes, split_axis=0, concat_axis=0, tiled=True)]
    pallas_call x1 -> x2, Pallas kernels: 2.86 us -> 5.33 us  [pack(): pl.pallas_call(functools.partial(kernel, levels), out_shape=(jax.ShapeDty...]
  transfers between devices with their start and end apart: 9 -> 9, of which waited for: 4 -> 3; matrix products, arithmetic and copies ran while one was open for 1% -> 1% of each run, Pallas kernels for 8% -> 12%
where the time goes in v5:
time: 77.6 us; the launch traced here: 77.3 us
  Pallas kernels  27.3 us (35%)
  blocking collectives  22.4 us (29%)
  starting transfers between devices  14.1 us (18%)
  waiting for transfers between devices  10.6 us (14%)
  between operations  2.11 us (3%)
    all_to_all x2, blocking collectives, from_all(): return lax.all_to_all(tiles, axes, split_axis=0, concat_axis=0, tiled=True)  22.4 us
    pallas_call x2, Pallas kernels, advance(): pl.pallas_call(functools.partial(advance_kernel, levels, total_rows, is_f...  11.1 us
    pallas_call x1, Pallas kernels, local_sums(): pl.pallas_call(functools.partial(sums_kernel, levels, total_rows), out_sh...  7.63 us
    ppermute x3, waiting for transfers between devices, swap(): return lax.ppermute(value, 'member', [(0, 1), (1, 0)])  7.21 us
    pallas_call x2, Pallas kernels, pack(): pl.pallas_call(functools.partial(kernel, levels), out_shape=(jax.ShapeDty...  5.33 us
    ppermute x4, starting transfers between devices, pair(): return lax.ppermute(value, 'gridy', list(enumerate(partners[which])))  5.3 us
    ppermute x2, starting transfers between devices, shift(): lax.ppermute(value, axis, [(i, (i + by) % count) for i in range(count)])  5.16 us
    ppermute x3, starting transfers between devices, swap(): return lax.ppermute(value, 'member', [(0, 1), (1, 0)])  3.68 us
  transfers between devices with their start and end apart: 9, of which 3 were waited for; matrix products, arithmetic and copies ran while one was open for 1% of the time, Pallas kernels for 12%

profile of v5, /device:TPU:0, one launch (start us, length us, event | category | flops | bytes accessed | tf_op | source)
XLA Modules:
  0.0 77.3 jit_solution(12603995303481434860)
XLA Ops:
  0.6 2.6 %pack_columns.1 = (f32[2,64,256]{2,1,0:T(8,128)}, f32[2,64,256]{2,1,0:T(8,128)}) custom-call(f32[2,4,64,256]{3,2,1,0:T(8,128)} %refs_0_.5, f32[2,4,64,256]{3,2,1,0:T(8,128)} %refs_1_.5, f32[2,4,64,256]{3,2,1,0:T(8,128)} %refs_2_.5, f32[2,4,64,256]{3,2,1,0:T(8,128)} %refs_3_.5, f32[2,64,256]{2,1,0:T(8,128)} %refs_4_.5, s32[64,256]{1,0:T(8,128)} %refs_5_.5), custom_call_target="tpu_custom_call" | custom-call | flops 1000000 | bytes 1000000 | tf_op jit(solution)/shard_map/pack_columns/pallas_call | solution.py:129
  3.2 5.1 %collective-permute-start.1 = (f32[2,64,256]{2,1,0:T(8,128)}, f32[2,64,256]{2,1,0:T(8,128)S(1)}, u32[]{:S(2)}, u32[]{:S(2)}) collective-permute-start(f32[2,64,256]{2,1,0:T(8,128)} %get-tuple-element.86), channel_id=1, source_target_pairs={{0,3},{1,0},{2,1},{3,2},{4,7},{5,4},{6,5},{7,6},{8,11},{9,8},{10,9... | collective-permute-start | bytes 393224 | tf_op jit(solution)/shard_map/ppermute | solution.py:732
  8.3 1.5 %collective-permute-start.3 = (s32[2]{0:T(128)S(1)}, s32[2]{0:T(128)S(1)}, u32[]{:S(2)}, u32[]{:S(2)}) collective-permute-start(s32[2]{0:T(128)S(1)} %copy-done.6), channel_id=1, source_target_pairs={{0,16},{16,0},{1,17},{17,1},{2,18},{18,2},{3,19},{19,3},{4,20},{20... | collective-permute-start | bytes 32 | tf_op jit(solution)/shard_map/ppermute | solution.py:762
  9.9 0.1 collective-permute-start.2
  10.0 2.7 %pack_rows.1 = (f32[2,184,256]{2,1,0:T(8,128)}, f32[2,184,256]{2,1,0:T(8,128)}) custom-call(f32[2,4,64,256]{3,2,1,0:T(8,128)} %refs_0_.5, f32[2,4,64,256]{3,2,1,0:T(8,128)} %refs_1_.5, f32[2,4,64,256]{3,2,1,0:T(8,128)} %refs_2_.5, f32[2,4,64,256]{3,2,1,0:T(8,128)} %refs_3_.5, f32[2,64,256]{2,1,0:T(8,128)} %refs_4_.5, s32[64,256]{1,0:T(8,128)} %refs_5_.5), custom_call_target="tpu_custom_call" | custom-call | flops 1000000 | bytes 1000000 | tf_op jit(solution)/shard_map/pack_rows/pallas_call | solution.py:129
  12.7 0.1 collective-permute-start.4
  12.8 1.6 %collective-permute-start.5 = (f32[2,184,256]{2,1,0:T(8,128)}, f32[2,184,256]{2,1,0:T(8,128)S(1)}, u32[]{:S(2)}, u32[]{:S(2)}) collective-permute-start(f32[2,184,256]{2,1,0:T(8,128)} %get-tuple-element.90), channel_id=1, source_target_pairs={{0,0},{4,8},{8,4},{12,12},{1,1},{5,9},{9,5},{13,13},{2,2},{6,10},{... | collective-permute-start | bytes 1130504 | tf_op jit(solution)/shard_map/ppermute | solution.py:743
  14.5 2.5 %collective-permute-done.2.refs_7_ = f32[2,64,256]{2,1,0:T(8,128)S(1)} collective-permute-done((f32[2,64,256]{2,1,0:T(8,128)}, f32[2,64,256]{2,1,0:T(8,128)S(1)}, u32[]{:S(2)}, u32[]{:S(2)}) %collective-permute-start.2) | collective-permute-done | bytes 131104 | tf_op jit(solution)/shard_map/ppermute | solution.py:732
  17.0 0.7 collective-permute-start.7
  17.6 2.9 %collective-permute-start.6 = (f32[2,16,512]{2,1,0:T(8,128)S(1)}, f32[2,16,512]{2,1,0:T(8,128)S(1)}, u32[]{:S(2)}, u32[]{:S(2)}) collective-permute-start(f32[2,16,512]{2,1,0:T(8,128)S(1)} %get-tuple-element.108), channel_id=1, source_target_pairs={{0,4},{4,0},{8,12},{12,8},{1,5},{5,1},{9,13},{13,9},{2,6},{6,2},{1... | collective-permute-start | bytes 196616 | tf_op jit(solution)/shard_map/ppermute | solution.py:743
  20.6 0.9 %collective-permute-done.6.refs_10_ = f32[2,16,512]{2,1,0:T(8,128)S(1)} collective-permute-done((f32[2,16,512]{2,1,0:T(8,128)S(1)}, f32[2,16,512]{2,1,0:T(8,128)S(1)}, u32[]{:S(2)}, u32[]{:S(2)}) %collective-permute-start.6) | collective-permute-done | bytes 65568 | tf_op jit(solution)/shard_map/ppermute | solution.py:743
  21.5 7.6 %local_sums.1 = (f32[2,128]{1,0:T(2,128)S(1)}, f32[2,24,112,384]{3,2,1,0:T(8,128)S(1)}, s32[5]{0:T(128)S(1)}) custom-call(s32[2]{0:T(128)S(1)} %copy-done.6, s32[2]{0:T(128)S(1)} %collective-permute-done.3.theirs, f32[2,4,64,256]{3,2,1,0:T(8,128)S(1)} %copy-done, f32[2,4,64,256]{3,2,1,0:T(8,128)S(1)} %copy-done.1, f32[2,4,64,256]{3,2,1,0:T(8,128)S(1)} %copy-done.2, ...), custom_call_target="tpu_custom_call" | custom-call | flops 100000000 | bytes 4000000 | tf_op jit(solution)/shard_map/local_sums/pallas_call | solution.py:420
  29.2 13.4 %all_to_all.10.refs_1_ = f32[16,2,128]{2,1,0:T(2,128)S(1)} all-to-all(f32[16,2,128]{2,1,0:T(2,128)S(1)} %broadcast_in_dim.2), channel_id=1, replica_groups=mesh['member'=2,'gridy'=4,'gridx'=4] {'gridy','gridx'}, dimensions={0} | all-to-all | bytes 32768 | tf_op jit(solution)/shard_map/all_to_all | solution.py:758
  42.6 5.5 %advance.3 = (f32[17,64,256]{2,1,0:T(8,128)S(1)}, f32[64,128]{1,0:T(8,128)S(1)}) custom-call(s32[5]{0:T(128)S(1)} %get-tuple-element.93.refs_0_, f32[16,2,128]{2,1,0:T(2,128)S(1)} %all_to_all.10.refs_1_, f32[2,24,112,384]{3,2,1,0:T(8,128)S(1)} %get-tuple-element.95.refs_2_), custom_call_target="tpu_custom_call" | custom-call | flops 100000000 | bytes 4000000 | tf_op jit(solution)/shard_map/advance/pallas_call | solution.py:624
  48.0 0.6 collective-permute-start.9
  48.6 0.6 fusion.2
  50.5 15.5 %conditional.2 = (f32[17,64,256]{2,1,0:T(8,128)S(1)}, f32[2,4,64]{2,1,0:T(4,128)}, f32[2]{0:T(128)S(1)}) conditional(s32[]{:T(128)} %bitcast.1, () %tuple.24, (s32[5]{0:T(128)S(1)}, f32[16,2,128]{2,1,0:T(2,128)S(1)}, f32[2,24,112,384]{3,2,1,0:T(8,128)S(1)}, f32[64,128]{1,0:T(8,128)S(1)}) %tuple.25), branch_computations={%region_0.1_spmd, %region_1.2_spmd} | conditional | flops 100000000 | bytes 4065560 | solution.py:787
  50.5 5.6 %advance.2 = (f32[17,64,256]{2,1,0:T(8,128)S(1)}, f32[16,4,128]{2,1,0:T(4,128)S(1)}) custom-call(s32[5]{0:T(128)S(1)} %get-tuple-element.36.refs_0_, f32[16,2,128]{2,1,0:T(2,128)S(1)} %get-tuple-element.37.refs_1_, f32[2,24,112,384]{3,2,1,0:T(8,128)S(1)} %get-tuple-element.38.refs_2_, f32[64,128]{1,0:T(8,128)S(1)} %get-tuple-element.39.refs_3_), custom_call_target="tpu_custom_call" | custom-call | flops 100000000 | bytes 4000000 | tf_op jit(solution)/shard_map/cond/branch_1_fun/advance/pallas_call | solution.py:624
  56.2 9.1 %all_to_all.9.spread = f32[16,4,128]{2,1,0:T(4,128)S(1)} all-to-all(f32[16,4,128]{2,1,0:T(4,128)S(1)} %get-tuple-element.41), channel_id=1, replica_groups=mesh['member'=2,'gridy'=4,'gridx'=4] {'gridy','gridx'}, dimensions={0} | all-to-all | bytes 65536 | tf_op jit(solution)/shard_map/cond/branch_1_fun/all_to_all | solution.py:758
  65.2 0.7 finish.1
  66.0 1.6 %collective-permute-start.8 = (f32[2]{0:T(128)S(1)}, f32[2]{0:T(128)S(1)}, u32[]{:S(2)}, u32[]{:S(2)}) collective-permute-start(f32[2]{0:T(128)S(1)} %get-tuple-element.97), channel_id=1, source_target_pairs={{0,16},{16,0},{1,17},{17,1},{2,18},{18,2},{3,19},{19,3},{4,20},{20... | collective-permute-start | bytes 32 | tf_op jit(solution)/shard_map/ppermute | solution.py:762
  67.5 7.2 %collective-permute-done.8 = f32[2]{0:T(128)S(1)} collective-permute-done((f32[2]{0:T(128)S(1)}, f32[2]{0:T(128)S(1)}, u32[]{:S(2)}, u32[]{:S(2)}) %collective-permute-start.8) | collective-permute-done | bytes 40 | tf_op jit(solution)/shard_map/ppermute | solution.py:762
  74.7 2.5 %conditional.3 = ((f32[2,4,64,256]{3,2,1,0:T(8,128)}, f32[2,4,64,256]{3,2,1,0:T(8,128)}, f32[2,4,64,256]{3,2,1,0:T(8,128)}, f32[2,4,64,256]{3,2,1,0:T(8,128)}, f32[2,64,256]{2,1,0:T(8,128)}, /*index=5*/f32[2]{0:T(128)})) conditional(s32[]{:T(128)} %bitcast, (s32[5]{0:T(128)S(1)}, s32[2]{0:T(128)S(1)}, f32[2]{0:T(128)S(1)}, f32[2]{0:T(128)S(1)}, ...), branch_computations={%region_2.3_spmd, %region_3.4_spmd} | conditional | bytes 4456496 | solution.py:797
  74.7 2.5 %pick.2 = (f32[2,4,64,256]{3,2,1,0:T(8,128)}, f32[2,4,64,256]{3,2,1,0:T(8,128)}, f32[2,4,64,256]{3,2,1,0:T(8,128)}, f32[2,4,64,256]{3,2,1,0:T(8,128)}, f32[2,64,256]{2,1,0:T(8,128)}, /*index=5*/f32[2]{0:T(128)}) custom-call(s32[5]{0:T(128)S(1)} %get-tuple-element.44.choice, s32[2]{0:T(128)S(1)} %get-tuple-element.45.source, f32[2]{0:T(128)S(1)} %get-tuple-element.46.score, ...), custom_call_target="tpu_custom_call" | custom-call | tf_op jit(solution)/shard_map/cond/branch_0_fun/pick/pallas_call | solution.py:719
  (25 shorter events, 0.1 us)
Async XLA Ops:
  0.6 7.7 %copy-start.6 = (s32[2]{0:T(128)S(1)}, s32[2]{0:T(128)}, u32[]{:S(2)}) copy-start(s32[2]{0:T(128)} %source.1) | copy-start | bytes 28
  3.2 11.2 %collective-permute-start.1 = (f32[2,64,256]{2,1,0:T(8,128)}, f32[2,64,256]{2,1,0:T(8,128)S(1)}, u32[]{:S(2)}, u32[]{:S(2)}) collective-permute-start(f32[2,64,256]{2,1,0:T(8,128)} %get-tuple-element.86), channel_id=1, source_target_pairs={{0,3},{1,0},{2,1},{3,2},{4,7},{5,4},{6,5},{7,6},{8,11},{9,8},{10,9... | collective-permute-start | bytes 393224 | tf_op jit(solution)/shard_map/ppermute | solution.py:732
  8.3 8.6 %collective-permute-start.3 = (s32[2]{0:T(128)S(1)}, s32[2]{0:T(128)S(1)}, u32[]{:S(2)}, u32[]{:S(2)}) collective-permute-start(s32[2]{0:T(128)S(1)} %copy-done.6), channel_id=1, source_target_pairs={{0,16},{16,0},{1,17},{17,1},{2,18},{18,2},{3,19},{19,3},{4,20},{20... | collective-permute-start | bytes 32 | tf_op jit(solution)/shard_map/ppermute | solution.py:762
  9.9 11.6 %copy-start = (f32[2,4,64,256]{3,2,1,0:T(8,128)S(1)}, f32[2,4,64,256]{3,2,1,0:T(8,128)}, u32[]{:S(2)}) copy-start(f32[2,4,64,256]{3,2,1,0:T(8,128)} %refs_0_.5) | copy-start | bytes 1572868
  9.9 11.6 %copy-start.1 = (f32[2,4,64,256]{3,2,1,0:T(8,128)S(1)}, f32[2,4,64,256]{3,2,1,0:T(8,128)}, u32[]{:S(2)}) copy-start(f32[2,4,64,256]{3,2,1,0:T(8,128)} %refs_1_.5) | copy-start | bytes 1572868
  9.9 11.6 %copy-start.2 = (f32[2,4,64,256]{3,2,1,0:T(8,128)S(1)}, f32[2,4,64,256]{3,2,1,0:T(8,128)}, u32[]{:S(2)}) copy-start(f32[2,4,64,256]{3,2,1,0:T(8,128)} %refs_2_.5) | copy-start | bytes 1572868
  9.9 11.6 %copy-start.3 = (f32[2,4,64,256]{3,2,1,0:T(8,128)S(1)}, f32[2,4,64,256]{3,2,1,0:T(8,128)}, u32[]{:S(2)}) copy-start(f32[2,4,64,256]{3,2,1,0:T(8,128)} %refs_3_.5) | copy-start | bytes 1572868
  9.9 11.6 %copy-start.4 = (f32[2,64,256]{2,1,0:T(8,128)S(1)}, f32[2,64,256]{2,1,0:T(8,128)}, u32[]{:S(2)}) copy-start(f32[2,64,256]{2,1,0:T(8,128)} %refs_4_.5) | copy-start | bytes 393220
  9.9 11.6 %copy-start.5 = (s32[64,256]{1,0:T(8,128)S(1)}, s32[64,256]{1,0:T(8,128)}, u32[]{:S(2)}) copy-start(s32[64,256]{1,0:T(8,128)} %refs_5_.5) | copy-start | bytes 196612
  9.9 7.0 %collective-permute-start.2 = (f32[2,64,256]{2,1,0:T(8,128)}, f32[2,64,256]{2,1,0:T(8,128)S(1)}, u32[]{:S(2)}, u32[]{:S(2)}) collective-permute-start(f32[2,64,256]{2,1,0:T(8,128)} %get-tuple-element.87), channel_id=1, source_target_pairs={{0,1},{1,2},{2,3},{3,0},{4,5},{5,6},{6,7},{7,4},{8,9},{9,10},{10,1... | collective-permute-start | bytes 393224 | tf_op jit(solution)/shard_map/ppermute | solution.py:732
  12.7 8.8 %collective-permute-start.4 = (f32[2,184,256]{2,1,0:T(8,128)}, f32[2,184,256]{2,1,0:T(8,128)S(1)}, u32[]{:S(2)}, u32[]{:S(2)}) collective-permute-start(f32[2,184,256]{2,1,0:T(8,128)} %get-tuple-element.89), channel_id=1, source_target_pairs={{0,4},{4,0},{8,12},{12,8},{1,5},{5,1},{9,13},{13,9},{2,6},{6,2},{1... | collective-permute-start | bytes 1130504 | tf_op jit(solution)/shard_map/ppermute | solution.py:743
  12.8 8.7 %collective-permute-start.5 = (f32[2,184,256]{2,1,0:T(8,128)}, f32[2,184,256]{2,1,0:T(8,128)S(1)}, u32[]{:S(2)}, u32[]{:S(2)}) collective-permute-start(f32[2,184,256]{2,1,0:T(8,128)} %get-tuple-element.90), channel_id=1, source_target_pairs={{0,0},{4,8},{8,4},{12,12},{1,1},{5,9},{9,5},{13,13},{2,2},{6,10},{... | collective-permute-start | bytes 1130504 | tf_op jit(solution)/shard_map/ppermute | solution.py:743
  17.0 3.6 %collective-permute-start.7 = (f32[2,16,512]{2,1,0:T(8,128)S(1)}, f32[2,16,512]{2,1,0:T(8,128)S(1)}, u32[]{:S(2)}, u32[]{:S(2)}) collective-permute-start(f32[2,16,512]{2,1,0:T(8,128)S(1)} %get-tuple-element.107), channel_id=1, source_target_pairs={{0,0},{4,8},{8,4},{12,12},{1,1},{5,9},{9,5},{13,13},{2,2},{6,10},{... | collective-permute-start | bytes 196616 | tf_op jit(solution)/shard_map/ppermute | solution.py:743
  17.6 3.8 %collective-permute-start.6 = (f32[2,16,512]{2,1,0:T(8,128)S(1)}, f32[2,16,512]{2,1,0:T(8,128)S(1)}, u32[]{:S(2)}, u32[]{:S(2)}) collective-permute-start(f32[2,16,512]{2,1,0:T(8,128)S(1)} %get-tuple-element.108), channel_id=1, source_target_pairs={{0,4},{4,0},{8,12},{12,8},{1,5},{5,1},{9,13},{13,9},{2,6},{6,2},{1... | collective-permute-start | bytes 196616 | tf_op jit(solution)/shard_map/ppermute | solution.py:743
  48.0 26.7 %collective-permute-start.9 = (f32[17,64,256]{2,1,0:T(8,128)S(1)}, f32[17,64,256]{2,1,0:T(8,128)S(1)}, u32[]{:S(2)}, u32[]{:S(2)}) collective-permute-start(f32[17,64,256]{2,1,0:T(8,128)S(1)} %get-tuple-element.98), channel_id=1, source_target_pairs={{0,16},{16,0},{1,17},{17,1},{2,18},{18,2},{3,19},{19,3},{4,20},{20... | collective-permute-start | bytes 3342344 | tf_op jit(solution)/shard_map/ppermute | solution.py:762
  66.0 8.8 %collective-permute-start.8 = (f32[2]{0:T(128)S(1)}, f32[2]{0:T(128)S(1)}, u32[]{:S(2)}, u32[]{:S(2)}) collective-permute-start(f32[2]{0:T(128)S(1)} %get-tuple-element.97), channel_id=1, source_target_pairs={{0,16},{16,0},{1,17},{17,1},{2,18},{18,2},{3,19},{19,3},{4,20},{20... | collective-permute-start | bytes 32 | tf_op jit(solution)/shard_map/ppermute | solution.py:762

commit v6 on v4

--- a/solution.py
+++ b/solution.py
@@ -384,7 +384,8 @@
             put_sums(6 + i * len(PAIRS), names[0], names[1], PAIRS)
         return carry
 
-    lax.fori_loop(0, members, one, 0)
+    for m in range(members):
+        one(m, 0)
     for m in range(members):
         out[m : m + 1, :] = jnp.sum(jnp.transpose(red[m]), axis=0, keepdims=True)
 
@@ -580,7 +581,8 @@
             zonal[here, :] = jnp.where(lanes_like((b - a, LANE)) == member * levels + l, row_sum, zonal[here, :])
         return carry
 
-    lax.fori_loop(0, levels, level, 0)
+    for l in range(levels):
+        level(l, 0)
     if not is_first:
         square = jnp.concatenate([zonal[...]] + [jnp.zeros_like(zonal)] * (LANE // rows - 1), axis=0)
         turned = jnp.transpose(square)[: members * levels]

time: 74.9 us -> 75.5 us (level)
    pallas_call x1, Pallas kernels: 7.57 us -> 8.33 us  [local_sums(): pl.pallas_call(functools.partial(sums_kernel, levels, total_rows), out_sh...]
where the time goes in v6:
time: 75.5 us; the launch traced here: 75.3 us
  Pallas kernels  24.4 us (32%)
  blocking collectives  19.9 us (26%)
  starting transfers between devices  14 us (19%)
  waiting for transfers between devices  14 us (19%)
  between operations  2.27 us (3%)
    all_to_all x2, blocking collectives, from_all(): return lax.all_to_all(tiles, axes, split_axis=0, concat_axis=0, tiled=True)  19.9 us
    pallas_call x2, Pallas kernels, advance(): pl.pallas_call(functools.partial(advance_kernel, levels, total_rows, is_f...  9.98 us
    pallas_call x1, Pallas kernels, local_sums(): pl.pallas_call(functools.partial(sums_kernel, levels, total_rows), out_sh...  8.33 us
    ppermute x3, waiting for transfers between devices, swap(): return lax.ppermute(value, 'member', [(0, 1), (1, 0)])  7.8 us
    ppermute x2, waiting for transfers between devices, shift(): lax.ppermute(value, axis, [(i, (i + by) % count) for i in range(count)])  5.32 us
    ppermute x4, starting transfers between devices, pair(): return lax.ppermute(value, 'gridy', list(enumerate(partners[which])))  5.22 us
    ppermute x2, starting transfers between devices, shift(): lax.ppermute(value, axis, [(i, (i + by) % count) for i in range(count)])  5.1 us
    ppermute x3, starting transfers between devices, swap(): return lax.ppermute(value, 'member', [(0, 1), (1, 0)])  3.68 us
  transfers between devices with their start and end apart: 9, of which 4 were waited for; matrix products, arithmetic and copies ran while one was open for 1% of the time, Pallas kernels for 8%

profile of v6, /device:TPU:0, one launch (start us, length us, event | category | flops | bytes accessed | tf_op | source)
XLA Modules:
  0.0 75.3 jit_solution(5969446674202920381)
XLA Ops:
  0.7 2.9 %pack_rims.1 = (f32[2,64,256]{2,1,0:T(8,128)}, f32[2,64,256]{2,1,0:T(8,128)}, f32[2,184,256]{2,1,0:T(8,128)}, f32[2,184,256]{2,1,0:T(8,128)}) custom-call(f32[2,4,64,256]{3,2,1,0:T(8,128)} %refs_0_.3, f32[2,4,64,256]{3,2,1,0:T(8,128)} %refs_1_.3, f32[2,4,64,256]{3,2,1,0:T(8,128)} %refs_2_.3, f32[2,4,64,256]{3,2,1,0:T(8,128)} %refs_3_.3, ...), custom_call_target="tpu_custom_call" | custom-call | tf_op jit(solution)/shard_map/pack_rims/pallas_call | solution.py:123
  3.6 5.1 %collective-permute-start.1 = (f32[2,64,256]{2,1,0:T(8,128)}, f32[2,64,256]{2,1,0:T(8,128)S(1)}, u32[]{:S(2)}, u32[]{:S(2)}) collective-permute-start(f32[2,64,256]{2,1,0:T(8,128)} %get-tuple-element.86), channel_id=1, source_target_pairs={{0,3},{1,0},{2,1},{3,2},{4,7},{5,4},{6,5},{7,6},{8,11},{9,8},{10,9... | collective-permute-start | bytes 393224 | tf_op jit(solution)/shard_map/ppermute | solution.py:715
  8.7 1.5 %collective-permute-start.3 = (s32[2]{0:T(128)S(1)}, s32[2]{0:T(128)S(1)}, u32[]{:S(2)}, u32[]{:S(2)}) collective-permute-start(s32[2]{0:T(128)S(1)} %copy-done.6), channel_id=1, source_target_pairs={{0,16},{16,0},{1,17},{17,1},{2,18},{18,2},{3,19},{19,3},{4,20},{20... | collective-permute-start | bytes 32 | tf_op jit(solution)/shard_map/ppermute | solution.py:744
  10.2 1.6 %collective-permute-start.5 = (f32[2,184,256]{2,1,0:T(8,128)}, f32[2,184,256]{2,1,0:T(8,128)S(1)}, u32[]{:S(2)}, u32[]{:S(2)}) collective-permute-start(f32[2,184,256]{2,1,0:T(8,128)} %get-tuple-element.90), channel_id=1, source_target_pairs={{0,0},{4,8},{8,4},{12,12},{1,1},{5,9},{9,5},{13,13},{2,2},{6,10},{... | collective-permute-start | bytes 1130504 | tf_op jit(solution)/shard_map/ppermute | solution.py:726
  11.8 1.1 %collective-permute-done.1.refs_6_ = f32[2,64,256]{2,1,0:T(8,128)S(1)} collective-permute-done((f32[2,64,256]{2,1,0:T(8,128)}, f32[2,64,256]{2,1,0:T(8,128)S(1)}, u32[]{:S(2)}, u32[]{:S(2)}) %collective-permute-start.1) | collective-permute-done | bytes 131104 | tf_op jit(solution)/shard_map/ppermute | solution.py:715
  12.9 4.3 %collective-permute-done.2.refs_7_ = f32[2,64,256]{2,1,0:T(8,128)S(1)} collective-permute-done((f32[2,64,256]{2,1,0:T(8,128)}, f32[2,64,256]{2,1,0:T(8,128)S(1)}, u32[]{:S(2)}, u32[]{:S(2)}) %collective-permute-start.2) | collective-permute-done | bytes 131104 | tf_op jit(solution)/shard_map/ppermute | solution.py:715
  17.2 0.0 collective-permute-done.3.theirs
  17.2 0.7 collective-permute-start.7
  17.9 2.9 %collective-permute-start.6 = (f32[2,16,512]{2,1,0:T(8,128)S(1)}, f32[2,16,512]{2,1,0:T(8,128)S(1)}, u32[]{:S(2)}, u32[]{:S(2)}) collective-permute-start(f32[2,16,512]{2,1,0:T(8,128)S(1)} %get-tuple-element.108), channel_id=1, source_target_pairs={{0,4},{4,0},{8,12},{12,8},{1,5},{5,1},{9,13},{13,9},{2,6},{6,2},{1... | collective-permute-start | bytes 196616 | tf_op jit(solution)/shard_map/ppermute | solution.py:726
  20.8 0.9 %collective-permute-done.6.refs_10_ = f32[2,16,512]{2,1,0:T(8,128)S(1)} collective-permute-done((f32[2,16,512]{2,1,0:T(8,128)S(1)}, f32[2,16,512]{2,1,0:T(8,128)S(1)}, u32[]{:S(2)}, u32[]{:S(2)}) %collective-permute-start.6) | collective-permute-done | bytes 65568 | tf_op jit(solution)/shard_map/ppermute | solution.py:726
  21.7 0.0 collective-permute-done.4.refs_8_
  21.8 8.3 %local_sums.1 = (f32[2,128]{1,0:T(2,128)S(1)}, f32[2,24,112,384]{3,2,1,0:T(8,128)S(1)}, s32[5]{0:T(128)S(1)}) custom-call(s32[2]{0:T(128)S(1)} %copy-done.6, s32[2]{0:T(128)S(1)} %collective-permute-done.3.theirs, f32[2,4,64,256]{3,2,1,0:T(8,128)S(1)} %copy-done, f32[2,4,64,256]{3,2,1,0:T(8,128)S(1)} %copy-done.1, f32[2,4,64,256]{3,2,1,0:T(8,128)S(1)} %copy-done.2, ...), custom_call_target="tpu_custom_call" | custom-call | flops 100000000 | bytes 4000000 | tf_op jit(solution)/shard_map/local_sums/pallas_call | solution.py:402
  30.1 10.8 %all_to_all.10.refs_1_ = f32[16,2,128]{2,1,0:T(2,128)S(1)} all-to-all(f32[16,2,128]{2,1,0:T(2,128)S(1)} %broadcast_in_dim.2), channel_id=1, replica_groups=mesh['member'=2,'gridy'=4,'gridx'=4] {'gridy','gridx'}, dimensions={0} | all-to-all | bytes 32768 | tf_op jit(solution)/shard_map/all_to_all | solution.py:740
  40.9 4.9 %advance.3 = (f32[17,64,256]{2,1,0:T(8,128)S(1)}, f32[64,128]{1,0:T(8,128)S(1)}) custom-call(s32[5]{0:T(128)S(1)} %get-tuple-element.93.refs_0_, f32[16,2,128]{2,1,0:T(2,128)S(1)} %all_to_all.10.refs_1_, f32[2,24,112,384]{3,2,1,0:T(8,128)S(1)} %get-tuple-element.95.refs_2_), custom_call_target="tpu_custom_call" | custom-call | flops 100000000 | bytes 4000000 | tf_op jit(solution)/shard_map/advance/pallas_call | solution.py:607
  45.9 0.6 collective-permute-start.9
  46.5 0.6 fusion.2
  48.3 14.9 %conditional.2 = (f32[17,64,256]{2,1,0:T(8,128)S(1)}, f32[2,4,64]{2,1,0:T(4,128)}, f32[2]{0:T(128)S(1)}) conditional(s32[]{:T(128)} %bitcast.1, () %tuple.24, (s32[5]{0:T(128)S(1)}, f32[16,2,128]{2,1,0:T(2,128)S(1)}, f32[2,24,112,384]{3,2,1,0:T(8,128)S(1)}, f32[64,128]{1,0:T(8,128)S(1)}) %tuple.25), branch_computations={%region_0.1_spmd, %region_1.2_spmd} | conditional | flops 100000000 | bytes 4065560 | solution.py:769
  48.4 5.1 %advance.2 = (f32[17,64,256]{2,1,0:T(8,128)S(1)}, f32[16,4,128]{2,1,0:T(4,128)S(1)}) custom-call(s32[5]{0:T(128)S(1)} %get-tuple-element.36.refs_0_, f32[16,2,128]{2,1,0:T(2,128)S(1)} %get-tuple-element.37.refs_1_, f32[2,24,112,384]{3,2,1,0:T(8,128)S(1)} %get-tuple-element.38.refs_2_, f32[64,128]{1,0:T(8,128)S(1)} %get-tuple-element.39.refs_3_), custom_call_target="tpu_custom_call" | custom-call | flops 100000000 | bytes 4000000 | tf_op jit(solution)/shard_map/cond/branch_1_fun/advance/pallas_call | solution.py:607
  53.4 9.1 %all_to_all.9.spread = f32[16,4,128]{2,1,0:T(4,128)S(1)} all-to-all(f32[16,4,128]{2,1,0:T(4,128)S(1)} %get-tuple-element.41), channel_id=1, replica_groups=mesh['member'=2,'gridy'=4,'gridx'=4] {'gridy','gridx'}, dimensions={0} | all-to-all | bytes 65536 | tf_op jit(solution)/shard_map/cond/branch_1_fun/all_to_all | solution.py:740
  62.5 0.7 finish.1
  63.2 1.6 %collective-permute-start.8 = (f32[2]{0:T(128)S(1)}, f32[2]{0:T(128)S(1)}, u32[]{:S(2)}, u32[]{:S(2)}) collective-permute-start(f32[2]{0:T(128)S(1)} %get-tuple-element.97), channel_id=1, source_target_pairs={{0,16},{16,0},{1,17},{17,1},{2,18},{18,2},{3,19},{19,3},{4,20},{20... | collective-permute-start | bytes 32 | tf_op jit(solution)/shard_map/ppermute | solution.py:744
  64.8 7.8 %collective-permute-done.8 = f32[2]{0:T(128)S(1)} collective-permute-done((f32[2]{0:T(128)S(1)}, f32[2]{0:T(128)S(1)}, u32[]{:S(2)}, u32[]{:S(2)}) %collective-permute-start.8) | collective-permute-done | bytes 40 | tf_op jit(solution)/shard_map/ppermute | solution.py:744
  72.6 2.5 %conditional.3 = ((f32[2,4,64,256]{3,2,1,0:T(8,128)}, f32[2,4,64,256]{3,2,1,0:T(8,128)}, f32[2,4,64,256]{3,2,1,0:T(8,128)}, f32[2,4,64,256]{3,2,1,0:T(8,128)}, f32[2,64,256]{2,1,0:T(8,128)}, /*index=5*/f32[2]{0:T(128)})) conditional(s32[]{:T(128)} %bitcast, (s32[5]{0:T(128)S(1)}, s32[2]{0:T(128)S(1)}, f32[2]{0:T(128)S(1)}, f32[2]{0:T(128)S(1)}, ...), branch_computations={%region_2.3_spmd, %region_3.4_spmd} | conditional | bytes 4456496 | solution.py:779
  72.6 2.5 %pick.2 = (f32[2,4,64,256]{3,2,1,0:T(8,128)}, f32[2,4,64,256]{3,2,1,0:T(8,128)}, f32[2,4,64,256]{3,2,1,0:T(8,128)}, f32[2,4,64,256]{3,2,1,0:T(8,128)}, f32[2,64,256]{2,1,0:T(8,128)}, /*index=5*/f32[2]{0:T(128)}) custom-call(s32[5]{0:T(128)S(1)} %get-tuple-element.44.choice, s32[2]{0:T(128)S(1)} %get-tuple-element.45.source, f32[2]{0:T(128)S(1)} %get-tuple-element.46.score, ...), custom_call_target="tpu_custom_call" | custom-call | tf_op jit(solution)/shard_map/cond/branch_0_fun/pick/pallas_call | solution.py:702
  (24 shorter events, 0.1 us)
Async XLA Ops:
  0.6 21.1 %copy-start.5 = (s32[64,256]{1,0:T(8,128)S(1)}, s32[64,256]{1,0:T(8,128)}, u32[]{:S(2)}) copy-start(s32[64,256]{1,0:T(8,128)} %refs_5_.3) | copy-start | bytes 196612
  0.6 21.1 %copy-start.4 = (f32[2,64,256]{2,1,0:T(8,128)S(1)}, f32[2,64,256]{2,1,0:T(8,128)}, u32[]{:S(2)}) copy-start(f32[2,64,256]{2,1,0:T(8,128)} %refs_4_.3) | copy-start | bytes 393220
  0.7 21.1 %copy-start.3 = (f32[2,4,64,256]{3,2,1,0:T(8,128)S(1)}, f32[2,4,64,256]{3,2,1,0:T(8,128)}, u32[]{:S(2)}) copy-start(f32[2,4,64,256]{3,2,1,0:T(8,128)} %refs_3_.3) | copy-start | bytes 1572868
  0.7 21.1 %copy-start.2 = (f32[2,4,64,256]{3,2,1,0:T(8,128)S(1)}, f32[2,4,64,256]{3,2,1,0:T(8,128)}, u32[]{:S(2)}) copy-start(f32[2,4,64,256]{3,2,1,0:T(8,128)} %refs_2_.3) | copy-start | bytes 1572868
  0.7 21.1 %copy-start.1 = (f32[2,4,64,256]{3,2,1,0:T(8,128)S(1)}, f32[2,4,64,256]{3,2,1,0:T(8,128)}, u32[]{:S(2)}) copy-start(f32[2,4,64,256]{3,2,1,0:T(8,128)} %refs_1_.3) | copy-start | bytes 1572868
  0.7 21.1 %copy-start = (f32[2,4,64,256]{3,2,1,0:T(8,128)S(1)}, f32[2,4,64,256]{3,2,1,0:T(8,128)}, u32[]{:S(2)}) copy-start(f32[2,4,64,256]{3,2,1,0:T(8,128)} %refs_0_.3) | copy-start | bytes 1572868
  0.7 8.0 %copy-start.6 = (s32[2]{0:T(128)S(1)}, s32[2]{0:T(128)}, u32[]{:S(2)}) copy-start(s32[2]{0:T(128)} %source.1) | copy-start | bytes 28
  3.6 9.3 %collective-permute-start.1 = (f32[2,64,256]{2,1,0:T(8,128)}, f32[2,64,256]{2,1,0:T(8,128)S(1)}, u32[]{:S(2)}, u32[]{:S(2)}) collective-permute-start(f32[2,64,256]{2,1,0:T(8,128)} %get-tuple-element.86), channel_id=1, source_target_pairs={{0,3},{1,0},{2,1},{3,2},{4,7},{5,4},{6,5},{7,6},{8,11},{9,8},{10,9... | collective-permute-start | bytes 393224 | tf_op jit(solution)/shard_map/ppermute | solution.py:715
  8.7 8.5 %collective-permute-start.3 = (s32[2]{0:T(128)S(1)}, s32[2]{0:T(128)S(1)}, u32[]{:S(2)}, u32[]{:S(2)}) collective-permute-start(s32[2]{0:T(128)S(1)} %copy-done.6), channel_id=1, source_target_pairs={{0,16},{16,0},{1,17},{17,1},{2,18},{18,2},{3,19},{19,3},{4,20},{20... | collective-permute-start | bytes 32 | tf_op jit(solution)/shard_map/ppermute | solution.py:744
  10.2 7.0 %collective-permute-start.2 = (f32[2,64,256]{2,1,0:T(8,128)}, f32[2,64,256]{2,1,0:T(8,128)S(1)}, u32[]{:S(2)}, u32[]{:S(2)}) collective-permute-start(f32[2,64,256]{2,1,0:T(8,128)} %get-tuple-element.87), channel_id=1, source_target_pairs={{0,1},{1,2},{2,3},{3,0},{4,5},{5,6},{6,7},{7,4},{8,9},{9,10},{10,1... | collective-permute-start | bytes 393224 | tf_op jit(solution)/shard_map/ppermute | solution.py:715
  10.2 11.5 %collective-permute-start.4 = (f32[2,184,256]{2,1,0:T(8,128)}, f32[2,184,256]{2,1,0:T(8,128)S(1)}, u32[]{:S(2)}, u32[]{:S(2)}) collective-permute-start(f32[2,184,256]{2,1,0:T(8,128)} %get-tuple-element.89), channel_id=1, source_target_pairs={{0,4},{4,0},{8,12},{12,8},{1,5},{5,1},{9,13},{13,9},{2,6},{6,2},{1... | collective-permute-start | bytes 1130504 | tf_op jit(solution)/shard_map/ppermute | solution.py:726
  10.2 11.5 %collective-permute-start.5 = (f32[2,184,256]{2,1,0:T(8,128)}, f32[2,184,256]{2,1,0:T(8,128)S(1)}, u32[]{:S(2)}, u32[]{:S(2)}) collective-permute-start(f32[2,184,256]{2,1,0:T(8,128)} %get-tuple-element.90), channel_id=1, source_target_pairs={{0,0},{4,8},{8,4},{12,12},{1,1},{5,9},{9,5},{13,13},{2,2},{6,10},{... | collective-permute-start | bytes 1130504 | tf_op jit(solution)/shard_map/ppermute | solution.py:726
  17.2 3.6 %collective-permute-start.7 = (f32[2,16,512]{2,1,0:T(8,128)S(1)}, f32[2,16,512]{2,1,0:T(8,128)S(1)}, u32[]{:S(2)}, u32[]{:S(2)}) collective-permute-start(f32[2,16,512]{2,1,0:T(8,128)S(1)} %get-tuple-element.107), channel_id=1, source_target_pairs={{0,0},{4,8},{8,4},{12,12},{1,1},{5,9},{9,5},{13,13},{2,2},{6,10},{... | collective-permute-start | bytes 196616 | tf_op jit(solution)/shard_map/ppermute | solution.py:726
  17.9 3.8 %collective-permute-start.6 = (f32[2,16,512]{2,1,0:T(8,128)S(1)}, f32[2,16,512]{2,1,0:T(8,128)S(1)}, u32[]{:S(2)}, u32[]{:S(2)}) collective-permute-start(f32[2,16,512]{2,1,0:T(8,128)S(1)} %get-tuple-element.108), channel_id=1, source_target_pairs={{0,4},{4,0},{8,12},{12,8},{1,5},{5,1},{9,13},{13,9},{2,6},{6,2},{1... | collective-permute-start | bytes 196616 | tf_op jit(solution)/shard_map/ppermute | solution.py:726
  45.9 26.7 %collective-permute-start.9 = (f32[17,64,256]{2,1,0:T(8,128)S(1)}, f32[17,64,256]{2,1,0:T(8,128)S(1)}, u32[]{:S(2)}, u32[]{:S(2)}) collective-permute-start(f32[17,64,256]{2,1,0:T(8,128)S(1)} %get-tuple-element.98), channel_id=1, source_target_pairs={{0,16},{16,0},{1,17},{17,1},{2,18},{18,2},{3,19},{19,3},{4,20},{20... | collective-permute-start | bytes 3342344 | tf_op jit(solution)/shard_map/ppermute | solution.py:744
  63.2 9.4 %collective-permute-start.8 = (f32[2]{0:T(128)S(1)}, f32[2]{0:T(128)S(1)}, u32[]{:S(2)}, u32[]{:S(2)}) collective-permute-start(f32[2]{0:T(128)S(1)} %get-tuple-element.97), channel_id=1, source_target_pairs={{0,16},{16,0},{1,17},{17,1},{2,18},{18,2},{3,19},{19,3},{4,20},{20... | collective-permute-start | bytes 32 | tf_op jit(solution)/shard_map/ppermute | solution.py:744
